TPU v7x, 32 devices: a whole 2x2x4 slice. The times are simulated.
32 devices in a mesh: blk: 8 (over y, x, core), sims: 4 (over z).
Axes of the slice: x: 2, y: 2, z: 4, core: 2. Of those that a mesh axis runs over, the one named last changes fastest.
Arguments:
- rhs: float32 [4, 8, 256, 512], P(None, 'blk', None, 'sims'), parts along dimension 3, may hold values from -6 to 6
- lower_blocks: float32 [4, 8, 3, 256, 256], P(None, 'blk'), may hold values from -0.16875 to 0.16875
- col_index: int32 [4, 8, 3], P(None, 'blk'), may hold values from -1 to 30, as said below
- diag_inverse: float32 [4, 8, 256, 256], P(None, 'blk'), may hold values from -1.5 to 1.5, as said below
- turnout: float32 [4, 8, 256], P(None, 'blk'), may hold values from 0.2 to 5
- district_of: int32 [4, 8, 256], P(None, 'blk'), may hold values from 0 to 255, as said below
Outputs:
- solution: float32 [4, 8, 256, 512], P(None, 'blk', None, 'sims'), parts along dimension 3
- district_mean: float32 [256, 512], P('blk', 'sims'), parts along dimension 1
There are 4 independent parts, one for each index of `sims`. A program takes and returns all parts, laid end to end along the dimension named above; an argument that names none is the same for every part. Nothing has to cross between parts.
Inputs may be any that keep to these rules, and one draw needn't show every extreme that they name: `col_index`: entry [r, p, k] belongs to block row i = r * 8 + p. Slot 0 holds i - 1 (-1 for i = 0); the other slots hold distinct columns from i - 4 to i - 2, or -1 where the block is absent. `diag_inverse`: each block is lower triangular. `district_of`: each district holds exactly 32 precincts.
All inputs are finite; a program needn't handle non-finite values.
Results may differ from a plain program's by a relative error of at most 0.0002.
Values sent between devices are 32-bit elements; how exact they have to be, the bound alone decides.
No kernel may reach another device: no remote copies, remote signals or barrier semaphores. Data moves between devices by JAX's collectives and lax.ppermute only.
A program may use at most 64 MiB of HBM per device.

v0:
```python
import jax
import jax.numpy as jnp
from jax import lax
from jax.sharding import PartitionSpec as P

WIN = 4
NDIST = 256


precise = lax.Precision.HIGHEST


def shifted(value, axis, by):
    size = lax.axis_size(axis)
    return lax.ppermute(value, axis, [(i, (i + by) % size) for i in range(size)])


def body(rhs, lower_blocks, col_index, diag_inverse, turnout, district_of):
    cycle_size = lax.axis_size("blk")
    device_index = lax.axis_index("blk")
    rows_here = rhs.shape[0]
    total_rows = rows_here * cycle_size
    block_size = rhs.shape[2]
    columns = rhs.shape[3]
    local_rhs = rhs[:, 0]
    factor = lower_blocks[:, 0]
    pattern = col_index[:, 0]
    inverses = diag_inverse[:, 0]
    piece_count = 1
    piece_width = columns // piece_count
    window_slots = jnp.arange(WIN, dtype=jnp.int32)
    zero_index = jnp.zeros((), jnp.int32)

    def advance(wave_step, loop_state):
        pending, solution = loop_state
        lead_row = (total_rows - 1 - wave_step).astype(jnp.int32)
        piece_now = jnp.mod(device_index - lead_row, cycle_size)
        row_now = lead_row + piece_now
        is_valid = (piece_now < piece_count) & (row_now >= 0) & (row_now <= total_rows - 1)
        row_safe = jnp.clip(row_now, 0, total_rows - 1)
        slot_now = row_safe // cycle_size
        start_col = jnp.minimum(piece_now, piece_count - 1) * piece_width
        pending = jnp.where(row_now == total_rows - 1, jnp.zeros_like(pending), pending)
        source = lax.dynamic_slice(
            local_rhs, (slot_now, zero_index, start_col), (1, block_size, piece_width)
        )[0]
        inverse_now = lax.dynamic_index_in_dim(inverses, slot_now, 0, keepdims=False)
        solved = jnp.einsum("ab,as->bs", inverse_now, source - pending[0], precision=precise)
        blocks_now = lax.dynamic_index_in_dim(factor, slot_now, 0, keepdims=False)
        columns_now = lax.dynamic_index_in_dim(pattern, slot_now, 0, keepdims=False)
        present = columns_now >= 0
        updates = jnp.einsum("kab,as->kbs", blocks_now, solved, precision=precise)
        target = row_safe - 1 - columns_now
        routing = (present[:, None] & (target[:, None] == window_slots[None, :])).astype(
            jnp.float32
        )
        added_terms = jnp.einsum("kw,kbs->wbs", routing, updates, precision=precise)
        moved_carry = jnp.concatenate([pending[1:], jnp.zeros_like(pending[:1])], 0) + added_terms
        old_piece = lax.dynamic_slice(
            solution, (slot_now, zero_index, start_col), (1, block_size, piece_width)
        )
        kept_piece = jnp.where(is_valid, solved[None], old_piece)
        solution = lax.dynamic_update_slice(solution, kept_piece, (slot_now, zero_index, start_col))
        pending = shifted(moved_carry, "blk", -1)
        return (pending, solution)

    start_carry = jnp.zeros((WIN, block_size, piece_width), jnp.float32)
    start_field = jnp.zeros_like(local_rhs)
    _, solution = lax.fori_loop(
        0, total_rows + piece_count - 1, advance, (start_carry, start_field)
    )
    cell_rows = solution.reshape(rows_here * block_size, columns)
    weights = turnout[:, 0].reshape(rows_here * block_size)
    district_ids = district_of[:, 0].reshape(rows_here * block_size)
    member = (district_ids[:, None] == jnp.arange(NDIST, dtype=jnp.int32)[None, :]).astype(
        jnp.float32
    )
    numerator = jnp.einsum("cd,cs->ds", member, weights[:, None] * cell_rows, precision=precise)
    denominator = jnp.einsum("cd,c->d", member, weights, precision=precise)
    numer_share, denom_share = (
        lax.psum_scatter(numerator, "blk", scatter_dimension=0, tiled=True),
        lax.psum_scatter(denominator, "blk", scatter_dimension=0, tiled=True),
    )
    return (solution[:, None], numer_share / denom_share[:, None])


def solution(mesh):
    placed = (
        P(None, "blk", None, "sims"),
        P(None, "blk", None, None, None),
        P(None, "blk", None),
        P(None, "blk", None, None),
        P(None, "blk", None),
        P(None, "blk", None),
    )
    return jax.shard_map(
        body,
        mesh=mesh,
        in_specs=placed,
        out_specs=(P(None, "blk", None, "sims"), P("blk", "sims")),
        check_vma=False,
    )
```

profile of v0, /device:TPU:0, one launch (start us, length us, event | category | flops | bytes accessed | tf_op | source)
XLA Modules:
  0.0 533.3 jit_solution(6697845679317788065)
XLA Ops:
  9.5 478.3 %while.19 = (s32[]{:T(128)}, f32[4,256,128]{2,0,1:T(4,128)S(1)}, f32[4,256,128]{2,1,0:T(8,128)S(1)}, s32[]{:T(128)}, s32[4,3]{1,0:T(4,128)S(1)}, /*index=5*/f32[...) while((s32[]{:T(128)}, f32[4,256,128]{2,0,1:T(4,128)S(1)}, ...), condition=%wide.region_1.2_spmd.clone, body=%wide.region_0.1_spmd.clone.sunk | while | flops 407699520 | bytes 7735383 | solution.py:69
  15.0 3.4 collective-permute-start
  18.3 6.7 %collective-permute-done = f32[4,256,128]{2,0,1:T(4,128)S(1)} collective-permute-done((f32[4,256,128]{2,0,1:T(4,128)S(1)}, f32[4,256,128]{2,0,1:T(4,128)S(1)}, u32[]{:S(2)}, u32[]{:S(2)}) %collective-permute-start) | collective-permute-done | bytes 524320 | tf_op jit(solution)/shard_map/while/body/eval_jaxpr/ppermute | solution.py:15
  30.4 2.9 collective-permute-start
  33.3 6.7 %collective-permute-done = f32[4,256,128]{2,0,1:T(4,128)S(1)} collective-permute-done((f32[4,256,128]{2,0,1:T(4,128)S(1)}, f32[4,256,128]{2,0,1:T(4,128)S(1)}, u32[]{:S(2)}, u32[]{:S(2)}) %collective-permute-start) | collective-permute-done | bytes 524320 | tf_op jit(solution)/shard_map/while/body/eval_jaxpr/ppermute | solution.py:15
  45.3 2.9 collective-permute-start
  48.2 6.7 %collective-permute-done = f32[4,256,128]{2,0,1:T(4,128)S(1)} collective-permute-done((f32[4,256,128]{2,0,1:T(4,128)S(1)}, f32[4,256,128]{2,0,1:T(4,128)S(1)}, u32[]{:S(2)}, u32[]{:S(2)}) %collective-permute-start) | collective-permute-done | bytes 524320 | tf_op jit(solution)/shard_map/while/body/eval_jaxpr/ppermute | solution.py:15
  63.1 6.7 %collective-permute-done = f32[4,256,128]{2,0,1:T(4,128)S(1)} collective-permute-done((f32[4,256,128]{2,0,1:T(4,128)S(1)}, f32[4,256,128]{2,0,1:T(4,128)S(1)}, u32[]{:S(2)}, u32[]{:S(2)}) %collective-permute-start) | collective-permute-done | bytes 524320 | tf_op jit(solution)/shard_map/while/body/eval_jaxpr/ppermute | solution.py:15
  75.2 2.9 collective-permute-start
  78.1 6.7 %collective-permute-done = f32[4,256,128]{2,0,1:T(4,128)S(1)} collective-permute-done((f32[4,256,128]{2,0,1:T(4,128)S(1)}, f32[4,256,128]{2,0,1:T(4,128)S(1)}, u32[]{:S(2)}, u32[]{:S(2)}) %collective-permute-start) | collective-permute-done | bytes 524320 | tf_op jit(solution)/shard_map/while/body/eval_jaxpr/ppermute | solution.py:15
  90.1 2.9 collective-permute-start
  93.0 6.7 %collective-permute-done = f32[4,256,128]{2,0,1:T(4,128)S(1)} collective-permute-done((f32[4,256,128]{2,0,1:T(4,128)S(1)}, f32[4,256,128]{2,0,1:T(4,128)S(1)}, u32[]{:S(2)}, u32[]{:S(2)}) %collective-permute-start) | collective-permute-done | bytes 524320 | tf_op jit(solution)/shard_map/while/body/eval_jaxpr/ppermute | solution.py:15
  107.9 6.7 %collective-permute-done = f32[4,256,128]{2,0,1:T(4,128)S(1)} collective-permute-done((f32[4,256,128]{2,0,1:T(4,128)S(1)}, f32[4,256,128]{2,0,1:T(4,128)S(1)}, u32[]{:S(2)}, u32[]{:S(2)}) %collective-permute-start) | collective-permute-done | bytes 524320 | tf_op jit(solution)/shard_map/while/body/eval_jaxpr/ppermute | solution.py:15
  122.8 6.7 %collective-permute-done = f32[4,256,128]{2,0,1:T(4,128)S(1)} collective-permute-done((f32[4,256,128]{2,0,1:T(4,128)S(1)}, f32[4,256,128]{2,0,1:T(4,128)S(1)}, u32[]{:S(2)}, u32[]{:S(2)}) %collective-permute-start) | collective-permute-done | bytes 524320 | tf_op jit(solution)/shard_map/while/body/eval_jaxpr/ppermute | solution.py:15
  134.9 2.9 collective-permute-start
  137.8 6.7 %collective-permute-done = f32[4,256,128]{2,0,1:T(4,128)S(1)} collective-permute-done((f32[4,256,128]{2,0,1:T(4,128)S(1)}, f32[4,256,128]{2,0,1:T(4,128)S(1)}, u32[]{:S(2)}, u32[]{:S(2)}) %collective-permute-start) | collective-permute-done | bytes 524320 | tf_op jit(solution)/shard_map/while/body/eval_jaxpr/ppermute | solution.py:15
  152.7 6.7 %collective-permute-done = f32[4,256,128]{2,0,1:T(4,128)S(1)} collective-permute-done((f32[4,256,128]{2,0,1:T(4,128)S(1)}, f32[4,256,128]{2,0,1:T(4,128)S(1)}, u32[]{:S(2)}, u32[]{:S(2)}) %collective-permute-start) | collective-permute-done | bytes 524320 | tf_op jit(solution)/shard_map/while/body/eval_jaxpr/ppermute | solution.py:15
  167.6 6.7 %collective-permute-done = f32[4,256,128]{2,0,1:T(4,128)S(1)} collective-permute-done((f32[4,256,128]{2,0,1:T(4,128)S(1)}, f32[4,256,128]{2,0,1:T(4,128)S(1)}, u32[]{:S(2)}, u32[]{:S(2)}) %collective-permute-start) | collective-permute-done | bytes 524320 | tf_op jit(solution)/shard_map/while/body/eval_jaxpr/ppermute | solution.py:15
  179.7 2.9 collective-permute-start
  182.5 6.7 %collective-permute-done = f32[4,256,128]{2,0,1:T(4,128)S(1)} collective-permute-done((f32[4,256,128]{2,0,1:T(4,128)S(1)}, f32[4,256,128]{2,0,1:T(4,128)S(1)}, u32[]{:S(2)}, u32[]{:S(2)}) %collective-permute-start) | collective-permute-done | bytes 524320 | tf_op jit(solution)/shard_map/while/body/eval_jaxpr/ppermute | solution.py:15
  197.5 6.7 %collective-permute-done = f32[4,256,128]{2,0,1:T(4,128)S(1)} collective-permute-done((f32[4,256,128]{2,0,1:T(4,128)S(1)}, f32[4,256,128]{2,0,1:T(4,128)S(1)}, u32[]{:S(2)}, u32[]{:S(2)}) %collective-permute-start) | collective-permute-done | bytes 524320 | tf_op jit(solution)/shard_map/while/body/eval_jaxpr/ppermute | solution.py:15
  212.4 6.7 %collective-permute-done = f32[4,256,128]{2,0,1:T(4,128)S(1)} collective-permute-done((f32[4,256,128]{2,0,1:T(4,128)S(1)}, f32[4,256,128]{2,0,1:T(4,128)S(1)}, u32[]{:S(2)}, u32[]{:S(2)}) %collective-permute-start) | collective-permute-done | bytes 524320 | tf_op jit(solution)/shard_map/while/body/eval_jaxpr/ppermute | solution.py:15
  224.5 2.9 collective-permute-start
  227.3 6.7 %collective-permute-done = f32[4,256,128]{2,0,1:T(4,128)S(1)} collective-permute-done((f32[4,256,128]{2,0,1:T(4,128)S(1)}, f32[4,256,128]{2,0,1:T(4,128)S(1)}, u32[]{:S(2)}, u32[]{:S(2)}) %collective-permute-start) | collective-permute-done | bytes 524320 | tf_op jit(solution)/shard_map/while/body/eval_jaxpr/ppermute | solution.py:15
  242.3 6.7 %collective-permute-done = f32[4,256,128]{2,0,1:T(4,128)S(1)} collective-permute-done((f32[4,256,128]{2,0,1:T(4,128)S(1)}, f32[4,256,128]{2,0,1:T(4,128)S(1)}, u32[]{:S(2)}, u32[]{:S(2)}) %collective-permute-start) | collective-permute-done | bytes 524320 | tf_op jit(solution)/shard_map/while/body/eval_jaxpr/ppermute | solution.py:15
  257.2 6.7 %collective-permute-done = f32[4,256,128]{2,0,1:T(4,128)S(1)} collective-permute-done((f32[4,256,128]{2,0,1:T(4,128)S(1)}, f32[4,256,128]{2,0,1:T(4,128)S(1)}, u32[]{:S(2)}, u32[]{:S(2)}) %collective-permute-start) | collective-permute-done | bytes 524320 | tf_op jit(solution)/shard_map/while/body/eval_jaxpr/ppermute | solution.py:15
  269.3 2.9 collective-permute-start
  272.1 6.7 %collective-permute-done = f32[4,256,128]{2,0,1:T(4,128)S(1)} collective-permute-done((f32[4,256,128]{2,0,1:T(4,128)S(1)}, f32[4,256,128]{2,0,1:T(4,128)S(1)}, u32[]{:S(2)}, u32[]{:S(2)}) %collective-permute-start) | collective-permute-done | bytes 524320 | tf_op jit(solution)/shard_map/while/body/eval_jaxpr/ppermute | solution.py:15
  287.0 6.7 %collective-permute-done = f32[4,256,128]{2,0,1:T(4,128)S(1)} collective-permute-done((f32[4,256,128]{2,0,1:T(4,128)S(1)}, f32[4,256,128]{2,0,1:T(4,128)S(1)}, u32[]{:S(2)}, u32[]{:S(2)}) %collective-permute-start) | collective-permute-done | bytes 524320 | tf_op jit(solution)/shard_map/while/body/eval_jaxpr/ppermute | solution.py:15
  302.0 6.7 %collective-permute-done = f32[4,256,128]{2,0,1:T(4,128)S(1)} collective-permute-done((f32[4,256,128]{2,0,1:T(4,128)S(1)}, f32[4,256,128]{2,0,1:T(4,128)S(1)}, u32[]{:S(2)}, u32[]{:S(2)}) %collective-permute-start) | collective-permute-done | bytes 524320 | tf_op jit(solution)/shard_map/while/body/eval_jaxpr/ppermute | solution.py:15
  314.0 2.9 collective-permute-start
  316.9 6.7 %collective-permute-done = f32[4,256,128]{2,0,1:T(4,128)S(1)} collective-permute-done((f32[4,256,128]{2,0,1:T(4,128)S(1)}, f32[4,256,128]{2,0,1:T(4,128)S(1)}, u32[]{:S(2)}, u32[]{:S(2)}) %collective-permute-start) | collective-permute-done | bytes 524320 | tf_op jit(solution)/shard_map/while/body/eval_jaxpr/ppermute | solution.py:15
  331.8 6.7 %collective-permute-done = f32[4,256,128]{2,0,1:T(4,128)S(1)} collective-permute-done((f32[4,256,128]{2,0,1:T(4,128)S(1)}, f32[4,256,128]{2,0,1:T(4,128)S(1)}, u32[]{:S(2)}, u32[]{:S(2)}) %collective-permute-start) | collective-permute-done | bytes 524320 | tf_op jit(solution)/shard_map/while/body/eval_jaxpr/ppermute | solution.py:15
  346.8 6.7 %collective-permute-done = f32[4,256,128]{2,0,1:T(4,128)S(1)} collective-permute-done((f32[4,256,128]{2,0,1:T(4,128)S(1)}, f32[4,256,128]{2,0,1:T(4,128)S(1)}, u32[]{:S(2)}, u32[]{:S(2)}) %collective-permute-start) | collective-permute-done | bytes 524320 | tf_op jit(solution)/shard_map/while/body/eval_jaxpr/ppermute | solution.py:15
  358.8 2.9 collective-permute-start
  361.7 6.7 %collective-permute-done = f32[4,256,128]{2,0,1:T(4,128)S(1)} collective-permute-done((f32[4,256,128]{2,0,1:T(4,128)S(1)}, f32[4,256,128]{2,0,1:T(4,128)S(1)}, u32[]{:S(2)}, u32[]{:S(2)}) %collective-permute-start) | collective-permute-done | bytes 524320 | tf_op jit(solution)/shard_map/while/body/eval_jaxpr/ppermute | solution.py:15
  376.6 6.7 %collective-permute-done = f32[4,256,128]{2,0,1:T(4,128)S(1)} collective-permute-done((f32[4,256,128]{2,0,1:T(4,128)S(1)}, f32[4,256,128]{2,0,1:T(4,128)S(1)}, u32[]{:S(2)}, u32[]{:S(2)}) %collective-permute-start) | collective-permute-done | bytes 524320 | tf_op jit(solution)/shard_map/while/body/eval_jaxpr/ppermute | solution.py:15
  391.5 6.7 %collective-permute-done = f32[4,256,128]{2,0,1:T(4,128)S(1)} collective-permute-done((f32[4,256,128]{2,0,1:T(4,128)S(1)}, f32[4,256,128]{2,0,1:T(4,128)S(1)}, u32[]{:S(2)}, u32[]{:S(2)}) %collective-permute-start) | collective-permute-done | bytes 524320 | tf_op jit(solution)/shard_map/while/body/eval_jaxpr/ppermute | solution.py:15
  403.6 2.9 collective-permute-start
  406.5 6.7 %collective-permute-done = f32[4,256,128]{2,0,1:T(4,128)S(1)} collective-permute-done((f32[4,256,128]{2,0,1:T(4,128)S(1)}, f32[4,256,128]{2,0,1:T(4,128)S(1)}, u32[]{:S(2)}, u32[]{:S(2)}) %collective-permute-start) | collective-permute-done | bytes 524320 | tf_op jit(solution)/shard_map/while/body/eval_jaxpr/ppermute | solution.py:15
  421.4 6.7 %collective-permute-done = f32[4,256,128]{2,0,1:T(4,128)S(1)} collective-permute-done((f32[4,256,128]{2,0,1:T(4,128)S(1)}, f32[4,256,128]{2,0,1:T(4,128)S(1)}, u32[]{:S(2)}, u32[]{:S(2)}) %collective-permute-start) | collective-permute-done | bytes 524320 | tf_op jit(solution)/shard_map/while/body/eval_jaxpr/ppermute | solution.py:15
  436.3 6.7 %collective-permute-done = f32[4,256,128]{2,0,1:T(4,128)S(1)} collective-permute-done((f32[4,256,128]{2,0,1:T(4,128)S(1)}, f32[4,256,128]{2,0,1:T(4,128)S(1)}, u32[]{:S(2)}, u32[]{:S(2)}) %collective-permute-start) | collective-permute-done | bytes 524320 | tf_op jit(solution)/shard_map/while/body/eval_jaxpr/ppermute | solution.py:15
  448.4 2.9 collective-permute-start
  451.2 6.7 %collective-permute-done = f32[4,256,128]{2,0,1:T(4,128)S(1)} collective-permute-done((f32[4,256,128]{2,0,1:T(4,128)S(1)}, f32[4,256,128]{2,0,1:T(4,128)S(1)}, u32[]{:S(2)}, u32[]{:S(2)}) %collective-permute-start) | collective-permute-done | bytes 524320 | tf_op jit(solution)/shard_map/while/body/eval_jaxpr/ppermute | solution.py:15
  466.2 6.7 %collective-permute-done = f32[4,256,128]{2,0,1:T(4,128)S(1)} collective-permute-done((f32[4,256,128]{2,0,1:T(4,128)S(1)}, f32[4,256,128]{2,0,1:T(4,128)S(1)}, u32[]{:S(2)}, u32[]{:S(2)}) %collective-permute-start) | collective-permute-done | bytes 524320 | tf_op jit(solution)/shard_map/while/body/eval_jaxpr/ppermute | solution.py:15
  481.1 6.7 %collective-permute-done = f32[4,256,128]{2,0,1:T(4,128)S(1)} collective-permute-done((f32[4,256,128]{2,0,1:T(4,128)S(1)}, f32[4,256,128]{2,0,1:T(4,128)S(1)}, u32[]{:S(2)}, u32[]{:S(2)}) %collective-permute-start) | collective-permute-done | bytes 524320 | tf_op jit(solution)/shard_map/while/body/eval_jaxpr/ppermute | solution.py:15
  491.6 14.6 %all-reduce.1 = f32[256]{0:T(256)S(1)} all-reduce(f32[256]{0:T(256)S(1)} %bitcast.69), channel_id=3, replica_groups=mesh['blk'=8,'sims'=4] {'blk'}, use_global_device_ids=true, to_apply=%region_3.4.clone | all-reduce | flops 256 | bytes 2048
  506.3 18.8 %reduce-scatter.2.cloned.1.call-done = f32[32,128]{1,0:T(8,128)} async-done(((f32[256,128]{1,0:T(8,128)}), f32[32,128]{1,0:T(8,128)}) %reduce-scatter.2.cloned.1.call-update) | async-done | bytes 16400 | tf_op jit(solution)/shard_map/reduce_scatter | solution.py:81
  (295 shorter events, 231.0 us)
Async XLA Ops:
  7.2 517.9 %reduce-scatter.2.cloned.1.call-start = ((), (), s32[]{:S(2)}) async-start(), calls=%async_computation.1 | async-start | bytes 147456 | tf_op jit(solution)/shard_map/reduce_scatter | solution.py:81
  9.5 478.3 %copy-start.1 = (f32[4,1,256]{2,1,0:T(1,128)S(1)}, f32[4,1,256]{2,1,0:T(1,128)}, u32[]{:S(2)}) copy-start(f32[4,1,256]{2,1,0:T(1,128)} %param.12) | copy-start | bytes 12292
  9.5 478.5 %copy-start.2 = (s32[4,1,256]{2,1,0:T(1,128)S(1)}, s32[4,1,256]{2,1,0:T(1,128)}, u32[]{:S(2)}) copy-start(s32[4,1,256]{2,1,0:T(1,128)} %param.13) | copy-start | bytes 12292
  9.5 480.4 %copy-start.3 = (u32[32]{0:T(128)S(1)}, u32[32]{0:T(128)}, u32[]{:S(2)}) copy-start(u32[32]{0:T(128)} %constant.153) | copy-start | bytes 388
  15.0 10.1 %collective-permute-start = (f32[4,256,128]{2,0,1:T(4,128)S(1)}, f32[4,256,128]{2,0,1:T(4,128)S(1)}, u32[]{:S(2)}, u32[]{:S(2)}) collective-permute-start(f32[4,256,128]{2,0,1:T(4,128)S(1)} %convolution_add_fusion.2), channel_id=1, source_target_pairs={{0,28},{4,0},{8,4},{12,8},{16,12},{20,16},{24,20},{28,24},{1,29},{... | collective-permute-start | bytes 1572872 | tf_op jit(solution)/shard_map/while/body/eval_jaxpr/ppermute | solution.py:15
  30.4 9.6 %collective-permute-start = (f32[4,256,128]{2,0,1:T(4,128)S(1)}, f32[4,256,128]{2,0,1:T(4,128)S(1)}, u32[]{:S(2)}, u32[]{:S(2)}) collective-permute-start(f32[4,256,128]{2,0,1:T(4,128)S(1)} %convolution_add_fusion.2), channel_id=1, source_target_pairs={{0,28},{4,0},{8,4},{12,8},{16,12},{20,16},{24,20},{28,24},{1,29},{... | collective-permute-start | bytes 1572872 | tf_op jit(solution)/shard_map/while/body/eval_jaxpr/ppermute | solution.py:15
  45.3 9.6 %collective-permute-start = (f32[4,256,128]{2,0,1:T(4,128)S(1)}, f32[4,256,128]{2,0,1:T(4,128)S(1)}, u32[]{:S(2)}, u32[]{:S(2)}) collective-permute-start(f32[4,256,128]{2,0,1:T(4,128)S(1)} %convolution_add_fusion.2), channel_id=1, source_target_pairs={{0,28},{4,0},{8,4},{12,8},{16,12},{20,16},{24,20},{28,24},{1,29},{... | collective-permute-start | bytes 1572872 | tf_op jit(solution)/shard_map/while/body/eval_jaxpr/ppermute | solution.py:15
  60.3 9.6 %collective-permute-start = (f32[4,256,128]{2,0,1:T(4,128)S(1)}, f32[4,256,128]{2,0,1:T(4,128)S(1)}, u32[]{:S(2)}, u32[]{:S(2)}) collective-permute-start(f32[4,256,128]{2,0,1:T(4,128)S(1)} %convolution_add_fusion.2), channel_id=1, source_target_pairs={{0,28},{4,0},{8,4},{12,8},{16,12},{20,16},{24,20},{28,24},{1,29},{... | collective-permute-start | bytes 1572872 | tf_op jit(solution)/shard_map/while/body/eval_jaxpr/ppermute | solution.py:15
  75.2 9.6 %collective-permute-start = (f32[4,256,128]{2,0,1:T(4,128)S(1)}, f32[4,256,128]{2,0,1:T(4,128)S(1)}, u32[]{:S(2)}, u32[]{:S(2)}) collective-permute-start(f32[4,256,128]{2,0,1:T(4,128)S(1)} %convolution_add_fusion.2), channel_id=1, source_target_pairs={{0,28},{4,0},{8,4},{12,8},{16,12},{20,16},{24,20},{28,24},{1,29},{... | collective-permute-start | bytes 1572872 | tf_op jit(solution)/shard_map/while/body/eval_jaxpr/ppermute | solution.py:15
  90.1 9.6 %collective-permute-start = (f32[4,256,128]{2,0,1:T(4,128)S(1)}, f32[4,256,128]{2,0,1:T(4,128)S(1)}, u32[]{:S(2)}, u32[]{:S(2)}) collective-permute-start(f32[4,256,128]{2,0,1:T(4,128)S(1)} %convolution_add_fusion.2), channel_id=1, source_target_pairs={{0,28},{4,0},{8,4},{12,8},{16,12},{20,16},{24,20},{28,24},{1,29},{... | collective-permute-start | bytes 1572872 | tf_op jit(solution)/shard_map/while/body/eval_jaxpr/ppermute | solution.py:15
  105.1 9.6 %collective-permute-start = (f32[4,256,128]{2,0,1:T(4,128)S(1)}, f32[4,256,128]{2,0,1:T(4,128)S(1)}, u32[]{:S(2)}, u32[]{:S(2)}) collective-permute-start(f32[4,256,128]{2,0,1:T(4,128)S(1)} %convolution_add_fusion.2), channel_id=1, source_target_pairs={{0,28},{4,0},{8,4},{12,8},{16,12},{20,16},{24,20},{28,24},{1,29},{... | collective-permute-start | bytes 1572872 | tf_op jit(solution)/shard_map/while/body/eval_jaxpr/ppermute | solution.py:15
  120.0 9.6 %collective-permute-start = (f32[4,256,128]{2,0,1:T(4,128)S(1)}, f32[4,256,128]{2,0,1:T(4,128)S(1)}, u32[]{:S(2)}, u32[]{:S(2)}) collective-permute-start(f32[4,256,128]{2,0,1:T(4,128)S(1)} %convolution_add_fusion.2), channel_id=1, source_target_pairs={{0,28},{4,0},{8,4},{12,8},{16,12},{20,16},{24,20},{28,24},{1,29},{... | collective-permute-start | bytes 1572872 | tf_op jit(solution)/shard_map/while/body/eval_jaxpr/ppermute | solution.py:15
  134.9 9.6 %collective-permute-start = (f32[4,256,128]{2,0,1:T(4,128)S(1)}, f32[4,256,128]{2,0,1:T(4,128)S(1)}, u32[]{:S(2)}, u32[]{:S(2)}) collective-permute-start(f32[4,256,128]{2,0,1:T(4,128)S(1)} %convolution_add_fusion.2), channel_id=1, source_target_pairs={{0,28},{4,0},{8,4},{12,8},{16,12},{20,16},{24,20},{28,24},{1,29},{... | collective-permute-start | bytes 1572872 | tf_op jit(solution)/shard_map/while/body/eval_jaxpr/ppermute | solution.py:15
  149.8 9.6 %collective-permute-start = (f32[4,256,128]{2,0,1:T(4,128)S(1)}, f32[4,256,128]{2,0,1:T(4,128)S(1)}, u32[]{:S(2)}, u32[]{:S(2)}) collective-permute-start(f32[4,256,128]{2,0,1:T(4,128)S(1)} %convolution_add_fusion.2), channel_id=1, source_target_pairs={{0,28},{4,0},{8,4},{12,8},{16,12},{20,16},{24,20},{28,24},{1,29},{... | collective-permute-start | bytes 1572872 | tf_op jit(solution)/shard_map/while/body/eval_jaxpr/ppermute | solution.py:15
  164.8 9.6 %collective-permute-start = (f32[4,256,128]{2,0,1:T(4,128)S(1)}, f32[4,256,128]{2,0,1:T(4,128)S(1)}, u32[]{:S(2)}, u32[]{:S(2)}) collective-permute-start(f32[4,256,128]{2,0,1:T(4,128)S(1)} %convolution_add_fusion.2), channel_id=1, source_target_pairs={{0,28},{4,0},{8,4},{12,8},{16,12},{20,16},{24,20},{28,24},{1,29},{... | collective-permute-start | bytes 1572872 | tf_op jit(solution)/shard_map/while/body/eval_jaxpr/ppermute | solution.py:15
  179.7 9.6 %collective-permute-start = (f32[4,256,128]{2,0,1:T(4,128)S(1)}, f32[4,256,128]{2,0,1:T(4,128)S(1)}, u32[]{:S(2)}, u32[]{:S(2)}) collective-permute-start(f32[4,256,128]{2,0,1:T(4,128)S(1)} %convolution_add_fusion.2), channel_id=1, source_target_pairs={{0,28},{4,0},{8,4},{12,8},{16,12},{20,16},{24,20},{28,24},{1,29},{... | collective-permute-start | bytes 1572872 | tf_op jit(solution)/shard_map/while/body/eval_jaxpr/ppermute | solution.py:15
  194.6 9.6 %collective-permute-start = (f32[4,256,128]{2,0,1:T(4,128)S(1)}, f32[4,256,128]{2,0,1:T(4,128)S(1)}, u32[]{:S(2)}, u32[]{:S(2)}) collective-permute-start(f32[4,256,128]{2,0,1:T(4,128)S(1)} %convolution_add_fusion.2), channel_id=1, source_target_pairs={{0,28},{4,0},{8,4},{12,8},{16,12},{20,16},{24,20},{28,24},{1,29},{... | collective-permute-start | bytes 1572872 | tf_op jit(solution)/shard_map/while/body/eval_jaxpr/ppermute | solution.py:15
  209.5 9.6 %collective-permute-start = (f32[4,256,128]{2,0,1:T(4,128)S(1)}, f32[4,256,128]{2,0,1:T(4,128)S(1)}, u32[]{:S(2)}, u32[]{:S(2)}) collective-permute-start(f32[4,256,128]{2,0,1:T(4,128)S(1)} %convolution_add_fusion.2), channel_id=1, source_target_pairs={{0,28},{4,0},{8,4},{12,8},{16,12},{20,16},{24,20},{28,24},{1,29},{... | collective-permute-start | bytes 1572872 | tf_op jit(solution)/shard_map/while/body/eval_jaxpr/ppermute | solution.py:15
  224.5 9.6 %collective-permute-start = (f32[4,256,128]{2,0,1:T(4,128)S(1)}, f32[4,256,128]{2,0,1:T(4,128)S(1)}, u32[]{:S(2)}, u32[]{:S(2)}) collective-permute-start(f32[4,256,128]{2,0,1:T(4,128)S(1)} %convolution_add_fusion.2), channel_id=1, source_target_pairs={{0,28},{4,0},{8,4},{12,8},{16,12},{20,16},{24,20},{28,24},{1,29},{... | collective-permute-start | bytes 1572872 | tf_op jit(solution)/shard_map/while/body/eval_jaxpr/ppermute | solution.py:15
  239.4 9.6 %collective-permute-start = (f32[4,256,128]{2,0,1:T(4,128)S(1)}, f32[4,256,128]{2,0,1:T(4,128)S(1)}, u32[]{:S(2)}, u32[]{:S(2)}) collective-permute-start(f32[4,256,128]{2,0,1:T(4,128)S(1)} %convolution_add_fusion.2), channel_id=1, source_target_pairs={{0,28},{4,0},{8,4},{12,8},{16,12},{20,16},{24,20},{28,24},{1,29},{... | collective-permute-start | bytes 1572872 | tf_op jit(solution)/shard_map/while/body/eval_jaxpr/ppermute | solution.py:15
  254.3 9.6 %collective-permute-start = (f32[4,256,128]{2,0,1:T(4,128)S(1)}, f32[4,256,128]{2,0,1:T(4,128)S(1)}, u32[]{:S(2)}, u32[]{:S(2)}) collective-permute-start(f32[4,256,128]{2,0,1:T(4,128)S(1)} %convolution_add_fusion.2), channel_id=1, source_target_pairs={{0,28},{4,0},{8,4},{12,8},{16,12},{20,16},{24,20},{28,24},{1,29},{... | collective-permute-start | bytes 1572872 | tf_op jit(solution)/shard_map/while/body/eval_jaxpr/ppermute | solution.py:15
  269.3 9.6 %collective-permute-start = (f32[4,256,128]{2,0,1:T(4,128)S(1)}, f32[4,256,128]{2,0,1:T(4,128)S(1)}, u32[]{:S(2)}, u32[]{:S(2)}) collective-permute-start(f32[4,256,128]{2,0,1:T(4,128)S(1)} %convolution_add_fusion.2), channel_id=1, source_target_pairs={{0,28},{4,0},{8,4},{12,8},{16,12},{20,16},{24,20},{28,24},{1,29},{... | collective-permute-start | bytes 1572872 | tf_op jit(solution)/shard_map/while/body/eval_jaxpr/ppermute | solution.py:15
  284.2 9.6 %collective-permute-start = (f32[4,256,128]{2,0,1:T(4,128)S(1)}, f32[4,256,128]{2,0,1:T(4,128)S(1)}, u32[]{:S(2)}, u32[]{:S(2)}) collective-permute-start(f32[4,256,128]{2,0,1:T(4,128)S(1)} %convolution_add_fusion.2), channel_id=1, source_target_pairs={{0,28},{4,0},{8,4},{12,8},{16,12},{20,16},{24,20},{28,24},{1,29},{... | collective-permute-start | bytes 1572872 | tf_op jit(solution)/shard_map/while/body/eval_jaxpr/ppermute | solution.py:15
  299.1 9.6 %collective-permute-start = (f32[4,256,128]{2,0,1:T(4,128)S(1)}, f32[4,256,128]{2,0,1:T(4,128)S(1)}, u32[]{:S(2)}, u32[]{:S(2)}) collective-permute-start(f32[4,256,128]{2,0,1:T(4,128)S(1)} %convolution_add_fusion.2), channel_id=1, source_target_pairs={{0,28},{4,0},{8,4},{12,8},{16,12},{20,16},{24,20},{28,24},{1,29},{... | collective-permute-start | bytes 1572872 | tf_op jit(solution)/shard_map/while/body/eval_jaxpr/ppermute | solution.py:15
  314.0 9.6 %collective-permute-start = (f32[4,256,128]{2,0,1:T(4,128)S(1)}, f32[4,256,128]{2,0,1:T(4,128)S(1)}, u32[]{:S(2)}, u32[]{:S(2)}) collective-permute-start(f32[4,256,128]{2,0,1:T(4,128)S(1)} %convolution_add_fusion.2), channel_id=1, source_target_pairs={{0,28},{4,0},{8,4},{12,8},{16,12},{20,16},{24,20},{28,24},{1,29},{... | collective-permute-start | bytes 1572872 | tf_op jit(solution)/shard_map/while/body/eval_jaxpr/ppermute | solution.py:15
  329.0 9.6 %collective-permute-start = (f32[4,256,128]{2,0,1:T(4,128)S(1)}, f32[4,256,128]{2,0,1:T(4,128)S(1)}, u32[]{:S(2)}, u32[]{:S(2)}) collective-permute-start(f32[4,256,128]{2,0,1:T(4,128)S(1)} %convolution_add_fusion.2), channel_id=1, source_target_pairs={{0,28},{4,0},{8,4},{12,8},{16,12},{20,16},{24,20},{28,24},{1,29},{... | collective-permute-start | bytes 1572872 | tf_op jit(solution)/shard_map/while/body/eval_jaxpr/ppermute | solution.py:15
  343.9 9.6 %collective-permute-start = (f32[4,256,128]{2,0,1:T(4,128)S(1)}, f32[4,256,128]{2,0,1:T(4,128)S(1)}, u32[]{:S(2)}, u32[]{:S(2)}) collective-permute-start(f32[4,256,128]{2,0,1:T(4,128)S(1)} %convolution_add_fusion.2), channel_id=1, source_target_pairs={{0,28},{4,0},{8,4},{12,8},{16,12},{20,16},{24,20},{28,24},{1,29},{... | collective-permute-start | bytes 1572872 | tf_op jit(solution)/shard_map/while/body/eval_jaxpr/ppermute | solution.py:15
  358.8 9.6 %collective-permute-start = (f32[4,256,128]{2,0,1:T(4,128)S(1)}, f32[4,256,128]{2,0,1:T(4,128)S(1)}, u32[]{:S(2)}, u32[]{:S(2)}) collective-permute-start(f32[4,256,128]{2,0,1:T(4,128)S(1)} %convolution_add_fusion.2), channel_id=1, source_target_pairs={{0,28},{4,0},{8,4},{12,8},{16,12},{20,16},{24,20},{28,24},{1,29},{... | collective-permute-start | bytes 1572872 | tf_op jit(solution)/shard_map/while/body/eval_jaxpr/ppermute | solution.py:15
  373.7 9.6 %collective-permute-start = (f32[4,256,128]{2,0,1:T(4,128)S(1)}, f32[4,256,128]{2,0,1:T(4,128)S(1)}, u32[]{:S(2)}, u32[]{:S(2)}) collective-permute-start(f32[4,256,128]{2,0,1:T(4,128)S(1)} %convolution_add_fusion.2), channel_id=1, source_target_pairs={{0,28},{4,0},{8,4},{12,8},{16,12},{20,16},{24,20},{28,24},{1,29},{... | collective-permute-start | bytes 1572872 | tf_op jit(solution)/shard_map/while/body/eval_jaxpr/ppermute | solution.py:15
  388.7 9.6 %collective-permute-start = (f32[4,256,128]{2,0,1:T(4,128)S(1)}, f32[4,256,128]{2,0,1:T(4,128)S(1)}, u32[]{:S(2)}, u32[]{:S(2)}) collective-permute-start(f32[4,256,128]{2,0,1:T(4,128)S(1)} %convolution_add_fusion.2), channel_id=1, source_target_pairs={{0,28},{4,0},{8,4},{12,8},{16,12},{20,16},{24,20},{28,24},{1,29},{... | collective-permute-start | bytes 1572872 | tf_op jit(solution)/shard_map/while/body/eval_jaxpr/ppermute | solution.py:15
  403.6 9.6 %collective-permute-start = (f32[4,256,128]{2,0,1:T(4,128)S(1)}, f32[4,256,128]{2,0,1:T(4,128)S(1)}, u32[]{:S(2)}, u32[]{:S(2)}) collective-permute-start(f32[4,256,128]{2,0,1:T(4,128)S(1)} %convolution_add_fusion.2), channel_id=1, source_target_pairs={{0,28},{4,0},{8,4},{12,8},{16,12},{20,16},{24,20},{28,24},{1,29},{... | collective-permute-start | bytes 1572872 | tf_op jit(solution)/shard_map/while/body/eval_jaxpr/ppermute | solution.py:15
  418.5 9.6 %collective-permute-start = (f32[4,256,128]{2,0,1:T(4,128)S(1)}, f32[4,256,128]{2,0,1:T(4,128)S(1)}, u32[]{:S(2)}, u32[]{:S(2)}) collective-permute-start(f32[4,256,128]{2,0,1:T(4,128)S(1)} %convolution_add_fusion.2), channel_id=1, source_target_pairs={{0,28},{4,0},{8,4},{12,8},{16,12},{20,16},{24,20},{28,24},{1,29},{... | collective-permute-start | bytes 1572872 | tf_op jit(solution)/shard_map/while/body/eval_jaxpr/ppermute | solution.py:15
  433.5 9.6 %collective-permute-start = (f32[4,256,128]{2,0,1:T(4,128)S(1)}, f32[4,256,128]{2,0,1:T(4,128)S(1)}, u32[]{:S(2)}, u32[]{:S(2)}) collective-permute-start(f32[4,256,128]{2,0,1:T(4,128)S(1)} %convolution_add_fusion.2), channel_id=1, source_target_pairs={{0,28},{4,0},{8,4},{12,8},{16,12},{20,16},{24,20},{28,24},{1,29},{... | collective-permute-start | bytes 1572872 | tf_op jit(solution)/shard_map/while/body/eval_jaxpr/ppermute | solution.py:15
  448.4 9.6 %collective-permute-start = (f32[4,256,128]{2,0,1:T(4,128)S(1)}, f32[4,256,128]{2,0,1:T(4,128)S(1)}, u32[]{:S(2)}, u32[]{:S(2)}) collective-permute-start(f32[4,256,128]{2,0,1:T(4,128)S(1)} %convolution_add_fusion.2), channel_id=1, source_target_pairs={{0,28},{4,0},{8,4},{12,8},{16,12},{20,16},{24,20},{28,24},{1,29},{... | collective-permute-start | bytes 1572872 | tf_op jit(solution)/shard_map/while/body/eval_jaxpr/ppermute | solution.py:15
  463.3 9.6 %collective-permute-start = (f32[4,256,128]{2,0,1:T(4,128)S(1)}, f32[4,256,128]{2,0,1:T(4,128)S(1)}, u32[]{:S(2)}, u32[]{:S(2)}) collective-permute-start(f32[4,256,128]{2,0,1:T(4,128)S(1)} %convolution_add_fusion.2), channel_id=1, source_target_pairs={{0,28},{4,0},{8,4},{12,8},{16,12},{20,16},{24,20},{28,24},{1,29},{... | collective-permute-start | bytes 1572872 | tf_op jit(solution)/shard_map/while/body/eval_jaxpr/ppermute | solution.py:15
  478.2 9.6 %collective-permute-start = (f32[4,256,128]{2,0,1:T(4,128)S(1)}, f32[4,256,128]{2,0,1:T(4,128)S(1)}, u32[]{:S(2)}, u32[]{:S(2)}) collective-permute-start(f32[4,256,128]{2,0,1:T(4,128)S(1)} %convolution_add_fusion.2), channel_id=1, source_target_pairs={{0,28},{4,0},{8,4},{12,8},{16,12},{20,16},{24,20},{28,24},{1,29},{... | collective-permute-start | bytes 1572872 | tf_op jit(solution)/shard_map/while/body/eval_jaxpr/ppermute | solution.py:15
  487.8 38.6 %copy-start = (f32[4,256,128]{2,1,0:T(8,128)}, f32[4,256,128]{2,1,0:T(8,128)S(1)}, u32[]{:S(2)}) copy-start(f32[4,256,128]{2,1,0:T(8,128)S(1)} %get-tuple-element.255) | copy-start | bytes 1572868
Sparse Core Ops, SparseCore 0:
  490.0 34.9 reduce-scatter.1
where the time goes:
time: 536 us; the launch traced here: 533 us
  waiting for transfers between devices  233 us (43%)
  matrix products  158 us (29%)
  starting transfers between devices  92 us (17%)
  between operations  14.8 us (3%)
  blocking collectives  14.6 us (3%)
  other arithmetic  11.6 us (2%)
  local copies, waits for them, and re-layouts  7.35 us (1%)
    ppermute x32, waiting for transfers between devices, shifted(): lax.ppermute(value, axis, [(i, (i + by) % size) for i in range(size)])  214 us
    ppermute x32, starting transfers between devices, shifted(): lax.ppermute(value, axis, [(i, (i + by) % size) for i in range(size)])  92 us
    dot_general x32, matrix products, advance(): updates = jnp.einsum('kab,as->kbs', blocks_now, solved, precision=precise)  81.2 us
    dot_general x32, matrix products, advance(): jnp.einsum('ab,as->bs', inverse_now, source - pending[0], precision=precise)  49.5 us
    dot_general x32, matrix products, advance(): added_terms = jnp.einsum('kw,kbs->wbs', routing, updates, precision=precise)  24.7 us
    reduce_scatter x1, waiting for transfers between devices, body(): lax.psum_scatter(numerator, 'blk', scatter_dimension=0, tiled=True)  18.8 us
    unnamed x1, blocking collectives  14.6 us
  transfers between devices with their start and end apart: 33, of which 33 were waited for; matrix products, arithmetic and copies ran while one was open for 0% of the time, Pallas kernels for 0%

commit v1 on v0

v1 whole, which is shorter than its diff:
```python
import functools

import jax
import jax.numpy as jnp
from jax import lax
from jax.experimental import pallas as pl
from jax.experimental.pallas import tpu as pltpu
from jax.sharding import PartitionSpec as P

NDIST = 256
F32 = jnp.float32
B16 = jnp.bfloat16
VMEM_BYTES = 20 * 1024 * 1024
SMEM_SPEC = pl.BlockSpec(memory_space=pltpu.SMEM)
VMEM_SPEC = pl.BlockSpec(memory_space=pltpu.VMEM)


def params():
    return pltpu.CompilerParams(vmem_limit_bytes=VMEM_BYTES)


def cost(flops, moved):
    return pl.CostEstimate(flops=flops, bytes_accessed=moved, transcendentals=0)


def halves(x):
    hi = x.astype(B16)
    lo = (x - hi.astype(F32)).astype(B16)
    return hi, lo


def dot(a, b):
    return jnp.dot(a, b, preferred_element_type=F32)


def dot3(x, y):
    rows = x[0].shape[0]
    both = dot(jnp.concatenate([x[0], x[1]], axis=0), y[0])
    return both[:rows] + both[rows:] + dot(x[0], y[1])


def setup_kernel(s, own_l, oth_l, own_d, oth_d, own_r, oth_r, gh, gl, mh, ml, rt):
    is_a = s[0] == 1
    bs = own_l.shape[1]
    half = rt.shape[0]

    def upper(k):
        return jnp.where(is_a, own_l[k], oth_l[k])

    def lower(k):
        return jnp.where(is_a, oth_l[k], own_l[k])

    def at_distance(block, row, first_col, d):
        found = jnp.zeros((bs, bs), F32)
        for k in range(1, own_l.shape[0]):
            col = s[first_col + k]
            found = jnp.where((col == row - d) & (col >= 0), block(k), found)
        return found

    row_a, row_b = s[1], s[2]
    col_a, col_b = 3, 3 + own_l.shape[0]
    da = halves(jnp.where(is_a, own_d[...], oth_d[...]))
    db = halves(jnp.where(is_a, oth_d[...], own_d[...]))
    la1 = halves(upper(0))
    lb1 = halves(jnp.where(s[col_b] >= 0, lower(0), 0.0))
    la2 = halves(at_distance(upper, row_a, col_a, 2))
    la3 = halves(at_distance(upper, row_a, col_a, 3))
    la4 = halves(at_distance(upper, row_a, col_a, 4))
    lb2 = halves(at_distance(lower, row_b, col_b, 2))
    lb3 = halves(at_distance(lower, row_b, col_b, 3))
    lb4 = halves(at_distance(lower, row_b, col_b, 4))
    for place, pair in enumerate((da, db, la1, la4, lb3, lb4)):
        mh[place] = pair[0]
        ml[place] = pair[1]

    def put(i, j, value):
        hi, lo = halves(value)
        gh[i * bs : (i + 1) * bs, j * bs : (j + 1) * bs] = hi
        gl[i * bs : (i + 1) * bs, j * bs : (j + 1) * bs] = lo

    w = halves(dot3(da, la1))
    b_hi = dot3(db, lb1)
    b_lo = dot3(db, lb2)
    put(1, 0, b_hi)
    put(1, 1, b_lo)
    put(0, 0, dot3(da, la2) - dot3(w, halves(b_hi)))
    put(0, 1, dot3(da, la3) - dot3(w, halves(b_lo)))
    ra = jnp.where(is_a, own_r[...], oth_r[...]).T
    rb = jnp.where(is_a, oth_r[...], own_r[...]).T
    rt[:, :bs] = jnp.where(is_a, ra[half:], ra[:half])
    rt[:, bs:] = jnp.where(is_a, rb[half:], rb[:half])


def near_kernel(has_near, has_far, r_ref, *refs):
    refs = list(refs)
    v = r_ref[...]
    if has_far:
        v = v - refs.pop(0)[...]
    if has_near:
        v = v - refs.pop(0)[...]
    gh, gl, near, v_out = refs
    v_out[...] = v
    near[...] = dot3(halves(v), (gh[...], gl[...]))


def far_kernel(s, v_ref, mh, ml, keep_in, give_in, far, keep, give):
    is_a = s[0] == 1
    active = s[1] == 1
    bs = mh.shape[1]

    def m(k):
        return mh[k], ml[k]

    xa = dot3(halves(v_ref[:, :bs]), m(0))
    xah = halves(xa)
    xb = dot3(halves(v_ref[:, bs:] - dot3(xah, m(2))), m(1))
    xbh = halves(xb)
    far[:, :bs] = dot3(xah, m(3)) + dot3(xbh, m(4))
    far[:, bs:] = dot3(xbh, m(5))
    keep[...] = jnp.where(active, jnp.where(is_a, xa, xb), keep_in[...])
    give[...] = jnp.where(active, jnp.where(is_a, xb, xa), give_in[...])


def district_kernel(rows_here, *refs):
    keeps = refs[:rows_here]
    gives = refs[rows_here : 2 * rows_here]
    own_w, oth_w, own_d, oth_d, out = refs[2 * rows_here :]
    half, bs = keeps[0].shape
    names = lax.broadcasted_iota(jnp.int32, (NDIST, bs), 0)
    total = jnp.zeros((NDIST, 2 * half), F32)
    for r in range(rows_here):
        for x, w, d in ((keeps[r], own_w, own_d), (gives[r], oth_w, oth_d)):
            wr = w[r : r + 1, :]
            member = (names == d[r : r + 1, :]).astype(F32).astype(B16)
            terms = jnp.concatenate(
                [x[...] * wr, jnp.broadcast_to(wr, (half, bs))], axis=0
            )
            for part in halves(terms):
                total = total + lax.dot_general(
                    member, part, (((1,), (1,)), ((), ())), preferred_element_type=F32
                )
    out[...] = total


def field_kernel(rows_here, s, *refs):
    keeps = refs[:rows_here]
    gots = refs[rows_here : 2 * rows_here]
    out = refs[2 * rows_here]
    is_a = s[0] == 1
    for r in range(rows_here):
        top = jnp.where(is_a, gots[r][...], keeps[r][...])
        bottom = jnp.where(is_a, keeps[r][...], gots[r][...])
        out[r, 0] = jnp.concatenate([top, bottom], axis=0).T


def mean_kernel(x, out):
    half = x.shape[2] // 2
    sums = [x[0], x[1]]
    for k in range(2, x.shape[0]):
        sums[k % 2] = sums[k % 2] + x[k]
    out[...] = jnp.concatenate([t[:, :half] / t[:, half:] for t in sums], axis=1)


def body(rhs, lower_blocks, col_index, diag_inverse, turnout, district_of):
    n = lax.axis_size("blk")
    p = lax.axis_index("blk").astype(jnp.int32)
    pairs = n // 2
    core = lax.rem(p, 2)
    chip = lax.div(p, 2)
    rows_here, _, bs, columns = rhs.shape
    slots = lower_blocks.shape[2]
    half = columns // 2
    count = rows_here * pairs

    def shaped(*shape, dtype=F32):
        return jax.ShapeDtypeStruct(shape, dtype)

    def swap(x):
        return lax.ppermute(x, "blk", [(i, i ^ 1) for i in range(n)])

    def pass_on(x, by):
        perm = [(i, (i - 2 * by) % n) for i in range(n)]
        return lax.ppermute(x, "blk", perm)

    own_col = col_index[:, 0]
    oth_col = swap(own_col)
    col_a = jnp.where(core == 1, own_col, oth_col)
    col_b = jnp.where(core == 1, oth_col, own_col)

    fixed = {}
    arrived = None
    for r in range(rows_here - 1, -1, -1):
        own = (lower_blocks[r, 0], diag_inverse[r, 0], rhs[r, 0])
        if arrived is not None:
            own, _ = lax.optimization_barrier((own, arrived))
        oth = tuple(swap(x) for x in own)
        arrived = oth
        row_b = r * n + 2 * chip
        scalars = jnp.concatenate(
            [jnp.stack([core, row_b + 1, row_b]), col_a[r], col_b[r]]
        ).astype(jnp.int32)
        fixed[r] = pl.pallas_call(
            setup_kernel,
            out_shape=(
                shaped(2 * bs, 2 * bs, dtype=B16),
                shaped(2 * bs, 2 * bs, dtype=B16),
                shaped(6, bs, bs, dtype=B16),
                shaped(6, bs, bs, dtype=B16),
                shaped(half, 2 * bs),
            ),
            in_specs=[SMEM_SPEC] + [VMEM_SPEC] * 6,
            out_specs=(VMEM_SPEC,) * 5,
            compiler_params=params(),
            cost_estimate=cost(14 * 3 * bs**3, 24 * bs * bs * 4),
            name="pair_setup",
        )(scalars, own[0], oth[0], own[1], oth[1], own[2], oth[2])

    own_w, own_d = turnout[:, 0], district_of[:, 0]
    oth_w, oth_d = swap(own_w), swap(own_d)

    keeps, gives = {}, {}
    near = far_now = far_next = None
    for step in range(count):
        k = count - 1 - step
        r = k // pairs
        gh, gl, mh, ml, rt = fixed[r]
        taken = [x for x in (far_now, near) if x is not None]
        near_out, v = pl.pallas_call(
            functools.partial(near_kernel, near is not None, far_now is not None),
            out_shape=(shaped(half, 2 * bs), shaped(half, 2 * bs)),
            in_specs=[VMEM_SPEC] * (3 + len(taken)),
            out_specs=(VMEM_SPEC,) * 2,
            compiler_params=params(),
            cost_estimate=cost(6 * half * 4 * bs * bs, 6 * half * bs * 4),
            name="near_terms",
        )(rt, *taken, gh, gl)
        near = pass_on(near_out, 1) if step + 1 < count else None
        if r not in keeps:
            keeps[r] = jnp.zeros((half, bs), F32)
            gives[r] = jnp.zeros((half, bs), F32)
        active = (chip == k % pairs).astype(jnp.int32)
        far_out, keeps[r], gives[r] = pl.pallas_call(
            far_kernel,
            out_shape=(shaped(half, 2 * bs), shaped(half, bs), shaped(half, bs)),
            in_specs=[SMEM_SPEC] + [VMEM_SPEC] * 5,
            out_specs=(VMEM_SPEC,) * 3,
            compiler_params=params(),
            cost_estimate=cost(6 * half * 6 * bs * bs, 8 * half * bs * 4),
            name="far_terms",
        )(jnp.stack([core, active]), v, mh, ml, keeps[r], gives[r])
        far_now = far_next
        far_next = pass_on(far_out, 2) if step + 2 < count else None

    order = range(rows_here)
    share = pl.pallas_call(
        functools.partial(district_kernel, rows_here),
        out_shape=shaped(NDIST, columns),
        in_specs=[VMEM_SPEC] * (2 * rows_here + 4),
        out_specs=VMEM_SPEC,
        compiler_params=params(),
        cost_estimate=cost(8 * rows_here * NDIST * bs * columns, 4 * rows_here * bs * columns),
        name="district_terms",
    )(
        *[keeps[r] for r in order],
        *[gives[r] for r in order],
        own_w, oth_w, own_d, oth_d,
    )
    parts = lax.all_to_all(share.reshape(n, NDIST // n, columns), "blk", 0, 0)
    gots = swap(jnp.stack([gives[r] for r in order]))
    field = pl.pallas_call(
        functools.partial(field_kernel, rows_here),
        out_shape=shaped(rows_here, 1, bs, columns),
        in_specs=[SMEM_SPEC] + [VMEM_SPEC] * (2 * rows_here),
        out_specs=VMEM_SPEC,
        compiler_params=params(),
        cost_estimate=cost(0, 8 * rows_here * bs * columns),
        name="field",
    )(core[None], *[keeps[r] for r in order], *[gots[r] for r in order])
    mean = pl.pallas_call(
        mean_kernel,
        out_shape=shaped(NDIST // n, columns),
        in_specs=[VMEM_SPEC],
        out_specs=VMEM_SPEC,
        compiler_params=params(),
        name="district_mean",
    )(parts)
    return field, mean


def solution(mesh):
    placed = (
        P(None, "blk", None, "sims"),
        P(None, "blk", None, None, None),
        P(None, "blk", None),
        P(None, "blk", None, None),
        P(None, "blk", None),
        P(None, "blk", None),
    )
    return jax.shard_map(
        body,
        mesh=mesh,
        in_specs=placed,
        out_specs=(P(None, "blk", None, "sims"), P("blk", "sims")),
        check_vma=False,
    )
```

time: 536 us -> 163 us (0.30)
  waiting for transfers between devices: 233 us -> 19.5 us
  matrix products: 158 us -> 0 us
  Pallas kernels: 0 us -> 48.7 us
  starting transfers between devices: 92 us -> 46 us
  local copies, waits for them, and re-layouts: 7.35 us -> 36.1 us
  between operations: 14.8 us -> 1.2 us
  other arithmetic: 11.6 us -> 0.32 us
    ppermute x32 -> x45, waiting for transfers between devices: 214 us -> 19.5 us  [the longest x29 15.7 us: pass_on(): return lax.ppermute(x, 'blk', perm)]
    dot_general x98 -> x0, matrix products: 158 us -> none  [the longest x32 81.2 us: advance(): updates = jnp.einsum('kab,as->kbs', blocks_now, solved, precision=precise)]
    pallas_call x0 -> x39, Pallas kernels: none -> 48.7 us  [the longest x16 24 us: body(): pl.pallas_call(far_kernel, out_shape=(shaped(half, 2 * bs), shaped(half,...]
    ppermute x32 -> x45, starting transfers between devices: 92 us -> 46 us  [the longest x29 42.7 us: pass_on(): return lax.ppermute(x, 'blk', perm)]
    unnamed x12 -> x117, local copies, waits for them, and re-layouts: 2.84 us -> 28.3 us
    reduce_scatter x1 -> x0, waiting for transfers between devices: 18.8 us -> none  [body(): lax.psum_scatter(numerator, 'blk', scatter_dimension=0, tiled=True)]
    unnamed x1 -> x0, blocking collectives: 14.6 us -> none
    all_to_all x0 -> x1, blocking collectives: none -> 9.95 us  [body(): parts = lax.all_to_all(share.reshape(n, NDIST // n, columns), 'blk', 0, 0)]
  transfers between devices with their start and end apart: 33 -> 45, of which waited for: 33 -> 12; matrix products, arithmetic and copies ran while one was open for 0% -> 3% of each run, Pallas kernels for 0% -> 28%
where the time goes in v1:
time: 163 us; the launch traced here: 162 us
  Pallas kernels  48.7 us (30%)
  starting transfers between devices  46 us (28%)
  local copies, waits for them, and re-layouts  36.1 us (22%)
  waiting for transfers between devices  19.5 us (12%)
  blocking collectives  9.95 us (6%)
    ppermute x29, starting transfers between devices, pass_on(): return lax.ppermute(x, 'blk', perm)  42.7 us
    unnamed x117, local copies, waits for them, and re-layouts  28.3 us
    pallas_call x16, Pallas kernels, body(): pl.pallas_call(far_kernel, out_shape=(shaped(half, 2 * bs), shaped(half,...  24 us
    ppermute x29, waiting for transfers between devices, pass_on(): return lax.ppermute(x, 'blk', perm)  15.7 us
    pallas_call x16, Pallas kernels, body(): pl.pallas_call(functools.partial(near_kernel, near is not None, far_now i...  13 us
    all_to_all x1, blocking collectives, body(): parts = lax.all_to_all(share.reshape(n, NDIST // n, columns), 'blk', 0, 0)  9.95 us
    pallas_call x4, Pallas kernels, body(): pl.pallas_call(setup_kernel, out_shape=(shaped(2 * bs, 2 * bs, dtype=B16)...  9.26 us
    squeeze x3, local copies, waits for them, and re-layouts, body(): own = (lower_blocks[r, 0], diag_inverse[r, 0], rhs[r, 0])  5.06 us
  transfers between devices with their start and end apart: 45, of which 12 were waited for; matrix products, arithmetic and copies ran while one was open for 3% of the time, Pallas kernels for 28%

profile of v1, /device:TPU:0, one launch (start us, length us, event | category | flops | bytes accessed | tf_op | source)
XLA Modules:
  0.0 161.8 jit_solution(4554960050607118753)
XLA Ops:
  0.6 3.4 %slice_bitcast_fusion = (f32[3,256,256]{2,1,0:T(8,128)S(1)}, f32[3,256,256]{2,1,0:T(8,128)}, f32[3,256,256]{2,1,0:T(8,128)}, f32[3,256,256]{2,1,0:T(8,128)}) fusion(f32[4,1,3,256,256]{4,3,2,1,0:T(8,128)} %param.7), kind=kLoop, calls=%fused_computation | loop fusion | bytes 6291456 | tf_op jit(solution)/shard_map/squeeze | solution.py:193
  11.4 1.7 %collective-permute-done = s32[4,3]{1,0:T(4,128)S(1)} collective-permute-done((s32[4,3]{1,0:T(4,128)S(1)}, s32[4,3]{1,0:T(4,128)S(1)}, u32[]{:S(2)}, u32[]{:S(2)}) %collective-permute-start) | collective-permute-done | bytes 80 | tf_op jit(solution)/shard_map/ppermute | solution.py:179
  19.3 1.7 %pair_setup.7 = (bf16[512,512]{1,0:T(8,128)(2,1)S(1)}, bf16[512,512]{1,0:T(8,128)(2,1)S(1)}, bf16[6,256,256]{2,1,0:T(8,128)(2,1)S(1)}, bf16[6,256,256]{2,1,0:T(8,128)(2,1)S(1)}, f32[64,512]{1,0:T(8,128)S(1)}) custom-call(s32[9]{0:T(128)S(1)} %concatenate.15.s, f32[3,256,256]{2,1,0:T(8,128)S(1)} %copy-done.3, f32[3,256,256]{2,1,0:T(8,128)S(1)} %copy-done.41, ...), custom_call_target="tpu_custom_call" | custom-call | flops 704643072 | bytes 6291456 | tf_op jit(solution)/shard_map/pair_setup/pallas_call | solution.py:202
  22.6 3.8 %collective-permute-start.13 = (f32[64,512]{1,0:T(8,128)}, f32[64,512]{1,0:T(8,128)S(1)}, u32[]{:S(2)}, u32[]{:S(2)}) collective-permute-start(f32[64,512]{1,0:T(8,128)} %get-tuple-element.123), channel_id=1, source_target_pairs={{0,24},{4,28},{8,0},{12,4},{16,8},{20,12},{24,16},{28,20},{1,25},{... | collective-permute-start | bytes 393224 | tf_op jit(solution)/shard_map/ppermute | solution.py:183
  27.5 1.9 %far_terms.16 = (f32[64,512]{1,0:T(8,128)}, f32[64,256]{1,0:T(8,128)S(1)}, f32[64,256]{1,0:T(8,128)S(1)}) custom-call(s32[2]{0:T(128)S(1)} %pad_add_fusion.2.s, f32[64,512]{1,0:T(8,128)S(1)} %copy-done.12, bf16[6,256,256]{2,1,0:T(8,128)(2,1)S(1)} %get-tuple-element.125.mh, bf16[6,256,256]{2,1,0:T(8,128)(2,1)S(1)} %get-tuple-element.126.ml, ...), custom_call_target="tpu_custom_call" | custom-call | flops 150994944 | bytes 524288 | tf_op jit(solution)/shard_map/far_terms/pallas_call | solution.py:242
  31.5 3.2 %collective-permute-start.16 = (f32[64,512]{1,0:T(8,128)}, f32[64,512]{1,0:T(8,128)}, u32[]{:S(2)}, u32[]{:S(2)}) collective-permute-start(f32[64,512]{1,0:T(8,128)} %get-tuple-element.132), channel_id=1, source_target_pairs={{0,24},{4,28},{8,0},{12,4},{16,8},{20,12},{24,16},{28,20},{1,25},{... | collective-permute-start | bytes 393224 | tf_op jit(solution)/shard_map/ppermute | solution.py:183
  36.5 1.9 %far_terms.17 = (f32[64,512]{1,0:T(8,128)}, f32[64,256]{1,0:T(8,128)S(1)}, f32[64,256]{1,0:T(8,128)S(1)}) custom-call(s32[2]{0:T(128)S(1)} %pad_add_fusion.1.s, f32[64,512]{1,0:T(8,128)S(1)} %copy-done.20, bf16[6,256,256]{2,1,0:T(8,128)(2,1)S(1)} %get-tuple-element.125.mh, bf16[6,256,256]{2,1,0:T(8,128)(2,1)S(1)} %get-tuple-element.126.ml, ...), custom_call_target="tpu_custom_call" | custom-call | flops 150994944 | bytes 524288 | tf_op jit(solution)/shard_map/far_terms/pallas_call | solution.py:242
  40.1 1.9 %near_terms.18 = (f32[64,512]{1,0:T(8,128)}, f32[64,512]{1,0:T(8,128)S(1)}) custom-call(f32[64,512]{1,0:T(8,128)S(1)} %get-tuple-element.120.r_ref, f32[64,512]{1,0:T(8,128)} %collective-permute-done.15.refs_0_, f32[64,512]{1,0:T(8,128)} %collective-permute-done.16.refs_1_, bf16[512,512]{1,0:T(8,128)(2,1)S(1)} %get-tuple-element.121.refs_0_.refs_1_.refs_2_, ...), custom_call_target="tpu_custom_call" | custom-call | flops 100663296 | bytes 393216 | tf_op jit(solution)/shard_map/near_terms/pallas_call | solution.py:228
  46.1 1.9 %far_terms.18 = (f32[64,512]{1,0:T(8,128)}, f32[64,256]{1,0:T(8,128)S(1)}, f32[64,256]{1,0:T(8,128)S(1)}) custom-call(s32[2]{0:T(128)S(1)} %pad_add_fusion.3.s, f32[64,512]{1,0:T(8,128)S(1)} %copy-done.18, bf16[6,256,256]{2,1,0:T(8,128)(2,1)S(1)} %get-tuple-element.125.mh, bf16[6,256,256]{2,1,0:T(8,128)(2,1)S(1)} %get-tuple-element.126.ml, ...), custom_call_target="tpu_custom_call" | custom-call | flops 150994944 | bytes 524288 | tf_op jit(solution)/shard_map/far_terms/pallas_call | solution.py:242
  48.7 1.8 %near_terms.19 = (f32[64,512]{1,0:T(8,128)}, f32[64,512]{1,0:T(8,128)S(1)}) custom-call(f32[64,512]{1,0:T(8,128)S(1)} %get-tuple-element.120.r_ref, f32[64,512]{1,0:T(8,128)S(1)} %collective-permute-done.14.refs_0_, f32[64,512]{1,0:T(8,128)} %collective-permute-done.17.refs_1_, bf16[512,512]{1,0:T(8,128)(2,1)S(1)} %get-tuple-element.121.refs_0_.refs_1_.refs_2_, ...), custom_call_target="tpu_custom_call" | custom-call | flops 100663296 | bytes 393216 | tf_op jit(solution)/shard_map/near_terms/pallas_call | solution.py:228
  51.2 2.0 %collective-permute-start.20 = (f32[64,512]{1,0:T(8,128)}, f32[64,512]{1,0:T(8,128)S(1)}, u32[]{:S(2)}, u32[]{:S(2)}) collective-permute-start(f32[64,512]{1,0:T(8,128)} %get-tuple-element.142), channel_id=1, source_target_pairs={{0,24},{4,28},{8,0},{12,4},{16,8},{20,12},{24,16},{28,20},{1,25},{... | collective-permute-start | bytes 393224 | tf_op jit(solution)/shard_map/ppermute | solution.py:183
  55.7 1.2 far_terms.19
  58.2 1.5 collective-permute-start.18
  59.7 2.8 %pair_setup.6 = (bf16[512,512]{1,0:T(8,128)(2,1)S(1)}, bf16[512,512]{1,0:T(8,128)(2,1)S(1)}, bf16[6,256,256]{2,1,0:T(8,128)(2,1)S(1)}, bf16[6,256,256]{2,1,0:T(8,128)(2,1)S(1)}, f32[64,512]{1,0:T(8,128)S(1)}) custom-call(s32[9]{0:T(128)S(1)} %concatenate.14.s, f32[3,256,256]{2,1,0:T(8,128)} %get-tuple-element.108.own_l, ...), custom_call_target="tpu_custom_call" | custom-call | flops 704643072 | bytes 6291456 | tf_op jit(solution)/shard_map/pair_setup/pallas_call | solution.py:202
  64.4 1.2 far_terms.20
  66.6 3.1 %collective-permute-done.21.refs_1_ = f32[64,512]{1,0:T(8,128)S(1)} collective-permute-done((f32[64,512]{1,0:T(8,128)S(1)}, f32[64,512]{1,0:T(8,128)S(1)}, u32[]{:S(2)}, u32[]{:S(2)}) %collective-permute-start.21) | collective-permute-done | bytes 131104 | tf_op jit(solution)/shard_map/ppermute | solution.py:183
  70.0 1.3 collective-permute-start.24
  71.4 1.2 far_terms.21
  73.7 1.5 collective-permute-done.24.refs_1_
  75.5 2.4 %collective-permute-start.25 = (f32[64,512]{1,0:T(8,128)S(1)}, f32[64,512]{1,0:T(8,128)S(1)}, u32[]{:S(2)}, u32[]{:S(2)}) collective-permute-start(f32[64,512]{1,0:T(8,128)S(1)} %get-tuple-element.155), channel_id=1, source_target_pairs={{0,24},{4,28},{8,0},{12,4},{16,8},{20,12},{24,16},{28,20},{1,25},{... | collective-permute-start | bytes 393224 | tf_op jit(solution)/shard_map/ppermute | solution.py:183
  77.9 1.9 %far_terms.22 = (f32[64,512]{1,0:T(8,128)}, f32[64,256]{1,0:T(8,128)S(1)}, f32[64,256]{1,0:T(8,128)S(1)}) custom-call(s32[2]{0:T(128)S(1)} %pad_add_fusion.3.s, f32[64,512]{1,0:T(8,128)S(1)} %get-tuple-element.157.v_ref, bf16[6,256,256]{2,1,0:T(8,128)(2,1)S(1)} %get-tuple-element.147.mh, bf16[6,256,256]{2,1,0:T(8,128)(2,1)S(1)} %get-tuple-element.148.ml, ...), custom_call_target="tpu_custom_call" | custom-call | flops 150994944 | bytes 524288 | tf_op jit(solution)/shard_map/far_terms/pallas_call | solution.py:242
  82.1 3.4 %collective-permute-start.28 = (f32[64,512]{1,0:T(8,128)}, f32[64,512]{1,0:T(8,128)}, u32[]{:S(2)}, u32[]{:S(2)}) collective-permute-start(f32[64,512]{1,0:T(8,128)} %get-tuple-element.164), channel_id=1, source_target_pairs={{0,24},{4,28},{8,0},{12,4},{16,8},{20,12},{24,16},{28,20},{1,25},{... | collective-permute-start | bytes 393224 | tf_op jit(solution)/shard_map/ppermute | solution.py:183
  85.5 1.2 concatenate.13.s
  88.5 1.2 far_terms.23
  95.9 2.3 %pair_setup.5 = (bf16[512,512]{1,0:T(8,128)(2,1)S(1)}, bf16[512,512]{1,0:T(8,128)(2,1)S(1)}, bf16[6,256,256]{2,1,0:T(8,128)(2,1)S(1)}, bf16[6,256,256]{2,1,0:T(8,128)(2,1)S(1)}, f32[64,512]{1,0:T(8,128)S(1)}) custom-call(s32[9]{0:T(128)S(1)} %copy-done.39, f32[3,256,256]{2,1,0:T(8,128)S(1)} %copy-done.1, f32[3,256,256]{2,1,0:T(8,128)} %collective-permute-done.7.oth_l, ...), custom_call_target="tpu_custom_call" | custom-call | flops 704643072 | bytes 6291456 | tf_op jit(solution)/shard_map/pair_setup/pallas_call | solution.py:202
  98.3 1.3 near_terms.24
  99.6 1.2 far_terms.24
  100.9 1.4 collective-permute-start.31
  102.3 3.4 %collective-permute-done.29.refs_1_ = f32[64,512]{1,0:T(8,128)S(1)} collective-permute-done((f32[64,512]{1,0:T(8,128)S(1)}, f32[64,512]{1,0:T(8,128)S(1)}, u32[]{:S(2)}, u32[]{:S(2)}) %collective-permute-start.29) | collective-permute-done | bytes 131104 | tf_op jit(solution)/shard_map/ppermute | solution.py:183
  106.4 1.2 far_terms.25
  107.6 1.2 collective-permute-start.30
  108.8 2.2 %collective-permute-done.32.refs_1_ = f32[64,512]{1,0:T(8,128)S(1)} collective-permute-done((f32[64,512]{1,0:T(8,128)S(1)}, f32[64,512]{1,0:T(8,128)S(1)}, u32[]{:S(2)}, u32[]{:S(2)}) %collective-permute-start.32) | collective-permute-done | bytes 131104 | tf_op jit(solution)/shard_map/ppermute | solution.py:183
  111.3 1.4 collective-permute-start.33
  112.7 1.9 %far_terms.26 = (f32[64,512]{1,0:T(8,128)}, f32[64,256]{1,0:T(8,128)S(1)}, f32[64,256]{1,0:T(8,128)S(1)}) custom-call(s32[2]{0:T(128)S(1)} %pad_add_fusion.3.s, f32[64,512]{1,0:T(8,128)S(1)} %get-tuple-element.179.v_ref, bf16[6,256,256]{2,1,0:T(8,128)(2,1)S(1)} %get-tuple-element.169.mh, bf16[6,256,256]{2,1,0:T(8,128)(2,1)S(1)} %get-tuple-element.170.ml, ...), custom_call_target="tpu_custom_call" | custom-call | flops 150994944 | bytes 524288 | tf_op jit(solution)/shard_map/far_terms/pallas_call | solution.py:242
  117.4 2.3 %collective-permute-start.36 = (f32[64,512]{1,0:T(8,128)}, f32[64,512]{1,0:T(8,128)S(1)}, u32[]{:S(2)}, u32[]{:S(2)}) collective-permute-start(f32[64,512]{1,0:T(8,128)} %get-tuple-element.186), channel_id=1, source_target_pairs={{0,24},{4,28},{8,0},{12,4},{16,8},{20,12},{24,16},{28,20},{1,25},{... | collective-permute-start | bytes 393224 | tf_op jit(solution)/shard_map/ppermute | solution.py:183
  119.9 1.2 far_terms.27
  121.1 2.1 %collective-permute-start.34 = (f32[64,512]{1,0:T(8,128)S(1)}, f32[64,512]{1,0:T(8,128)S(1)}, u32[]{:S(2)}, u32[]{:S(2)}) collective-permute-start(f32[64,512]{1,0:T(8,128)S(1)} %get-tuple-element.184), channel_id=1, source_target_pairs={{0,16},{4,20},{8,24},{12,28},{16,0},{20,4},{24,8},{28,12},{1,17},{... | collective-permute-start | bytes 393224 | tf_op jit(solution)/shard_map/ppermute | solution.py:183
  123.2 2.4 %pair_setup.4 = (bf16[512,512]{1,0:T(8,128)(2,1)S(1)}, bf16[512,512]{1,0:T(8,128)(2,1)S(1)}, bf16[6,256,256]{2,1,0:T(8,128)(2,1)S(1)}, bf16[6,256,256]{2,1,0:T(8,128)(2,1)S(1)}, f32[64,512]{1,0:T(8,128)S(1)}) custom-call(s32[9]{0:T(128)S(1)} %concatenate.12.s, f32[3,256,256]{2,1,0:T(8,128)S(1)} %copy-done, f32[3,256,256]{2,1,0:T(8,128)} %collective-permute-done.10.oth_l, ...), custom_call_target="tpu_custom_call" | custom-call | flops 704643072 | bytes 6291456 | tf_op jit(solution)/shard_map/pair_setup/pallas_call | solution.py:202
  126.0 1.8 %collective-permute-start.37 = (f32[64,512]{1,0:T(8,128)S(1)}, f32[64,512]{1,0:T(8,128)S(1)}, u32[]{:S(2)}, u32[]{:S(2)}) collective-permute-start(f32[64,512]{1,0:T(8,128)S(1)} %get-tuple-element.189), channel_id=1, source_target_pairs={{0,24},{4,28},{8,0},{12,4},{16,8},{20,12},{24,16},{28,20},{1,25},{... | collective-permute-start | bytes 393224 | tf_op jit(solution)/shard_map/ppermute | solution.py:183
  127.8 1.2 far_terms.28
  129.6 2.1 %collective-permute-done.37.refs_1_ = f32[64,512]{1,0:T(8,128)S(1)} collective-permute-done((f32[64,512]{1,0:T(8,128)S(1)}, f32[64,512]{1,0:T(8,128)S(1)}, u32[]{:S(2)}, u32[]{:S(2)}) %collective-permute-start.37) | collective-permute-done | bytes 131104 | tf_op jit(solution)/shard_map/ppermute | solution.py:183
  132.0 3.1 %collective-permute-start.40 = (f32[64,512]{1,0:T(8,128)S(1)}, f32[64,512]{1,0:T(8,128)S(1)}, u32[]{:S(2)}, u32[]{:S(2)}) collective-permute-start(f32[64,512]{1,0:T(8,128)S(1)} %get-tuple-element.198), channel_id=1, source_target_pairs={{0,24},{4,28},{8,0},{12,4},{16,8},{20,12},{24,16},{28,20},{1,25},{... | collective-permute-start | bytes 393224 | tf_op jit(solution)/shard_map/ppermute | solution.py:183
  135.2 1.2 far_terms.29
  136.5 1.8 %collective-permute-done.40.refs_1_ = f32[64,512]{1,0:T(8,128)S(1)} collective-permute-done((f32[64,512]{1,0:T(8,128)S(1)}, f32[64,512]{1,0:T(8,128)S(1)}, u32[]{:S(2)}, u32[]{:S(2)}) %collective-permute-start.40) | collective-permute-done | bytes 131104 | tf_op jit(solution)/shard_map/ppermute | solution.py:183
  138.6 3.5 %collective-permute-start.41 = (f32[64,512]{1,0:T(8,128)S(1)}, f32[64,512]{1,0:T(8,128)S(1)}, u32[]{:S(2)}, u32[]{:S(2)}) collective-permute-start(f32[64,512]{1,0:T(8,128)S(1)} %get-tuple-element.199), channel_id=1, source_target_pairs={{0,24},{4,28},{8,0},{12,4},{16,8},{20,12},{24,16},{28,20},{1,25},{... | collective-permute-start | bytes 393224 | tf_op jit(solution)/shard_map/ppermute | solution.py:183
  142.2 1.9 %far_terms.30 = (f32[64,512]{1,0:T(8,128)}, f32[64,256]{1,0:T(8,128)S(1)}, f32[64,256]{1,0:T(8,128)S(1)}) custom-call(s32[2]{0:T(128)S(1)} %pad_add_fusion.3.s, f32[64,512]{1,0:T(8,128)S(1)} %get-tuple-element.201.v_ref, bf16[6,256,256]{2,1,0:T(8,128)(2,1)S(1)} %get-tuple-element.191.mh, bf16[6,256,256]{2,1,0:T(8,128)(2,1)S(1)} %get-tuple-element.192.ml, ...), custom_call_target="tpu_custom_call" | custom-call | flops 150994944 | bytes 524288 | tf_op jit(solution)/shard_map/far_terms/pallas_call | solution.py:242
  145.7 1.9 %far_terms.31 = (f32[64,512]{1,0:T(8,128)}, f32[64,256]{1,0:T(8,128)S(1)}, f32[64,256]{1,0:T(8,128)S(1)}) custom-call(s32[2]{0:T(128)S(1)} %pad_add_fusion.s, f32[64,512]{1,0:T(8,128)S(1)} %get-tuple-element.200.v_ref, bf16[6,256,256]{2,1,0:T(8,128)(2,1)S(1)} %get-tuple-element.191.mh, bf16[6,256,256]{2,1,0:T(8,128)(2,1)S(1)} %get-tuple-element.192.ml, ...), custom_call_target="tpu_custom_call" | custom-call | flops 150994944 | bytes 524288 | tf_op jit(solution)/shard_map/far_terms/pallas_call | solution.py:242
  150.1 9.9 %all_to_all.5.x = f32[8,32,128]{2,1,0:T(8,128)S(1)} all-to-all(f32[8,32,128]{2,1,0:T(8,128)S(1)} %bitcast.75), channel_id=1, replica_groups=mesh['blk'=8,'sims'=4] {'blk'}, dimensions={0} | all-to-all | bytes 262144 | tf_op jit(solution)/shard_map/all_to_all | solution.py:268
  (215 shorter events, 57.3 us)
Async XLA Ops:
  4.1 5.8 %collective-permute-start.1 = (f32[3,256,256]{2,1,0:T(8,128)S(1)}, f32[3,256,256]{2,1,0:T(8,128)S(1)}, u32[]{:S(2)}, u32[]{:S(2)}) collective-permute-start(f32[3,256,256]{2,1,0:T(8,128)S(1)} %get-tuple-element.214.own_l), channel_id=1, source_target_pairs={{0,4},{4,0},{8,12},{12,8},{16,20},{20,16},{24,28},{28,24},{1,5},{5... | collective-permute-start | bytes 2359304 | tf_op jit(solution)/shard_map/ppermute | solution.py:179
  6.2 53.5 %copy-start.4 = (f32[256,256]{1,0:T(8,128)}, f32[256,256]{1,0:T(8,128)S(1)}, u32[]{:S(2)}) copy-start(f32[256,256]{1,0:T(8,128)S(1)} %get-tuple-element.112.own_d) | copy-start | bytes 786436
  6.2 3.0 %collective-permute-start.2 = (f32[256,256]{1,0:T(8,128)S(1)}, f32[256,256]{1,0:T(8,128)S(1)}, u32[]{:S(2)}, u32[]{:S(2)}) collective-permute-start(f32[256,256]{1,0:T(8,128)S(1)} %get-tuple-element.218.own_d), channel_id=1, source_target_pairs={{0,4},{4,0},{8,12},{12,8},{16,20},{20,16},{24,28},{28,24},{1,5},{5... | collective-permute-start | bytes 786440 | tf_op jit(solution)/shard_map/ppermute | solution.py:179
  7.1 1.4 collective-permute-start.3
  10.8 15.7 %collective-permute-start.4 = (f32[3,256,256]{2,1,0:T(8,128)}, f32[3,256,256]{2,1,0:T(8,128)}, u32[]{:S(2)}, u32[]{:S(2)}) collective-permute-start(f32[3,256,256]{2,1,0:T(8,128)} %get-tuple-element.108.own_l), channel_id=1, source_target_pairs={{0,4},{4,0},{8,12},{12,8},{16,20},{20,16},{24,28},{28,24},{1,5},{5... | collective-permute-start | bytes 2359304 | tf_op jit(solution)/shard_map/ppermute | solution.py:179
  11.2 1.8 %collective-permute-start = (s32[4,3]{1,0:T(4,128)S(1)}, s32[4,3]{1,0:T(4,128)S(1)}, u32[]{:S(2)}, u32[]{:S(2)}) collective-permute-start(s32[4,3]{1,0:T(4,128)S(1)} %bitcast.84), channel_id=1, source_target_pairs={{0,4},{4,0},{8,12},{12,8},{16,20},{20,16},{24,28},{28,24},{1,5},{5... | collective-permute-start | bytes 152 | tf_op jit(solution)/shard_map/ppermute | solution.py:179
  13.0 13.4 %collective-permute-start.5 = (f32[256,256]{1,0:T(8,128)}, f32[256,256]{1,0:T(8,128)}, u32[]{:S(2)}, u32[]{:S(2)}) collective-permute-start(f32[256,256]{1,0:T(8,128)} %get-tuple-element.109.own_d), channel_id=1, source_target_pairs={{0,4},{4,0},{8,12},{12,8},{16,20},{20,16},{24,28},{28,24},{1,5},{5... | collective-permute-start | bytes 786440 | tf_op jit(solution)/shard_map/ppermute | solution.py:179
  13.4 13.0 %collective-permute-start.6 = (f32[256,128]{1,0:T(8,128)}, f32[256,128]{1,0:T(8,128)}, u32[]{:S(2)}, u32[]{:S(2)}) collective-permute-start(f32[256,128]{1,0:T(8,128)} %get-tuple-element.110.own_r), channel_id=1, source_target_pairs={{0,4},{4,0},{8,12},{12,8},{16,20},{20,16},{24,28},{28,24},{1,5},{5... | collective-permute-start | bytes 393224 | tf_op jit(solution)/shard_map/ppermute | solution.py:179
  22.6 7.3 %collective-permute-start.13 = (f32[64,512]{1,0:T(8,128)}, f32[64,512]{1,0:T(8,128)S(1)}, u32[]{:S(2)}, u32[]{:S(2)}) collective-permute-start(f32[64,512]{1,0:T(8,128)} %get-tuple-element.123), channel_id=1, source_target_pairs={{0,24},{4,28},{8,0},{12,4},{16,8},{20,12},{24,16},{28,20},{1,25},{... | collective-permute-start | bytes 393224 | tf_op jit(solution)/shard_map/ppermute | solution.py:183
  26.4 44.9 %collective-permute-start.7 = (f32[3,256,256]{2,1,0:T(8,128)}, f32[3,256,256]{2,1,0:T(8,128)}, u32[]{:S(2)}, u32[]{:S(2)}) collective-permute-start(f32[3,256,256]{2,1,0:T(8,128)} %get-tuple-element.111.own_l), channel_id=1, source_target_pairs={{0,4},{4,0},{8,12},{12,8},{16,20},{20,16},{24,28},{28,24},{1,5},{5... | collective-permute-start | bytes 2359304 | tf_op jit(solution)/shard_map/ppermute | solution.py:179
  29.4 10.7 %collective-permute-start.15 = (f32[64,512]{1,0:T(8,128)}, f32[64,512]{1,0:T(8,128)}, u32[]{:S(2)}, u32[]{:S(2)}) collective-permute-start(f32[64,512]{1,0:T(8,128)} %get-tuple-element.131), channel_id=1, source_target_pairs={{0,16},{4,20},{8,24},{12,28},{16,0},{20,4},{24,8},{28,12},{1,17},{... | collective-permute-start | bytes 393224 | tf_op jit(solution)/shard_map/ppermute | solution.py:183
  31.5 8.6 %collective-permute-start.16 = (f32[64,512]{1,0:T(8,128)}, f32[64,512]{1,0:T(8,128)}, u32[]{:S(2)}, u32[]{:S(2)}) collective-permute-start(f32[64,512]{1,0:T(8,128)} %get-tuple-element.132), channel_id=1, source_target_pairs={{0,24},{4,28},{8,0},{12,4},{16,8},{20,12},{24,16},{28,20},{1,25},{... | collective-permute-start | bytes 393224 | tf_op jit(solution)/shard_map/ppermute | solution.py:183
  39.6 9.1 %collective-permute-start.14 = (f32[64,512]{1,0:T(8,128)}, f32[64,512]{1,0:T(8,128)S(1)}, u32[]{:S(2)}, u32[]{:S(2)}) collective-permute-start(f32[64,512]{1,0:T(8,128)} %get-tuple-element.130), channel_id=1, source_target_pairs={{0,16},{4,20},{8,24},{12,28},{16,0},{20,4},{24,8},{28,12},{1,17},{... | collective-permute-start | bytes 393224 | tf_op jit(solution)/shard_map/ppermute | solution.py:183
  42.7 6.1 %collective-permute-start.17 = (f32[64,512]{1,0:T(8,128)}, f32[64,512]{1,0:T(8,128)}, u32[]{:S(2)}, u32[]{:S(2)}) collective-permute-start(f32[64,512]{1,0:T(8,128)} %get-tuple-element.133), channel_id=1, source_target_pairs={{0,24},{4,28},{8,0},{12,4},{16,8},{20,12},{24,16},{28,20},{1,25},{... | collective-permute-start | bytes 393224 | tf_op jit(solution)/shard_map/ppermute | solution.py:183
  47.9 14.6 %collective-permute-start.19 = (f32[64,512]{1,0:T(8,128)}, f32[64,512]{1,0:T(8,128)}, u32[]{:S(2)}, u32[]{:S(2)}) collective-permute-start(f32[64,512]{1,0:T(8,128)} %get-tuple-element.141), channel_id=1, source_target_pairs={{0,16},{4,20},{8,24},{12,28},{16,0},{20,4},{24,8},{28,12},{1,17},{... | collective-permute-start | bytes 393224 | tf_op jit(solution)/shard_map/ppermute | solution.py:183
  51.2 11.3 %collective-permute-start.20 = (f32[64,512]{1,0:T(8,128)}, f32[64,512]{1,0:T(8,128)S(1)}, u32[]{:S(2)}, u32[]{:S(2)}) collective-permute-start(f32[64,512]{1,0:T(8,128)} %get-tuple-element.142), channel_id=1, source_target_pairs={{0,24},{4,28},{8,0},{12,4},{16,8},{20,12},{24,16},{28,20},{1,25},{... | collective-permute-start | bytes 393224 | tf_op jit(solution)/shard_map/ppermute | solution.py:183
  58.2 7.4 %collective-permute-start.18 = (f32[64,512]{1,0:T(8,128)S(1)}, f32[64,512]{1,0:T(8,128)S(1)}, u32[]{:S(2)}, u32[]{:S(2)}) collective-permute-start(f32[64,512]{1,0:T(8,128)S(1)} %get-tuple-element.140), channel_id=1, source_target_pairs={{0,16},{4,20},{8,24},{12,28},{16,0},{20,4},{24,8},{28,12},{1,17},{... | collective-permute-start | bytes 393224 | tf_op jit(solution)/shard_map/ppermute | solution.py:183
  59.7 11.6 %collective-permute-start.8 = (f32[256,256]{1,0:T(8,128)S(1)}, f32[256,256]{1,0:T(8,128)S(1)}, u32[]{:S(2)}, u32[]{:S(2)}) collective-permute-start(f32[256,256]{1,0:T(8,128)S(1)} %get-tuple-element.112.own_d), channel_id=1, source_target_pairs={{0,4},{4,0},{8,12},{12,8},{16,20},{20,16},{24,28},{28,24},{1,5},{5... | collective-permute-start | bytes 786440 | tf_op jit(solution)/shard_map/ppermute | solution.py:179
  63.7 6.0 %collective-permute-start.21 = (f32[64,512]{1,0:T(8,128)S(1)}, f32[64,512]{1,0:T(8,128)S(1)}, u32[]{:S(2)}, u32[]{:S(2)}) collective-permute-start(f32[64,512]{1,0:T(8,128)S(1)} %get-tuple-element.145), channel_id=1, source_target_pairs={{0,24},{4,28},{8,0},{12,4},{16,8},{20,12},{24,16},{28,20},{1,25},{... | collective-permute-start | bytes 393224 | tf_op jit(solution)/shard_map/ppermute | solution.py:183
  63.8 7.5 %collective-permute-start.9 = (f32[256,128]{1,0:T(8,128)S(1)}, f32[256,128]{1,0:T(8,128)S(1)}, u32[]{:S(2)}, u32[]{:S(2)}) collective-permute-start(f32[256,128]{1,0:T(8,128)S(1)} %copy-done.9), channel_id=1, source_target_pairs={{0,4},{4,0},{8,12},{12,8},{16,20},{20,16},{24,28},{28,24},{1,5},{5... | collective-permute-start | bytes 393224 | tf_op jit(solution)/shard_map/ppermute | solution.py:179
  65.6 8.0 %collective-permute-start.23 = (f32[64,512]{1,0:T(8,128)S(1)}, f32[64,512]{1,0:T(8,128)S(1)}, u32[]{:S(2)}, u32[]{:S(2)}) collective-permute-start(f32[64,512]{1,0:T(8,128)S(1)} %get-tuple-element.153), channel_id=1, source_target_pairs={{0,16},{4,20},{8,24},{12,28},{16,0},{20,4},{24,8},{28,12},{1,17},{... | collective-permute-start | bytes 393224 | tf_op jit(solution)/shard_map/ppermute | solution.py:183
  70.0 5.2 %collective-permute-start.24 = (f32[64,512]{1,0:T(8,128)S(1)}, f32[64,512]{1,0:T(8,128)S(1)}, u32[]{:S(2)}, u32[]{:S(2)}) collective-permute-start(f32[64,512]{1,0:T(8,128)S(1)} %get-tuple-element.154), channel_id=1, source_target_pairs={{0,24},{4,28},{8,0},{12,4},{16,8},{20,12},{24,16},{28,20},{1,25},{... | collective-permute-start | bytes 393224 | tf_op jit(solution)/shard_map/ppermute | solution.py:183
  71.3 51.9 %collective-permute-start.10 = (f32[3,256,256]{2,1,0:T(8,128)S(1)}, f32[3,256,256]{2,1,0:T(8,128)}, u32[]{:S(2)}, u32[]{:S(2)}) collective-permute-start(f32[3,256,256]{2,1,0:T(8,128)S(1)} %copy-done), channel_id=1, source_target_pairs={{0,4},{4,0},{8,12},{12,8},{16,20},{20,16},{24,28},{28,24},{1,5},{5... | collective-permute-start | bytes 2359304 | tf_op jit(solution)/shard_map/ppermute | solution.py:179
  72.7 19.0 %copy-start.1 = (f32[3,256,256]{2,1,0:T(8,128)S(1)}, f32[3,256,256]{2,1,0:T(8,128)}, u32[]{:S(2)}) copy-start(f32[3,256,256]{2,1,0:T(8,128)} %get-tuple-element.111.own_l) | copy-start | bytes 2359300
  72.7 7.8 %collective-permute-start.22 = (f32[64,512]{1,0:T(8,128)S(1)}, f32[64,512]{1,0:T(8,128)S(1)}, u32[]{:S(2)}, u32[]{:S(2)}) collective-permute-start(f32[64,512]{1,0:T(8,128)S(1)} %get-tuple-element.152), channel_id=1, source_target_pairs={{0,16},{4,20},{8,24},{12,28},{16,0},{20,4},{24,8},{28,12},{1,17},{... | collective-permute-start | bytes 393224 | tf_op jit(solution)/shard_map/ppermute | solution.py:183
  75.5 5.0 %collective-permute-start.25 = (f32[64,512]{1,0:T(8,128)S(1)}, f32[64,512]{1,0:T(8,128)S(1)}, u32[]{:S(2)}, u32[]{:S(2)}) collective-permute-start(f32[64,512]{1,0:T(8,128)S(1)} %get-tuple-element.155), channel_id=1, source_target_pairs={{0,24},{4,28},{8,0},{12,4},{16,8},{20,12},{24,16},{28,20},{1,25},{... | collective-permute-start | bytes 393224 | tf_op jit(solution)/shard_map/ppermute | solution.py:183
  79.8 18.5 %collective-permute-start.27 = (f32[64,512]{1,0:T(8,128)}, f32[64,512]{1,0:T(8,128)}, u32[]{:S(2)}, u32[]{:S(2)}) collective-permute-start(f32[64,512]{1,0:T(8,128)} %get-tuple-element.163), channel_id=1, source_target_pairs={{0,16},{4,20},{8,24},{12,28},{16,0},{20,4},{24,8},{28,12},{1,17},{... | collective-permute-start | bytes 393224 | tf_op jit(solution)/shard_map/ppermute | solution.py:183
  82.1 16.2 %collective-permute-start.28 = (f32[64,512]{1,0:T(8,128)}, f32[64,512]{1,0:T(8,128)}, u32[]{:S(2)}, u32[]{:S(2)}) collective-permute-start(f32[64,512]{1,0:T(8,128)} %get-tuple-element.164), channel_id=1, source_target_pairs={{0,24},{4,28},{8,0},{12,4},{16,8},{20,12},{24,16},{28,20},{1,25},{... | collective-permute-start | bytes 393224 | tf_op jit(solution)/shard_map/ppermute | solution.py:183
  90.9 11.3 %collective-permute-start.26 = (f32[64,512]{1,0:T(8,128)S(1)}, f32[64,512]{1,0:T(8,128)S(1)}, u32[]{:S(2)}, u32[]{:S(2)}) collective-permute-start(f32[64,512]{1,0:T(8,128)S(1)} %get-tuple-element.162), channel_id=1, source_target_pairs={{0,16},{4,20},{8,24},{12,28},{16,0},{20,4},{24,8},{28,12},{1,17},{... | collective-permute-start | bytes 393224 | tf_op jit(solution)/shard_map/ppermute | solution.py:183
  99.6 6.1 %collective-permute-start.29 = (f32[64,512]{1,0:T(8,128)S(1)}, f32[64,512]{1,0:T(8,128)S(1)}, u32[]{:S(2)}, u32[]{:S(2)}) collective-permute-start(f32[64,512]{1,0:T(8,128)S(1)} %get-tuple-element.167), channel_id=1, source_target_pairs={{0,24},{4,28},{8,0},{12,4},{16,8},{20,12},{24,16},{28,20},{1,25},{... | collective-permute-start | bytes 393224 | tf_op jit(solution)/shard_map/ppermute | solution.py:183
  100.9 7.9 %collective-permute-start.31 = (f32[64,512]{1,0:T(8,128)S(1)}, f32[64,512]{1,0:T(8,128)S(1)}, u32[]{:S(2)}, u32[]{:S(2)}) collective-permute-start(f32[64,512]{1,0:T(8,128)S(1)} %get-tuple-element.175), channel_id=1, source_target_pairs={{0,16},{4,20},{8,24},{12,28},{16,0},{20,4},{24,8},{28,12},{1,17},{... | collective-permute-start | bytes 393224 | tf_op jit(solution)/shard_map/ppermute | solution.py:183
  106.0 5.0 %collective-permute-start.32 = (f32[64,512]{1,0:T(8,128)S(1)}, f32[64,512]{1,0:T(8,128)S(1)}, u32[]{:S(2)}, u32[]{:S(2)}) collective-permute-start(f32[64,512]{1,0:T(8,128)S(1)} %get-tuple-element.176), channel_id=1, source_target_pairs={{0,24},{4,28},{8,0},{12,4},{16,8},{20,12},{24,16},{28,20},{1,25},{... | collective-permute-start | bytes 393224 | tf_op jit(solution)/shard_map/ppermute | solution.py:183
  106.3 16.9 %collective-permute-start.11 = (f32[256,256]{1,0:T(8,128)S(1)}, f32[256,256]{1,0:T(8,128)}, u32[]{:S(2)}, u32[]{:S(2)}) collective-permute-start(f32[256,256]{1,0:T(8,128)S(1)} %get-tuple-element.115.own_d), channel_id=1, source_target_pairs={{0,4},{4,0},{8,12},{12,8},{16,20},{20,16},{24,28},{28,24},{1,5},{5... | collective-permute-start | bytes 786440 | tf_op jit(solution)/shard_map/ppermute | solution.py:179
  106.3 13.4 %copy-start.55 = (s32[3]{0:T(128)S(1)}, s32[3]{0:T(128)}, u32[]{:S(2)}) copy-start(s32[3]{0:T(128)} %get-tuple-element.240) | copy-start | bytes 40
  107.6 7.0 %collective-permute-start.30 = (f32[64,512]{1,0:T(8,128)S(1)}, f32[64,512]{1,0:T(8,128)S(1)}, u32[]{:S(2)}, u32[]{:S(2)}) collective-permute-start(f32[64,512]{1,0:T(8,128)S(1)} %get-tuple-element.174), channel_id=1, source_target_pairs={{0,16},{4,20},{8,24},{12,28},{16,0},{20,4},{24,8},{28,12},{1,17},{... | collective-permute-start | bytes 393224 | tf_op jit(solution)/shard_map/ppermute | solution.py:183
  111.3 5.2 %collective-permute-start.33 = (f32[64,512]{1,0:T(8,128)S(1)}, f32[64,512]{1,0:T(8,128)S(1)}, u32[]{:S(2)}, u32[]{:S(2)}) collective-permute-start(f32[64,512]{1,0:T(8,128)S(1)} %get-tuple-element.177), channel_id=1, source_target_pairs={{0,24},{4,28},{8,0},{12,4},{16,8},{20,12},{24,16},{28,20},{1,25},{... | collective-permute-start | bytes 393224 | tf_op jit(solution)/shard_map/ppermute | solution.py:183
  112.7 8.4 %collective-permute-start.12 = (f32[256,128]{1,0:T(8,128)S(1)}, f32[256,128]{1,0:T(8,128)}, u32[]{:S(2)}, u32[]{:S(2)}) collective-permute-start(f32[256,128]{1,0:T(8,128)S(1)} %copy-done.8), channel_id=1, source_target_pairs={{0,4},{4,0},{8,12},{12,8},{16,20},{20,16},{24,28},{28,24},{1,5},{5... | collective-permute-start | bytes 393224 | tf_op jit(solution)/shard_map/ppermute | solution.py:179
  114.6 11.0 %collective-permute-start.35 = (f32[64,512]{1,0:T(8,128)}, f32[64,512]{1,0:T(8,128)S(1)}, u32[]{:S(2)}, u32[]{:S(2)}) collective-permute-start(f32[64,512]{1,0:T(8,128)} %get-tuple-element.185), channel_id=1, source_target_pairs={{0,16},{4,20},{8,24},{12,28},{16,0},{20,4},{24,8},{28,12},{1,17},{... | collective-permute-start | bytes 393224 | tf_op jit(solution)/shard_map/ppermute | solution.py:183
  117.4 8.2 %collective-permute-start.36 = (f32[64,512]{1,0:T(8,128)}, f32[64,512]{1,0:T(8,128)S(1)}, u32[]{:S(2)}, u32[]{:S(2)}) collective-permute-start(f32[64,512]{1,0:T(8,128)} %get-tuple-element.186), channel_id=1, source_target_pairs={{0,24},{4,28},{8,0},{12,4},{16,8},{20,12},{24,16},{28,20},{1,25},{... | collective-permute-start | bytes 393224 | tf_op jit(solution)/shard_map/ppermute | solution.py:183
  121.1 8.5 %collective-permute-start.34 = (f32[64,512]{1,0:T(8,128)S(1)}, f32[64,512]{1,0:T(8,128)S(1)}, u32[]{:S(2)}, u32[]{:S(2)}) collective-permute-start(f32[64,512]{1,0:T(8,128)S(1)} %get-tuple-element.184), channel_id=1, source_target_pairs={{0,16},{4,20},{8,24},{12,28},{16,0},{20,4},{24,8},{28,12},{1,17},{... | collective-permute-start | bytes 393224 | tf_op jit(solution)/shard_map/ppermute | solution.py:183
  126.0 5.8 %collective-permute-start.37 = (f32[64,512]{1,0:T(8,128)S(1)}, f32[64,512]{1,0:T(8,128)S(1)}, u32[]{:S(2)}, u32[]{:S(2)}) collective-permute-start(f32[64,512]{1,0:T(8,128)S(1)} %get-tuple-element.189), channel_id=1, source_target_pairs={{0,24},{4,28},{8,0},{12,4},{16,8},{20,12},{24,16},{28,20},{1,25},{... | collective-permute-start | bytes 393224 | tf_op jit(solution)/shard_map/ppermute | solution.py:183
  129.0 7.5 %collective-permute-start.39 = (f32[64,512]{1,0:T(8,128)S(1)}, f32[64,512]{1,0:T(8,128)S(1)}, u32[]{:S(2)}, u32[]{:S(2)}) collective-permute-start(f32[64,512]{1,0:T(8,128)S(1)} %get-tuple-element.197), channel_id=1, source_target_pairs={{0,16},{4,20},{8,24},{12,28},{16,0},{20,4},{24,8},{28,12},{1,17},{... | collective-permute-start | bytes 393224 | tf_op jit(solution)/shard_map/ppermute | solution.py:183
  132.0 6.2 %collective-permute-start.40 = (f32[64,512]{1,0:T(8,128)S(1)}, f32[64,512]{1,0:T(8,128)S(1)}, u32[]{:S(2)}, u32[]{:S(2)}) collective-permute-start(f32[64,512]{1,0:T(8,128)S(1)} %get-tuple-element.198), channel_id=1, source_target_pairs={{0,24},{4,28},{8,0},{12,4},{16,8},{20,12},{24,16},{28,20},{1,25},{... | collective-permute-start | bytes 393224 | tf_op jit(solution)/shard_map/ppermute | solution.py:183
  136.4 7.6 %collective-permute-start.38 = (f32[64,512]{1,0:T(8,128)S(1)}, f32[64,512]{1,0:T(8,128)S(1)}, u32[]{:S(2)}, u32[]{:S(2)}) collective-permute-start(f32[64,512]{1,0:T(8,128)S(1)} %get-tuple-element.196), channel_id=1, source_target_pairs={{0,16},{4,20},{8,24},{12,28},{16,0},{20,4},{24,8},{28,12},{1,17},{... | collective-permute-start | bytes 393224 | tf_op jit(solution)/shard_map/ppermute | solution.py:183
  138.6 6.1 %collective-permute-start.41 = (f32[64,512]{1,0:T(8,128)S(1)}, f32[64,512]{1,0:T(8,128)S(1)}, u32[]{:S(2)}, u32[]{:S(2)}) collective-permute-start(f32[64,512]{1,0:T(8,128)S(1)} %get-tuple-element.199), channel_id=1, source_target_pairs={{0,24},{4,28},{8,0},{12,4},{16,8},{20,12},{24,16},{28,20},{1,25},{... | collective-permute-start | bytes 393224 | tf_op jit(solution)/shard_map/ppermute | solution.py:183
  147.6 13.2 %collective-permute-start.42 = (f32[4,64,256]{2,1,0:T(8,128)S(1)}, f32[4,64,256]{2,1,0:T(8,128)S(1)}, u32[]{:S(2)}, u32[]{:S(2)}) collective-permute-start(f32[4,64,256]{2,1,0:T(8,128)S(1)} %pad_maximum_fusion), channel_id=1, source_target_pairs={{0,4},{4,0},{8,12},{12,8},{16,20},{20,16},{24,28},{28,24},{1,5},{5... | collective-permute-start | bytes 786440 | tf_op jit(solution)/shard_map/ppermute | solution.py:179
  147.7 1.5 collective-permute-start.43
  148.1 1.2 collective-permute-start.44
  (54 other events, 181.0 us)

commit v2 on v0

v2 whole, which is shorter than its diff:
```python
import functools

import jax
import jax.numpy as jnp
from jax import lax
from jax.experimental import pallas as pl
from jax.experimental.pallas import tpu as pltpu
from jax.sharding import PartitionSpec as P

NDIST = 256
F32 = jnp.float32
B16 = jnp.bfloat16
SMEM_SPEC = pl.BlockSpec(memory_space=pltpu.SMEM)
VMEM_SPEC = pl.BlockSpec(memory_space=pltpu.VMEM)
HBM_SPEC = pl.BlockSpec(memory_space=pltpu.HBM)


def params(mib):
    return pltpu.CompilerParams(vmem_limit_bytes=mib * 1024 * 1024)


def cost(flops, moved):
    return pl.CostEstimate(flops=flops, bytes_accessed=moved, transcendentals=0)


def shaped(*shape, dtype=F32):
    return jax.ShapeDtypeStruct(shape, dtype)


def halves(x):
    hi = x.astype(B16)
    lo = (x - hi.astype(F32)).astype(B16)
    return hi, lo


def dot(a, b):
    return jnp.dot(a, b, preferred_element_type=F32)


def dot3(x, y):
    rows = x[0].shape[0]
    both = dot(jnp.concatenate([x[0], x[1]], axis=0), y[0])
    return both[:rows] + both[rows:] + dot(x[0], y[1])


def packed_places(slots, bs, columns):
    rhs_at = (slots + 1) * bs
    col_at = rhs_at + columns
    turnout_at = col_at + 8 * slots
    district_at = turnout_at + 8
    return rhs_at, col_at, turnout_at, district_at, district_at + 8


def chip_now():
    return lax.div(lax.axis_index("blk").astype(jnp.int32), 2)


def upper_here():
    return lax.rem(lax.axis_index("blk").astype(jnp.int32), 2) == 1


def pack_kernel(rows, cols, turnout, district, l_ref, d_ref, r_ref, *refs):
    outs = refs[: len(rows)]
    held, sems = refs[len(rows) :]
    slots, bs = l_ref.shape[2], l_ref.shape[3]
    columns = r_ref.shape[3]
    rhs_at, col_at, turnout_at, district_at, _ = packed_places(slots, bs, columns)
    copies = []

    def copy(source, target):
        copies.append(pltpu.make_async_copy(source, target, sems.at[len(copies)]))
        copies[-1].start()

    for i, r in enumerate(rows):
        copy(r_ref.at[r, 0], held.at[i])
    for out, r in zip(outs, rows):
        for k in range(slots):
            copy(l_ref.at[r, 0, k], out.at[pl.ds(k * bs, bs)])
        copy(d_ref.at[r, 0], out.at[pl.ds(slots * bs, bs)])
    for out, r in zip(outs, rows):
        for k in range(slots):
            at = col_at + 8 * k
            out[at : at + 8] = jnp.full((8, bs), cols[k, 0, r].astype(F32))
        out[turnout_at : turnout_at + 8] = jnp.broadcast_to(turnout[r], (8, bs))
        out[district_at : district_at + 8] = jnp.broadcast_to(
            district[r].astype(F32), (8, bs)
        )
    for i, out in enumerate(outs):
        copies[i].wait()
        out[rhs_at:col_at] = held[i].T
    for started in copies[len(rows) :]:
        started.wait()


def put(high, low, i, j, value):
    bs = value.shape[0]
    hi, lo = halves(value)
    high[i * bs : (i + 1) * bs, j * bs : (j + 1) * bs] = hi
    low[i * bs : (i + 1) * bs, j * bs : (j + 1) * bs] = lo


def blocks_of(r, n, slots, columns, own, oth):
    is_a = upper_here()
    bs = own.shape[1]
    _, col_at, _, _, _ = packed_places(slots, bs, columns)
    row_b = r * n + 2 * chip_now()
    row_a = row_b + 1

    def upper(at, size):
        return jnp.where(is_a, own[at : at + size], oth[at : at + size])

    def lower(at, size):
        return jnp.where(is_a, oth[at : at + size], own[at : at + size])

    def at_distance(side, row, d):
        found = jnp.zeros((bs, bs), F32)
        column = (row - d).astype(F32)
        for k in range(1, slots):
            col = side(col_at + 8 * k, 1)
            here = (col == column) & (col >= 0.0)
            found = jnp.where(here, side(k * bs, bs), found)
        return halves(found)

    return upper, lower, lambda d: at_distance(upper, row_a, d), lambda d: at_distance(lower, row_b, d)


def near_setup_kernel(r, n, slots, columns, own, oth, gh, gl, mh, ml, rt):
    bs = own.shape[1]
    half = columns // 2
    rhs_at, col_at, _, _, _ = packed_places(slots, bs, columns)
    upper, lower, upper_at, lower_at = blocks_of(r, n, slots, columns, own, oth)
    is_a = upper_here()
    da, db = halves(upper(slots * bs, bs)), halves(lower(slots * bs, bs))
    la1 = halves(upper(0, bs))
    lb1 = halves(jnp.where(lower(col_at, 1) >= 0.0, lower(0, bs), 0.0))
    w = dot3(da, la1)
    wh = halves(w)
    for place, pair in enumerate((da, db, la1, wh)):
        mh[place] = pair[0]
        ml[place] = pair[1]
    for j, (la, lb) in enumerate(((upper_at(2), lb1), (upper_at(3), lower_at(2)))):
        from_b = dot3(db, lb)
        put(gh, gl, 1, j, from_b)
        put(gh, gl, 0, j, dot3(da, la) - dot3(wh, halves(from_b)))
    ra, rb = upper(rhs_at, columns), lower(rhs_at, columns)
    rt[:, :bs] = jnp.where(is_a, ra[half:], ra[:half])
    rt[:, bs:] = jnp.where(is_a, rb[half:], rb[:half])


def far_setup_kernel(r, n, slots, columns, own, oth, mh, ml, fh, fl):
    _, _, upper_at, lower_at = blocks_of(r, n, slots, columns, own, oth)
    da, db, w = ((mh[k], ml[k]) for k in (0, 1, 3))
    for j, lb in enumerate((lower_at(3), lower_at(4))):
        from_b = dot3(db, lb)
        put(fh, fl, 1, j, from_b)
        from_a = -dot3(w, halves(from_b))
        if j == 0:
            from_a = from_a + dot3(da, upper_at(4))
        put(fh, fl, 0, j, from_a)


def place_of(lead, pairs, pieces):
    ahead = lax.rem(chip_now() - lead % pairs + pairs, pairs)
    piece = jnp.minimum(lax.div(ahead, 2), pieces - 1)
    return piece, lead + ahead


def choose(choices, pair, split, run):
    if len(choices) == 1:
        run(*choices[0])
        return

    @pl.when(pair < split)
    def _():
        run(*choices[0])

    @pl.when(pair >= split)
    def _():
        run(*choices[1])


def near_kernel(lead, pairs, pieces, split, received, has_near, *refs):
    taken = refs[:received]
    outs = refs[-2:] if has_near else refs[-1:]
    refs = refs[received : -len(outs)]
    each = 3 if has_near else 1
    choices = [refs[i : i + each] for i in range(0, len(refs), each)]
    v_out = outs[0]
    width = v_out.shape[0]
    piece, pair = place_of(lead, pairs, pieces)
    rows = pl.ds(pl.multiple_of(piece * width, width), width)

    def run(rt, gh=None, gl=None):
        v = rt[rows, :]
        for x in taken:
            v = v - x[...]
        v_out[...] = v
        if has_near:
            outs[1][...] = dot3(halves(v), (gh[...], gl[...]))

    choose(choices, pair, split, run)


def far_kernel(lead, pairs, pieces, split, v_ref, *refs):
    out = refs[-1]
    refs = refs[:-1]
    _, pair = place_of(lead, pairs, pieces)

    def run(fh, fl):
        out[...] = dot3(halves(v_ref[...]), (fh[...], fl[...]))

    choose([refs[i : i + 2] for i in range(0, len(refs), 2)], pair, split, run)


def finish_kernel(slots, pairs, pieces, window, has_total, is_last, *refs):
    values = refs[:window]
    mh, ml, own, oth = refs[window : window + 4]
    refs = refs[window + 4 :]
    start = refs[0][...] if has_total else None
    keep, give, *outs = refs[1:] if has_total else refs
    chip, is_a = chip_now(), upper_here()
    bs = mh.shape[1]
    half = keep.shape[0]
    _, _, turnout_at, district_at, _ = packed_places(slots, bs, 2 * half)
    parts = []
    for m in range(pieces):
        v = values[pairs - 1 + 2 * m][...]
        for q in range(1, pairs):
            v = jnp.where(chip == q, values[pairs - 1 - q + 2 * m][...], v)
        parts.append(v)
    v = jnp.concatenate(parts, axis=0)

    def m(k):
        return mh[k], ml[k]

    xa = dot3(halves(v[:, :bs]), m(0))
    xb = dot3(halves(v[:, bs:] - dot3(halves(xa), m(2))), m(1))
    kept, given = jnp.where(is_a, xa, xb), jnp.where(is_a, xb, xa)
    keep[...] = kept
    give[...] = given
    names = lax.broadcasted_iota(jnp.int32, (NDIST, bs), 0).astype(F32)
    sums = jnp.zeros((NDIST, 2 * half), F32) if start is None else start
    for x, pack in ((kept, own), (given, oth)):
        weight = pack[turnout_at : turnout_at + 1]
        member = names == pack[district_at : district_at + 1]
        member = member.astype(F32).astype(B16)
        terms = jnp.concatenate([x * weight, jnp.broadcast_to(weight, (half, bs))], axis=0)
        for part in halves(terms):
            sums = sums + lax.dot_general(
                member, part, (((1,), (1,)), ((), ())), preferred_element_type=F32
            )
    if not is_last:
        outs[0][...] = sums
        return
    held = outs.pop()
    held[...] = sums
    rows = NDIST // pairs
    for by, part in enumerate(outs):
        to = lax.rem(chip + by, pairs)
        part[...] = held[pl.ds(pl.multiple_of(to * rows, rows), rows), :]


def add_kernel(*refs):
    mine, theirs = refs[-2:]
    total = refs[0][...]
    for part in refs[1:-2]:
        total = total + part[...]
    rows = mine.shape[0]
    is_a = upper_here()
    mine[...] = jnp.where(is_a, total[rows:], total[:rows])
    theirs[...] = jnp.where(is_a, total[:rows], total[rows:])


def mean_kernel(mine, got, out):
    half = out.shape[1] // 2
    own, oth = (x[:, :half] / x[:, half:] for x in (mine, got))
    is_a = upper_here()
    out[...] = jnp.concatenate(
        [jnp.where(is_a, oth, own), jnp.where(is_a, own, oth)], axis=1
    )


def field_kernel(rows_here, *refs):
    keeps = refs[:rows_here]
    gots = refs[rows_here : 2 * rows_here]
    out = refs[2 * rows_here]
    is_a = upper_here()
    for r in range(rows_here):
        top = jnp.where(is_a, gots[r][...], keeps[r][...])
        bottom = jnp.where(is_a, keeps[r][...], gots[r][...])
        out[r, 0] = jnp.concatenate([top, bottom], axis=0).T


def body(rhs, lower_blocks, col_index, diag_inverse, turnout, district_of):
    n = lax.axis_size("blk")
    pairs = n // 2
    pieces = max(pairs // 2, 1)
    rows_here, _, bs, columns = rhs.shape
    slots = lower_blocks.shape[2]
    half = columns // 2
    width = half // pieces
    count = rows_here * pairs
    packed_rows = packed_places(slots, bs, columns)[-1]
    wide = shaped(width, 2 * bs)
    square = shaped(2 * bs, 2 * bs, dtype=B16)

    def call(kernel, name, outs, operands, mib, flops=0, moved=0, **more):
        several = isinstance(outs, tuple)
        return pl.pallas_call(
            kernel,
            out_shape=outs,
            in_specs=more.pop("in_specs", [VMEM_SPEC] * len(operands)),
            out_specs=(VMEM_SPEC,) * len(outs) if several else VMEM_SPEC,
            compiler_params=params(mib),
            cost_estimate=cost(flops, moved),
            name=name,
            **more,
        )(*operands)

    def swap(x):
        return lax.ppermute(x, "blk", [(i, i ^ 1) for i in range(n)])

    def shift(x, by):
        return lax.ppermute(x, "blk", [(i, (i + 2 * by) % n) for i in range(n)])

    def pass_on(x, lead, by):
        perm = []
        for k in range(lead, lead + 2 * pieces, 2):
            if by <= k < count:
                sender, target = k % pairs, (k - by) % pairs
                perm += [(2 * sender + c, 2 * target + c) for c in range(2)]
        return lax.ppermute(x, "blk", perm)

    def pack(rows):
        return call(
            functools.partial(pack_kernel, rows),
            "pack",
            (shaped(packed_rows, bs),) * len(rows),
            (jnp.transpose(col_index, (2, 1, 0)), turnout, district_of, lower_blocks, diag_inverse, rhs),
            56,
            moved=8 * packed_rows * bs * len(rows),
            in_specs=[SMEM_SPEC, VMEM_SPEC, VMEM_SPEC] + [HBM_SPEC] * 3,
            scratch_shapes=[
                pltpu.VMEM((len(rows), bs, columns), F32),
                pltpu.SemaphoreType.DMA((len(rows) * (slots + 2),)),
            ],
        )

    def setup(r):
        args = (r, n, slots, columns)
        held = shaped(4, bs, bs, dtype=B16)
        gh, gl, mh, ml, rt = call(
            functools.partial(near_setup_kernel, *args),
            "near_setup",
            (square, square, held, held, shaped(half, 2 * bs)),
            packs[r],
            10,
            14 * 3 * bs**3,
            24 * bs * bs * 4,
        )
        fh, fl = call(
            functools.partial(far_setup_kernel, *args),
            "far_setup",
            (square, square),
            (*packs[r], mh, ml),
            10,
            10 * 3 * bs**3,
            24 * bs * bs * 4,
        )
        return gh, gl, mh, ml, rt, fh, fl

    def finish(r, values, total):
        first = count - 1 - (r * pairs + pairs - 1)
        window = values[first : first + pairs + 2 * (pieces - 1)]
        is_last = r == 0
        outs = (shaped(half, bs), shaped(half, bs))
        outs += (shaped(NDIST // pairs, columns),) * pairs if is_last else (shaped(NDIST, columns),)
        extra = () if total is None else (total,)
        return call(
            functools.partial(
                finish_kernel, slots, pairs, pieces, len(window), total is not None, is_last
            ),
            "finish",
            outs,
            (*window, *fixed[r][2:4], *packs[r], *extra),
            8,
            6 * 3 * half * bs * bs,
            16 * bs * bs,
            scratch_shapes=[pltpu.VMEM((NDIST, columns), F32)] if is_last else [],
        )

    top = rows_here - 1
    packs, fixed = {}, {}
    (own,) = pack((top,))
    packs[top] = (own, swap(own))
    packed = pack(tuple(range(top))) if top else ()
    fixed[top] = setup(top)

    keeps, gots = {}, {}
    values = []
    total = near = far_now = far_next = None
    steps = count + 2 * (pieces - 1)
    for step in range(steps):
        lead = count - 1 - step
        low = max(lead, 0) // pairs
        high = min(lead + 2 * (pieces - 1), count - 1) // pairs
        rows = range(low, high + 1)
        taken = [x for x in (far_now, near) if x is not None]
        has_near = step + 1 < steps
        has_far = step + 2 < steps
        operands = []
        for r in rows:
            gh, gl, _, _, rt, _, _ = fixed[r]
            operands += [rt, gh, gl] if has_near else [rt]
        place = (lead, pairs, pieces, high * pairs)
        v, *near_out = call(
            functools.partial(near_kernel, *place, len(taken), has_near),
            "near_terms",
            (wide, wide) if has_near else (wide,),
            (*taken, *operands),
            4,
            6 * width * 4 * bs * bs,
            6 * width * bs * 4,
        )
        values.append(v)
        near = pass_on(near_out[0], lead, 1) if has_near else None
        if has_near and (lead + 1) % pairs == 0 and 0 < lead // pairs:
            r = lead // pairs - 1
            own, _ = lax.optimization_barrier((packed[r], near_out[0]))
            packs[r] = (own, swap(own))
            fixed[r] = setup(r)
        far_now, far_next = far_next, None
        if has_far:
            operands = [x for r in rows for x in fixed[r][5:]]
            far_out = call(
                functools.partial(far_kernel, *place),
                "far_terms",
                wide,
                (v, *operands),
                4,
                6 * width * 4 * bs * bs,
                6 * width * bs * 4,
            )
            far_next = pass_on(far_out, lead, 2)
        done = lead + 2 * (pieces - 1)
        if done % pairs == 0 and 0 < done // pairs <= top:
            r = done // pairs
            keeps[r], give, total = finish(r, values, total)
            gots[r] = swap(give)
            near, total = lax.optimization_barrier((near, total))

    keeps[0], give, *parts = finish(0, values, total)
    gots[0] = swap(give)
    parts = [parts[0]] + [shift(parts[by], by) for by in range(1, pairs)]
    order = range(rows_here)
    field = call(
        functools.partial(field_kernel, rows_here),
        "field",
        shaped(rows_here, 1, bs, columns),
        (*[keeps[r] for r in order], *[gots[r] for r in order]),
        4,
        0,
        8 * rows_here * bs * columns,
    )
    parts, field = lax.optimization_barrier((parts, field))
    held = shaped(NDIST // n, columns)
    mine, theirs = call(add_kernel, "district_add", (held, held), tuple(parts), 4)
    mean = call(mean_kernel, "district_mean", held, (mine, swap(theirs)), 4)
    return field, mean


def solution(mesh):
    placed = (
        P(None, "blk", None, "sims"),
        P(None, "blk", None, None, None),
        P(None, "blk", None),
        P(None, "blk", None, None),
        P(None, "blk", None),
        P(None, "blk", None),
    )
    return jax.shard_map(
        body,
        mesh=mesh,
        in_specs=placed,
        out_specs=(P(None, "blk", None, "sims"), P("blk", "sims")),
        check_vma=False,
    )
```

time: 536 us -> 136 us (0.25)
  waiting for transfers between devices: 233 us -> 43.7 us
  matrix products: 158 us -> 0 us
  starting transfers between devices: 92 us -> 56.7 us
  Pallas kernels: 0 us -> 31.5 us
  blocking collectives: 14.6 us -> 0 us
  between operations: 14.8 us -> 1.27 us
  other arithmetic: 11.6 us -> 0 us
    ppermute x32 -> x45, waiting for transfers between devices: 214 us -> 43.7 us  [the longest x33 41.1 us: pass_on(): return lax.ppermute(x, 'blk', perm)]
    dot_general x98 -> x0, matrix products: 158 us -> none  [the longest x32 81.2 us: advance(): updates = jnp.einsum('kab,as->kbs', blocks_now, solved, precision=precise)]
    ppermute x32 -> x45, starting transfers between devices: 92 us -> 56.7 us  [the longest x33 52.2 us: pass_on(): return lax.ppermute(x, 'blk', perm)]
    pallas_call x0 -> x51, Pallas kernels: none -> 31.5 us  [call(): pl.pallas_call(kernel, out_shape=outs, in_specs=more.pop('in_specs', [VME...]
    reduce_scatter x1 -> x0, waiting for transfers between devices: 18.8 us -> none  [body(): lax.psum_scatter(numerator, 'blk', scatter_dimension=0, tiled=True)]
    unnamed x1 -> x0, blocking collectives: 14.6 us -> none
    sub x64 -> x0, other arithmetic: 5.93 us -> none  [the longest x32 5.54 us: advance(): source - pending[0]]
  transfers between devices with their start and end apart: 33 -> 45, of which waited for: 33 -> 18; matrix products, arithmetic and copies ran while one was open for 0% -> 0% of each run, Pallas kernels for 0% -> 19%
where the time goes in v2:
time: 136 us; the launch traced here: 135 us
  starting transfers between devices  56.7 us (42%)
  waiting for transfers between devices  43.7 us (32%)
  Pallas kernels  31.5 us (23%)
  local copies, waits for them, and re-layouts  2.03 us (1%)
    ppermute x33, starting transfers between devices, pass_on(): return lax.ppermute(x, 'blk', perm)  52.2 us
    ppermute x33, waiting for transfers between devices, pass_on(): return lax.ppermute(x, 'blk', perm)  41.1 us
    pallas_call x51, Pallas kernels, call(): pl.pallas_call(kernel, out_shape=outs, in_specs=more.pop('in_specs', [VME...  31.5 us
    ppermute x3, starting transfers between devices, shift(): return lax.ppermute(x, 'blk', [(i, (i + 2 * by) % n) for i in range(n)])  3 us
  transfers between devices with their start and end apart: 45, of which 18 were waited for; matrix products, arithmetic and copies ran while one was open for 0% of the time, Pallas kernels for 19%

profile of v2, /device:TPU:0, one launch (start us, length us, event | category | flops | bytes accessed | tf_op | source)
XLA Modules:
  0.0 135.1 jit_solution(17833249759864311681)
XLA Ops:
  0.6 3.1 %pack.2.own.refs_8_ = f32[1192,256]{1,0:T(8,128)} custom-call(s32[3,1,4]{2,1,0:T(1,128)} %bitcast.1, f32[4,1,256]{2,1,0:T(1,128)} %turnout.3, s32[4,1,256]{2,1,0:T(1,128)} %district.3, f32[4,1,3,256,256]{4,3,2,1,0:T(8,128)} %l_ref.3, f32[4,1,256,256]{3,2,1,0:T(8,128)} %d_ref.3, f32[4,1,256,128]{3,2,1,0:T(8,128)} %r_ref.3), custom_call_target="tpu_custom_call" | custom-call | bytes 2441216 | tf_op jit(solution)/shard_map/pack/pallas_call | solution.py:309
  4.2 4.7 %pack.3 = (f32[1192,256]{1,0:T(8,128)}, f32[1192,256]{1,0:T(8,128)}, f32[1192,256]{1,0:T(8,128)}) custom-call(s32[3,1,4]{2,1,0:T(1,128)} %bitcast.2, f32[4,1,256]{2,1,0:T(1,128)} %turnout.3, s32[4,1,256]{2,1,0:T(1,128)} %district.3, f32[4,1,3,256,256]{4,3,2,1,0:T(8,128)} %l_ref.3, f32[4,1,256,256]{3,2,1,0:T(8,128)} %d_ref.3, f32[4,1,256,128]{3,2,1,0:T(8,128)} %r_ref.3), custom_call_target="tpu_custom_call" | custom-call | bytes 7323648 | tf_op jit(solution)/shard_map/pack/pallas_call | solution.py:309
  9.0 1.2 near_setup.4
  11.3 1.2 far_setup.4
  14.7 1.3 collective-permute-start.5
  16.3 1.3 collective-permute-start.6
  18.5 6.5 %collective-permute-done.5.refs_0_ = f32[32,512]{1,0:T(8,128)S(1)} collective-permute-done((f32[32,512]{1,0:T(8,128)S(1)}, f32[32,512]{1,0:T(8,128)S(1)}, u32[]{:S(2)}, u32[]{:S(2)}) %collective-permute-start.5) | collective-permute-done | bytes 65568 | tf_op jit(solution)/shard_map/ppermute | solution.py:332
  25.0 3.7 %collective-permute-done.6.refs_1_ = f32[32,512]{1,0:T(8,128)S(1)} collective-permute-done((f32[32,512]{1,0:T(8,128)S(1)}, f32[32,512]{1,0:T(8,128)S(1)}, u32[]{:S(2)}, u32[]{:S(2)}) %collective-permute-start.6) | collective-permute-done | bytes 65568 | tf_op jit(solution)/shard_map/ppermute | solution.py:332
  29.0 3.4 %collective-permute-start.7 = (f32[32,512]{1,0:T(8,128)S(1)}, f32[32,512]{1,0:T(8,128)S(1)}, u32[]{:S(2)}, u32[]{:S(2)}) collective-permute-start(f32[32,512]{1,0:T(8,128)S(1)} %get-tuple-element.111), channel_id=1, source_target_pairs={{0,24},{4,28},{16,8},{20,12},{1,25},{5,29},{17,9},{21,13},{2,26},{... | collective-permute-start | bytes 196616 | tf_op jit(solution)/shard_map/ppermute | solution.py:332
  32.3 1.1 near_setup.5
  34.5 1.0 copy-done.2
  35.8 2.8 %collective-permute-start.10 = (f32[32,512]{1,0:T(8,128)S(1)}, f32[32,512]{1,0:T(8,128)S(1)}, u32[]{:S(2)}, u32[]{:S(2)}) collective-permute-start(f32[32,512]{1,0:T(8,128)S(1)} %far_terms.20), channel_id=1, source_target_pairs={{0,16},{4,20},{16,0},{20,4},{1,17},{5,21},{17,1},{21,5},{2,18},{6,... | collective-permute-start | bytes 196616 | tf_op jit(solution)/shard_map/ppermute | solution.py:332
  38.5 1.3 collective-permute-start.11
  39.9 1.2 far_setup.5
  41.0 1.2 collective-permute-done.10.refs_0_
  42.2 2.5 %collective-permute-done.11.refs_1_ = f32[32,512]{1,0:T(8,128)S(1)} collective-permute-done((f32[32,512]{1,0:T(8,128)S(1)}, f32[32,512]{1,0:T(8,128)S(1)}, u32[]{:S(2)}, u32[]{:S(2)}) %collective-permute-start.11) | collective-permute-done | bytes 65568 | tf_op jit(solution)/shard_map/ppermute | solution.py:332
  45.0 2.2 %collective-permute-start.12 = (f32[32,512]{1,0:T(8,128)S(1)}, f32[32,512]{1,0:T(8,128)S(1)}, u32[]{:S(2)}, u32[]{:S(2)}) collective-permute-start(f32[32,512]{1,0:T(8,128)S(1)} %get-tuple-element.124), channel_id=1, source_target_pairs={{16,8},{20,12},{0,24},{4,28},{17,9},{21,13},{1,25},{5,29},{18,10},... | collective-permute-start | bytes 196616 | tf_op jit(solution)/shard_map/ppermute | solution.py:332
  48.5 2.8 %collective-permute-start.14 = (f32[32,512]{1,0:T(8,128)S(1)}, f32[32,512]{1,0:T(8,128)S(1)}, u32[]{:S(2)}, u32[]{:S(2)}) collective-permute-start(f32[32,512]{1,0:T(8,128)S(1)} %far_terms.22), channel_id=1, source_target_pairs={{16,0},{20,4},{0,16},{4,20},{17,1},{21,5},{1,17},{5,21},{18,2},{22... | collective-permute-start | bytes 196616 | tf_op jit(solution)/shard_map/ppermute | solution.py:332
  52.4 1.3 collective-permute-start.15
  54.6 3.9 %collective-permute-done.15.refs_1_ = f32[32,512]{1,0:T(8,128)S(1)} collective-permute-done((f32[32,512]{1,0:T(8,128)S(1)}, f32[32,512]{1,0:T(8,128)S(1)}, u32[]{:S(2)}, u32[]{:S(2)}) %collective-permute-start.15) | collective-permute-done | bytes 65568 | tf_op jit(solution)/shard_map/ppermute | solution.py:332
  58.8 3.4 %collective-permute-start.16 = (f32[32,512]{1,0:T(8,128)S(1)}, f32[32,512]{1,0:T(8,128)S(1)}, u32[]{:S(2)}, u32[]{:S(2)}) collective-permute-start(f32[32,512]{1,0:T(8,128)S(1)} %get-tuple-element.130), channel_id=1, source_target_pairs={{0,24},{4,28},{16,8},{20,12},{1,25},{5,29},{17,9},{21,13},{2,26},{... | collective-permute-start | bytes 196616 | tf_op jit(solution)/shard_map/ppermute | solution.py:332
  62.2 1.2 near_setup.6
  64.3 1.0 copy-done.1
  65.6 3.1 %collective-permute-start.19 = (f32[32,512]{1,0:T(8,128)S(1)}, f32[32,512]{1,0:T(8,128)S(1)}, u32[]{:S(2)}, u32[]{:S(2)}) collective-permute-start(f32[32,512]{1,0:T(8,128)S(1)} %far_terms.24), channel_id=1, source_target_pairs={{0,16},{4,20},{16,0},{20,4},{1,17},{5,21},{17,1},{21,5},{2,18},{6,... | collective-permute-start | bytes 196616 | tf_op jit(solution)/shard_map/ppermute | solution.py:332
  68.7 1.3 collective-permute-start.20
  70.0 1.2 far_setup.6
  72.0 2.9 %collective-permute-done.20.refs_1_ = f32[32,512]{1,0:T(8,128)S(1)} collective-permute-done((f32[32,512]{1,0:T(8,128)S(1)}, f32[32,512]{1,0:T(8,128)S(1)}, u32[]{:S(2)}, u32[]{:S(2)}) %collective-permute-start.20) | collective-permute-done | bytes 65568 | tf_op jit(solution)/shard_map/ppermute | solution.py:332
  75.2 1.9 %collective-permute-start.21 = (f32[32,512]{1,0:T(8,128)S(1)}, f32[32,512]{1,0:T(8,128)S(1)}, u32[]{:S(2)}, u32[]{:S(2)}) collective-permute-start(f32[32,512]{1,0:T(8,128)S(1)} %get-tuple-element.143), channel_id=1, source_target_pairs={{16,8},{20,12},{0,24},{4,28},{17,9},{21,13},{1,25},{5,29},{18,10},... | collective-permute-start | bytes 196616 | tf_op jit(solution)/shard_map/ppermute | solution.py:332
  78.3 3.1 %collective-permute-start.23 = (f32[32,512]{1,0:T(8,128)S(1)}, f32[32,512]{1,0:T(8,128)S(1)}, u32[]{:S(2)}, u32[]{:S(2)}) collective-permute-start(f32[32,512]{1,0:T(8,128)S(1)} %far_terms.26), channel_id=1, source_target_pairs={{16,0},{20,4},{0,16},{4,20},{17,1},{21,5},{1,17},{5,21},{18,2},{22... | collective-permute-start | bytes 196616 | tf_op jit(solution)/shard_map/ppermute | solution.py:332
  82.6 1.3 collective-permute-start.24
  85.0 3.7 %collective-permute-done.24.refs_1_ = f32[32,512]{1,0:T(8,128)S(1)} collective-permute-done((f32[32,512]{1,0:T(8,128)S(1)}, f32[32,512]{1,0:T(8,128)S(1)}, u32[]{:S(2)}, u32[]{:S(2)}) %collective-permute-start.24) | collective-permute-done | bytes 65568 | tf_op jit(solution)/shard_map/ppermute | solution.py:332
  89.3 2.8 %collective-permute-start.27 = (f32[32,512]{1,0:T(8,128)S(1)}, f32[32,512]{1,0:T(8,128)S(1)}, u32[]{:S(2)}, u32[]{:S(2)}) collective-permute-start(f32[32,512]{1,0:T(8,128)S(1)} %far_terms.27), channel_id=1, source_target_pairs={{0,16},{4,20},{16,0},{20,4},{1,17},{5,21},{17,1},{21,5},{2,18},{6,... | collective-permute-start | bytes 196616 | tf_op jit(solution)/shard_map/ppermute | solution.py:332
  92.1 1.5 %collective-permute-start.25 = (f32[32,512]{1,0:T(8,128)S(1)}, f32[32,512]{1,0:T(8,128)S(1)}, u32[]{:S(2)}, u32[]{:S(2)}) collective-permute-start(f32[32,512]{1,0:T(8,128)S(1)} %get-tuple-element.150), channel_id=1, source_target_pairs={{0,24},{4,28},{16,8},{20,12},{1,25},{5,29},{17,9},{21,13},{2,26},{... | collective-permute-start | bytes 196616 | tf_op jit(solution)/shard_map/ppermute | solution.py:332
  93.5 1.1 near_setup.7
  95.7 1.3 collective-permute-start.28
  97.0 1.2 far_setup.7
  98.2 3.9 %collective-permute-done.28.refs_1_ = f32[32,512]{1,0:T(8,128)S(1)} collective-permute-done((f32[32,512]{1,0:T(8,128)S(1)}, f32[32,512]{1,0:T(8,128)S(1)}, u32[]{:S(2)}, u32[]{:S(2)}) %collective-permute-start.28) | collective-permute-done | bytes 65568 | tf_op jit(solution)/shard_map/ppermute | solution.py:332
  102.3 2.0 %collective-permute-start.30 = (f32[32,512]{1,0:T(8,128)S(1)}, f32[32,512]{1,0:T(8,128)S(1)}, u32[]{:S(2)}, u32[]{:S(2)}) collective-permute-start(f32[32,512]{1,0:T(8,128)S(1)} %get-tuple-element.164), channel_id=1, source_target_pairs={{16,8},{20,12},{0,24},{4,28},{17,9},{21,13},{1,25},{5,29},{18,10},... | collective-permute-start | bytes 196616 | tf_op jit(solution)/shard_map/ppermute | solution.py:332
  105.6 2.9 %collective-permute-start.31 = (f32[32,512]{1,0:T(8,128)S(1)}, f32[32,512]{1,0:T(8,128)S(1)}, u32[]{:S(2)}, u32[]{:S(2)}) collective-permute-start(f32[32,512]{1,0:T(8,128)S(1)} %far_terms.29), channel_id=1, source_target_pairs={{16,0},{20,4},{0,16},{4,20},{17,1},{21,5},{1,17},{5,21},{18,2},{22... | collective-permute-start | bytes 196616 | tf_op jit(solution)/shard_map/ppermute | solution.py:332
  109.7 1.3 collective-permute-start.32
  112.0 3.9 %collective-permute-done.32.refs_1_ = f32[32,512]{1,0:T(8,128)S(1)} collective-permute-done((f32[32,512]{1,0:T(8,128)S(1)}, f32[32,512]{1,0:T(8,128)S(1)}, u32[]{:S(2)}, u32[]{:S(2)}) %collective-permute-start.32) | collective-permute-done | bytes 65568 | tf_op jit(solution)/shard_map/ppermute | solution.py:332
  117.1 1.3 collective-permute-start.35
  118.7 1.3 collective-permute-start.36
  120.6 2.6 %collective-permute-done.35.refs_0_ = f32[32,512]{1,0:T(8,128)S(1)} collective-permute-done((f32[32,512]{1,0:T(8,128)S(1)}, f32[32,512]{1,0:T(8,128)S(1)}, u32[]{:S(2)}, u32[]{:S(2)}) %collective-permute-start.35) | collective-permute-done | bytes 65568 | tf_op jit(solution)/shard_map/ppermute | solution.py:332
  123.2 3.4 %collective-permute-done.36.refs_1_ = f32[32,512]{1,0:T(8,128)S(1)} collective-permute-done((f32[32,512]{1,0:T(8,128)S(1)}, f32[32,512]{1,0:T(8,128)S(1)}, u32[]{:S(2)}, u32[]{:S(2)}) %collective-permute-start.36) | collective-permute-done | bytes 65568 | tf_op jit(solution)/shard_map/ppermute | solution.py:332
  127.8 2.9 %collective-permute-start.39 = (f32[64,128]{1,0:T(8,128)S(1)}, f32[64,128]{1,0:T(8,128)S(1)}, u32[]{:S(2)}, u32[]{:S(2)}) collective-permute-start(f32[64,128]{1,0:T(8,128)S(1)} %get-tuple-element.178), channel_id=1, source_target_pairs={{0,24},{4,28},{8,0},{12,4},{16,8},{20,12},{24,16},{28,20},{1,25},{... | collective-permute-start | bytes 98312 | tf_op jit(solution)/shard_map/ppermute | solution.py:324
  130.7 1.0 field.1
  133.2 1.2 collective-permute-done.44.got
  (101 shorter events, 27.0 us)
Async XLA Ops:
  3.7 5.2 %copy-start = (f32[1192,256]{1,0:T(8,128)S(1)}, f32[1192,256]{1,0:T(8,128)}, u32[]{:S(2)}) copy-start(f32[1192,256]{1,0:T(8,128)} %pack.2.own.refs_8_) | copy-start | bytes 3661828
  3.7 5.2 %collective-permute-start = (f32[1192,256]{1,0:T(8,128)}, f32[1192,256]{1,0:T(8,128)S(1)}, u32[]{:S(2)}, u32[]{:S(2)}) collective-permute-start(f32[1192,256]{1,0:T(8,128)} %pack.2.own.refs_8_), channel_id=1, source_target_pairs={{0,4},{4,0},{8,12},{12,8},{16,20},{20,16},{24,28},{28,24},{1,5},{5... | collective-permute-start | bytes 3661832 | tf_op jit(solution)/shard_map/ppermute | solution.py:321
  8.9 1.5 %copy-start.3 = (f32[1192,256]{1,0:T(8,128)S(1)}, f32[1192,256]{1,0:T(8,128)}, u32[]{:S(2)}) copy-start(f32[1192,256]{1,0:T(8,128)} %get-tuple-element.113.own.refs_8_) | copy-start | bytes 3661828
  10.4 21.9 %collective-permute-start.8 = (f32[1192,256]{1,0:T(8,128)S(1)}, f32[1192,256]{1,0:T(8,128)S(1)}, u32[]{:S(2)}, u32[]{:S(2)}) collective-permute-start(f32[1192,256]{1,0:T(8,128)S(1)} %copy-done.3), channel_id=1, source_target_pairs={{0,4},{4,0},{8,12},{12,8},{16,20},{20,16},{24,28},{28,24},{1,5},{5... | collective-permute-start | bytes 3661832 | tf_op jit(solution)/shard_map/ppermute | solution.py:321
  10.6 2.8 %collective-permute-start.2 = (f32[32,512]{1,0:T(8,128)S(1)}, f32[32,512]{1,0:T(8,128)S(1)}, u32[]{:S(2)}, u32[]{:S(2)}) collective-permute-start(f32[32,512]{1,0:T(8,128)S(1)} %get-tuple-element.106), channel_id=1, source_target_pairs={{24,16},{28,20},{25,17},{29,21},{26,18},{30,22},{27,19},{31,23}} | collective-permute-start | bytes 196616 | tf_op jit(solution)/shard_map/ppermute | solution.py:332
  12.7 3.2 %collective-permute-start.1 = (f32[32,512]{1,0:T(8,128)S(1)}, f32[32,512]{1,0:T(8,128)S(1)}, u32[]{:S(2)}, u32[]{:S(2)}) collective-permute-start(f32[32,512]{1,0:T(8,128)S(1)} %far_terms.16), channel_id=1, source_target_pairs={{24,8},{28,12},{25,9},{29,13},{26,10},{30,14},{27,11},{31,15}} | collective-permute-start | bytes 196616 | tf_op jit(solution)/shard_map/ppermute | solution.py:332
  13.7 2.3 %collective-permute-start.3 = (f32[32,512]{1,0:T(8,128)S(1)}, f32[32,512]{1,0:T(8,128)S(1)}, u32[]{:S(2)}, u32[]{:S(2)}) collective-permute-start(f32[32,512]{1,0:T(8,128)S(1)} %get-tuple-element.107), channel_id=1, source_target_pairs={{16,8},{20,12},{17,9},{21,13},{18,10},{22,14},{19,11},{23,15}} | collective-permute-start | bytes 196616 | tf_op jit(solution)/shard_map/ppermute | solution.py:332
  14.7 10.3 %collective-permute-start.5 = (f32[32,512]{1,0:T(8,128)S(1)}, f32[32,512]{1,0:T(8,128)S(1)}, u32[]{:S(2)}, u32[]{:S(2)}) collective-permute-start(f32[32,512]{1,0:T(8,128)S(1)} %far_terms.18), channel_id=1, source_target_pairs={{16,0},{20,4},{17,1},{21,5},{18,2},{22,6},{19,3},{23,7}} | collective-permute-start | bytes 196616 | tf_op jit(solution)/shard_map/ppermute | solution.py:332
  16.3 12.4 %collective-permute-start.6 = (f32[32,512]{1,0:T(8,128)S(1)}, f32[32,512]{1,0:T(8,128)S(1)}, u32[]{:S(2)}, u32[]{:S(2)}) collective-permute-start(f32[32,512]{1,0:T(8,128)S(1)} %get-tuple-element.110), channel_id=1, source_target_pairs={{8,0},{12,4},{24,16},{28,20},{9,1},{13,5},{25,17},{29,21},{10,2},{... | collective-permute-start | bytes 196616 | tf_op jit(solution)/shard_map/ppermute | solution.py:332
  17.8 15.7 %collective-permute-start.4 = (f32[32,512]{1,0:T(8,128)S(1)}, f32[32,512]{1,0:T(8,128)S(1)}, u32[]{:S(2)}, u32[]{:S(2)}) collective-permute-start(f32[32,512]{1,0:T(8,128)S(1)} %far_terms.17), channel_id=1, source_target_pairs={{8,24},{12,28},{24,8},{28,12},{9,25},{13,29},{25,9},{29,13},{10,26... | collective-permute-start | bytes 196616 | tf_op jit(solution)/shard_map/ppermute | solution.py:332
  29.0 5.3 %collective-permute-start.7 = (f32[32,512]{1,0:T(8,128)S(1)}, f32[32,512]{1,0:T(8,128)S(1)}, u32[]{:S(2)}, u32[]{:S(2)}) collective-permute-start(f32[32,512]{1,0:T(8,128)S(1)} %get-tuple-element.111), channel_id=1, source_target_pairs={{0,24},{4,28},{16,8},{20,12},{1,25},{5,29},{17,9},{21,13},{2,26},{... | collective-permute-start | bytes 196616 | tf_op jit(solution)/shard_map/ppermute | solution.py:332
  34.2 1.3 copy-start.2
  35.5 26.7 %collective-permute-start.17 = (f32[1192,256]{1,0:T(8,128)S(1)}, f32[1192,256]{1,0:T(8,128)S(1)}, u32[]{:S(2)}, u32[]{:S(2)}) collective-permute-start(f32[1192,256]{1,0:T(8,128)S(1)} %copy-done.2), channel_id=1, source_target_pairs={{0,4},{4,0},{8,12},{12,8},{16,20},{20,16},{24,28},{28,24},{1,5},{5... | collective-permute-start | bytes 3661832 | tf_op jit(solution)/shard_map/ppermute | solution.py:321
  35.8 6.4 %collective-permute-start.10 = (f32[32,512]{1,0:T(8,128)S(1)}, f32[32,512]{1,0:T(8,128)S(1)}, u32[]{:S(2)}, u32[]{:S(2)}) collective-permute-start(f32[32,512]{1,0:T(8,128)S(1)} %far_terms.20), channel_id=1, source_target_pairs={{0,16},{4,20},{16,0},{20,4},{1,17},{5,21},{17,1},{21,5},{2,18},{6,... | collective-permute-start | bytes 196616 | tf_op jit(solution)/shard_map/ppermute | solution.py:332
  38.5 6.2 %collective-permute-start.11 = (f32[32,512]{1,0:T(8,128)S(1)}, f32[32,512]{1,0:T(8,128)S(1)}, u32[]{:S(2)}, u32[]{:S(2)}) collective-permute-start(f32[32,512]{1,0:T(8,128)S(1)} %get-tuple-element.123), channel_id=1, source_target_pairs={{24,16},{28,20},{8,0},{12,4},{25,17},{29,21},{9,1},{13,5},{26,18},... | collective-permute-start | bytes 196616 | tf_op jit(solution)/shard_map/ppermute | solution.py:332
  45.0 7.1 %collective-permute-start.12 = (f32[32,512]{1,0:T(8,128)S(1)}, f32[32,512]{1,0:T(8,128)S(1)}, u32[]{:S(2)}, u32[]{:S(2)}) collective-permute-start(f32[32,512]{1,0:T(8,128)S(1)} %get-tuple-element.124), channel_id=1, source_target_pairs={{16,8},{20,12},{0,24},{4,28},{17,9},{21,13},{1,25},{5,29},{18,10},... | collective-permute-start | bytes 196616 | tf_op jit(solution)/shard_map/ppermute | solution.py:332
  47.5 4.6 %collective-permute-start.9 = (f32[32,512]{1,0:T(8,128)S(1)}, f32[32,512]{1,0:T(8,128)S(1)}, u32[]{:S(2)}, u32[]{:S(2)}) collective-permute-start(f32[32,512]{1,0:T(8,128)S(1)} %far_terms.19), channel_id=1, source_target_pairs={{24,8},{28,12},{8,24},{12,28},{25,9},{29,13},{9,25},{13,29},{26,10... | collective-permute-start | bytes 196616 | tf_op jit(solution)/shard_map/ppermute | solution.py:332
  48.5 6.2 %collective-permute-start.14 = (f32[32,512]{1,0:T(8,128)S(1)}, f32[32,512]{1,0:T(8,128)S(1)}, u32[]{:S(2)}, u32[]{:S(2)}) collective-permute-start(f32[32,512]{1,0:T(8,128)S(1)} %far_terms.22), channel_id=1, source_target_pairs={{16,0},{20,4},{0,16},{4,20},{17,1},{21,5},{1,17},{5,21},{18,2},{22... | collective-permute-start | bytes 196616 | tf_op jit(solution)/shard_map/ppermute | solution.py:332
  52.4 6.2 %collective-permute-start.15 = (f32[32,512]{1,0:T(8,128)S(1)}, f32[32,512]{1,0:T(8,128)S(1)}, u32[]{:S(2)}, u32[]{:S(2)}) collective-permute-start(f32[32,512]{1,0:T(8,128)S(1)} %get-tuple-element.129), channel_id=1, source_target_pairs={{8,0},{12,4},{24,16},{28,20},{9,1},{13,5},{25,17},{29,21},{10,2},{... | collective-permute-start | bytes 196616 | tf_op jit(solution)/shard_map/ppermute | solution.py:332
  53.9 9.5 %collective-permute-start.13 = (f32[32,512]{1,0:T(8,128)S(1)}, f32[32,512]{1,0:T(8,128)S(1)}, u32[]{:S(2)}, u32[]{:S(2)}) collective-permute-start(f32[32,512]{1,0:T(8,128)S(1)} %far_terms.21), channel_id=1, source_target_pairs={{8,24},{12,28},{24,8},{28,12},{9,25},{13,29},{25,9},{29,13},{10,26... | collective-permute-start | bytes 196616 | tf_op jit(solution)/shard_map/ppermute | solution.py:332
  58.8 5.3 %collective-permute-start.16 = (f32[32,512]{1,0:T(8,128)S(1)}, f32[32,512]{1,0:T(8,128)S(1)}, u32[]{:S(2)}, u32[]{:S(2)}) collective-permute-start(f32[32,512]{1,0:T(8,128)S(1)} %get-tuple-element.130), channel_id=1, source_target_pairs={{0,24},{4,28},{16,8},{20,12},{1,25},{5,29},{17,9},{21,13},{2,26},{... | collective-permute-start | bytes 196616 | tf_op jit(solution)/shard_map/ppermute | solution.py:332
  65.4 28.2 %collective-permute-start.26 = (f32[1192,256]{1,0:T(8,128)S(1)}, f32[1192,256]{1,0:T(8,128)S(1)}, u32[]{:S(2)}, u32[]{:S(2)}) collective-permute-start(f32[1192,256]{1,0:T(8,128)S(1)} %copy-done.1), channel_id=1, source_target_pairs={{0,4},{4,0},{8,12},{12,8},{16,20},{20,16},{24,28},{28,24},{1,5},{5... | collective-permute-start | bytes 3661832 | tf_op jit(solution)/shard_map/ppermute | solution.py:321
  65.6 6.4 %collective-permute-start.19 = (f32[32,512]{1,0:T(8,128)S(1)}, f32[32,512]{1,0:T(8,128)S(1)}, u32[]{:S(2)}, u32[]{:S(2)}) collective-permute-start(f32[32,512]{1,0:T(8,128)S(1)} %far_terms.24), channel_id=1, source_target_pairs={{0,16},{4,20},{16,0},{20,4},{1,17},{5,21},{17,1},{21,5},{2,18},{6,... | collective-permute-start | bytes 196616 | tf_op jit(solution)/shard_map/ppermute | solution.py:332
  68.7 6.2 %collective-permute-start.20 = (f32[32,512]{1,0:T(8,128)S(1)}, f32[32,512]{1,0:T(8,128)S(1)}, u32[]{:S(2)}, u32[]{:S(2)}) collective-permute-start(f32[32,512]{1,0:T(8,128)S(1)} %get-tuple-element.142), channel_id=1, source_target_pairs={{24,16},{28,20},{8,0},{12,4},{25,17},{29,21},{9,1},{13,5},{26,18},... | collective-permute-start | bytes 196616 | tf_op jit(solution)/shard_map/ppermute | solution.py:332
  75.2 7.1 %collective-permute-start.21 = (f32[32,512]{1,0:T(8,128)S(1)}, f32[32,512]{1,0:T(8,128)S(1)}, u32[]{:S(2)}, u32[]{:S(2)}) collective-permute-start(f32[32,512]{1,0:T(8,128)S(1)} %get-tuple-element.143), channel_id=1, source_target_pairs={{16,8},{20,12},{0,24},{4,28},{17,9},{21,13},{1,25},{5,29},{18,10},... | collective-permute-start | bytes 196616 | tf_op jit(solution)/shard_map/ppermute | solution.py:332
  77.3 5.0 %collective-permute-start.18 = (f32[32,512]{1,0:T(8,128)S(1)}, f32[32,512]{1,0:T(8,128)S(1)}, u32[]{:S(2)}, u32[]{:S(2)}) collective-permute-start(f32[32,512]{1,0:T(8,128)S(1)} %far_terms.23), channel_id=1, source_target_pairs={{24,8},{28,12},{8,24},{12,28},{25,9},{29,13},{9,25},{13,29},{26,10... | collective-permute-start | bytes 196616 | tf_op jit(solution)/shard_map/ppermute | solution.py:332
  78.3 6.7 %collective-permute-start.23 = (f32[32,512]{1,0:T(8,128)S(1)}, f32[32,512]{1,0:T(8,128)S(1)}, u32[]{:S(2)}, u32[]{:S(2)}) collective-permute-start(f32[32,512]{1,0:T(8,128)S(1)} %far_terms.26), channel_id=1, source_target_pairs={{16,0},{20,4},{0,16},{4,20},{17,1},{21,5},{1,17},{5,21},{18,2},{22... | collective-permute-start | bytes 196616 | tf_op jit(solution)/shard_map/ppermute | solution.py:332
  82.6 6.2 %collective-permute-start.24 = (f32[32,512]{1,0:T(8,128)S(1)}, f32[32,512]{1,0:T(8,128)S(1)}, u32[]{:S(2)}, u32[]{:S(2)}) collective-permute-start(f32[32,512]{1,0:T(8,128)S(1)} %get-tuple-element.149), channel_id=1, source_target_pairs={{8,0},{12,4},{24,16},{28,20},{9,1},{13,5},{25,17},{29,21},{10,2},{... | collective-permute-start | bytes 196616 | tf_op jit(solution)/shard_map/ppermute | solution.py:332
  84.1 10.5 %collective-permute-start.22 = (f32[32,512]{1,0:T(8,128)S(1)}, f32[32,512]{1,0:T(8,128)S(1)}, u32[]{:S(2)}, u32[]{:S(2)}) collective-permute-start(f32[32,512]{1,0:T(8,128)S(1)} %far_terms.25), channel_id=1, source_target_pairs={{8,24},{12,28},{24,8},{28,12},{9,25},{13,29},{25,9},{29,13},{10,26... | collective-permute-start | bytes 196616 | tf_op jit(solution)/shard_map/ppermute | solution.py:332
  89.3 8.9 %collective-permute-start.27 = (f32[32,512]{1,0:T(8,128)S(1)}, f32[32,512]{1,0:T(8,128)S(1)}, u32[]{:S(2)}, u32[]{:S(2)}) collective-permute-start(f32[32,512]{1,0:T(8,128)S(1)} %far_terms.27), channel_id=1, source_target_pairs={{0,16},{4,20},{16,0},{20,4},{1,17},{5,21},{17,1},{21,5},{2,18},{6,... | collective-permute-start | bytes 196616 | tf_op jit(solution)/shard_map/ppermute | solution.py:332
  92.1 3.3 %collective-permute-start.25 = (f32[32,512]{1,0:T(8,128)S(1)}, f32[32,512]{1,0:T(8,128)S(1)}, u32[]{:S(2)}, u32[]{:S(2)}) collective-permute-start(f32[32,512]{1,0:T(8,128)S(1)} %get-tuple-element.150), channel_id=1, source_target_pairs={{0,24},{4,28},{16,8},{20,12},{1,25},{5,29},{17,9},{21,13},{2,26},{... | collective-permute-start | bytes 196616 | tf_op jit(solution)/shard_map/ppermute | solution.py:332
  95.7 6.3 %collective-permute-start.28 = (f32[32,512]{1,0:T(8,128)S(1)}, f32[32,512]{1,0:T(8,128)S(1)}, u32[]{:S(2)}, u32[]{:S(2)}) collective-permute-start(f32[32,512]{1,0:T(8,128)S(1)} %get-tuple-element.158), channel_id=1, source_target_pairs={{24,16},{28,20},{8,0},{12,4},{25,17},{29,21},{9,1},{13,5},{26,18},... | collective-permute-start | bytes 196616 | tf_op jit(solution)/shard_map/ppermute | solution.py:332
  102.3 7.1 %collective-permute-start.30 = (f32[32,512]{1,0:T(8,128)S(1)}, f32[32,512]{1,0:T(8,128)S(1)}, u32[]{:S(2)}, u32[]{:S(2)}) collective-permute-start(f32[32,512]{1,0:T(8,128)S(1)} %get-tuple-element.164), channel_id=1, source_target_pairs={{16,8},{20,12},{0,24},{4,28},{17,9},{21,13},{1,25},{5,29},{18,10},... | collective-permute-start | bytes 196616 | tf_op jit(solution)/shard_map/ppermute | solution.py:332
  104.6 4.8 %collective-permute-start.29 = (f32[32,512]{1,0:T(8,128)S(1)}, f32[32,512]{1,0:T(8,128)S(1)}, u32[]{:S(2)}, u32[]{:S(2)}) collective-permute-start(f32[32,512]{1,0:T(8,128)S(1)} %far_terms.28), channel_id=1, source_target_pairs={{24,8},{28,12},{8,24},{12,28},{25,9},{29,13},{9,25},{13,29},{26,10... | collective-permute-start | bytes 196616 | tf_op jit(solution)/shard_map/ppermute | solution.py:332
  105.6 6.4 %collective-permute-start.31 = (f32[32,512]{1,0:T(8,128)S(1)}, f32[32,512]{1,0:T(8,128)S(1)}, u32[]{:S(2)}, u32[]{:S(2)}) collective-permute-start(f32[32,512]{1,0:T(8,128)S(1)} %far_terms.29), channel_id=1, source_target_pairs={{16,0},{20,4},{0,16},{4,20},{17,1},{21,5},{1,17},{5,21},{18,2},{22... | collective-permute-start | bytes 196616 | tf_op jit(solution)/shard_map/ppermute | solution.py:332
  109.7 6.2 %collective-permute-start.32 = (f32[32,512]{1,0:T(8,128)S(1)}, f32[32,512]{1,0:T(8,128)S(1)}, u32[]{:S(2)}, u32[]{:S(2)}) collective-permute-start(f32[32,512]{1,0:T(8,128)S(1)} %get-tuple-element.169), channel_id=1, source_target_pairs={{8,0},{12,4},{24,16},{28,20},{9,1},{13,5},{25,17},{29,21},{10,2},{... | collective-permute-start | bytes 196616 | tf_op jit(solution)/shard_map/ppermute | solution.py:332
  111.3 7.1 %collective-permute-start.33 = (f32[32,512]{1,0:T(8,128)S(1)}, f32[32,512]{1,0:T(8,128)S(1)}, u32[]{:S(2)}, u32[]{:S(2)}) collective-permute-start(f32[32,512]{1,0:T(8,128)S(1)} %far_terms.30), channel_id=1, source_target_pairs={{24,8},{28,12},{25,9},{29,13},{26,10},{30,14},{27,11},{31,15}} | collective-permute-start | bytes 196616 | tf_op jit(solution)/shard_map/ppermute | solution.py:332
  116.1 2.3 %collective-permute-start.34 = (f32[32,512]{1,0:T(8,128)S(1)}, f32[32,512]{1,0:T(8,128)S(1)}, u32[]{:S(2)}, u32[]{:S(2)}) collective-permute-start(f32[32,512]{1,0:T(8,128)S(1)} %get-tuple-element.171), channel_id=1, source_target_pairs={{16,8},{20,12},{17,9},{21,13},{18,10},{22,14},{19,11},{23,15}} | collective-permute-start | bytes 196616 | tf_op jit(solution)/shard_map/ppermute | solution.py:332
  117.1 6.2 %collective-permute-start.35 = (f32[32,512]{1,0:T(8,128)S(1)}, f32[32,512]{1,0:T(8,128)S(1)}, u32[]{:S(2)}, u32[]{:S(2)}) collective-permute-start(f32[32,512]{1,0:T(8,128)S(1)} %far_terms.31), channel_id=1, source_target_pairs={{16,0},{20,4},{17,1},{21,5},{18,2},{22,6},{19,3},{23,7}} | collective-permute-start | bytes 196616 | tf_op jit(solution)/shard_map/ppermute | solution.py:332
  118.7 8.0 %collective-permute-start.36 = (f32[32,512]{1,0:T(8,128)S(1)}, f32[32,512]{1,0:T(8,128)S(1)}, u32[]{:S(2)}, u32[]{:S(2)}) collective-permute-start(f32[32,512]{1,0:T(8,128)S(1)} %get-tuple-element.173), channel_id=1, source_target_pairs={{8,0},{12,4},{9,1},{13,5},{10,2},{14,6},{11,3},{15,7}} | collective-permute-start | bytes 196616 | tf_op jit(solution)/shard_map/ppermute | solution.py:332
  120.0 7.7 %collective-permute-start.43 = (f32[64,256]{1,0:T(8,128)S(1)}, f32[64,256]{1,0:T(8,128)S(1)}, u32[]{:S(2)}, u32[]{:S(2)}) collective-permute-start(f32[64,256]{1,0:T(8,128)S(1)} %get-tuple-element.186), channel_id=1, source_target_pairs={{0,4},{4,0},{8,12},{12,8},{16,20},{20,16},{24,28},{28,24},{1,5},{5... | collective-permute-start | bytes 196616 | tf_op jit(solution)/shard_map/ppermute | solution.py:321
  120.1 7.7 %collective-permute-start.42 = (f32[64,256]{1,0:T(8,128)S(1)}, f32[64,256]{1,0:T(8,128)S(1)}, u32[]{:S(2)}, u32[]{:S(2)}) collective-permute-start(f32[64,256]{1,0:T(8,128)S(1)} %get-tuple-element.185), channel_id=1, source_target_pairs={{0,4},{4,0},{8,12},{12,8},{16,20},{20,16},{24,28},{28,24},{1,5},{5... | collective-permute-start | bytes 196616 | tf_op jit(solution)/shard_map/ppermute | solution.py:321
  120.6 10.1 %collective-permute-start.41 = (f32[64,256]{1,0:T(8,128)S(1)}, f32[64,256]{1,0:T(8,128)S(1)}, u32[]{:S(2)}, u32[]{:S(2)}) collective-permute-start(f32[64,256]{1,0:T(8,128)S(1)} %get-tuple-element.184), channel_id=1, source_target_pairs={{0,4},{4,0},{8,12},{12,8},{16,20},{20,16},{24,28},{28,24},{1,5},{5... | collective-permute-start | bytes 196616 | tf_op jit(solution)/shard_map/ppermute | solution.py:321
  127.6 3.1 %collective-permute-start.40 = (f32[64,256]{1,0:T(8,128)S(1)}, f32[64,256]{1,0:T(8,128)S(1)}, u32[]{:S(2)}, u32[]{:S(2)}) collective-permute-start(f32[64,256]{1,0:T(8,128)S(1)} %get-tuple-element.183), channel_id=1, source_target_pairs={{0,4},{4,0},{8,12},{12,8},{16,20},{20,16},{24,28},{28,24},{1,5},{5... | collective-permute-start | bytes 196616 | tf_op jit(solution)/shard_map/ppermute | solution.py:321
  127.7 5.0 %collective-permute-start.37 = (f32[64,128]{1,0:T(8,128)S(1)}, f32[64,128]{1,0:T(8,128)S(1)}, u32[]{:S(2)}, u32[]{:S(2)}) collective-permute-start(f32[64,128]{1,0:T(8,128)S(1)} %get-tuple-element.176), channel_id=1, source_target_pairs={{0,8},{4,12},{8,16},{12,20},{16,24},{20,28},{24,0},{28,4},{1,9},{5... | collective-permute-start | bytes 98312 | tf_op jit(solution)/shard_map/ppermute | solution.py:324
  127.7 5.0 %collective-permute-start.38 = (f32[64,128]{1,0:T(8,128)S(1)}, f32[64,128]{1,0:T(8,128)S(1)}, u32[]{:S(2)}, u32[]{:S(2)}) collective-permute-start(f32[64,128]{1,0:T(8,128)S(1)} %get-tuple-element.177), channel_id=1, source_target_pairs={{0,16},{4,20},{8,24},{12,28},{16,0},{20,4},{24,8},{28,12},{1,17},{... | collective-permute-start | bytes 98312 | tf_op jit(solution)/shard_map/ppermute | solution.py:324
  127.8 5.3 %collective-permute-start.39 = (f32[64,128]{1,0:T(8,128)S(1)}, f32[64,128]{1,0:T(8,128)S(1)}, u32[]{:S(2)}, u32[]{:S(2)}) collective-permute-start(f32[64,128]{1,0:T(8,128)S(1)} %get-tuple-element.178), channel_id=1, source_target_pairs={{0,24},{4,28},{8,0},{12,4},{16,8},{20,12},{24,16},{28,20},{1,25},{... | collective-permute-start | bytes 98312 | tf_op jit(solution)/shard_map/ppermute | solution.py:324
  133.1 1.2 collective-permute-start.44
  (1 other events, 1.3 us)

commit v3 on v2

--- a/solution.py
+++ b/solution.py
@@ -61,10 +61,10 @@
 
 def pack_kernel(rows, cols, turnout, district, l_ref, d_ref, r_ref, *refs):
     outs = refs[: len(rows)]
-    held, sems = refs[len(rows) :]
+    held, tail, sems = refs[len(rows) :]
     slots, bs = l_ref.shape[2], l_ref.shape[3]
     columns = r_ref.shape[3]
-    rhs_at, col_at, turnout_at, district_at, _ = packed_places(slots, bs, columns)
+    rhs_at, col_at, turnout_at, district_at, end = packed_places(slots, bs, columns)
     copies = []
 
     def copy(source, target):
@@ -77,17 +77,18 @@
         for k in range(slots):
             copy(l_ref.at[r, 0, k], out.at[pl.ds(k * bs, bs)])
         copy(d_ref.at[r, 0], out.at[pl.ds(slots * bs, bs)])
-    for out, r in zip(outs, rows):
+    for i, r in enumerate(rows):
         for k in range(slots):
-            at = col_at + 8 * k
-            out[at : at + 8] = jnp.full((8, bs), cols[k, 0, r].astype(F32))
-        out[turnout_at : turnout_at + 8] = jnp.broadcast_to(turnout[r], (8, bs))
-        out[district_at : district_at + 8] = jnp.broadcast_to(
-            district[r].astype(F32), (8, bs)
-        )
+            at = col_at - rhs_at + 8 * k
+            tail[i, at : at + 8] = jnp.full((8, bs), cols[k, 0, r].astype(F32))
+        at = turnout_at - rhs_at
+        tail[i, at : at + 8] = jnp.broadcast_to(turnout[r], (8, bs))
+        at = district_at - rhs_at
+        tail[i, at : at + 8] = jnp.broadcast_to(district[r].astype(F32), (8, bs))
     for i, out in enumerate(outs):
         copies[i].wait()
-        out[rhs_at:col_at] = held[i].T
+        tail[i, :columns] = held[i].T
+        copy(tail.at[i], out.at[pl.ds(rhs_at, end - rhs_at)])
     for started in copies[len(rows) :]:
         started.wait()
 
@@ -294,7 +295,7 @@
 def body(rhs, lower_blocks, col_index, diag_inverse, turnout, district_of):
     n = lax.axis_size("blk")
     pairs = n // 2
-    pieces = max(pairs // 2, 1)
+    pieces = 1
     rows_here, _, bs, columns = rhs.shape
     slots = lower_blocks.shape[2]
     half = columns // 2
@@ -310,7 +311,7 @@
             kernel,
             out_shape=outs,
             in_specs=more.pop("in_specs", [VMEM_SPEC] * len(operands)),
-            out_specs=(VMEM_SPEC,) * len(outs) if several else VMEM_SPEC,
+            out_specs=more.pop("out_specs", (VMEM_SPEC,) * len(outs) if several else VMEM_SPEC),
             compiler_params=params(mib),
             cost_estimate=cost(flops, moved),
             name=name,
@@ -322,14 +323,6 @@
 
     def shift(x, by):
         return lax.ppermute(x, "blk", [(i, (i + 2 * by) % n) for i in range(n)])
-
-    def pass_on(x, lead, by):
-        perm = []
-        for k in range(lead, lead + 2 * pieces, 2):
-            if by <= k < count:
-                sender, target = k % pairs, (k - by) % pairs
-                perm += [(2 * sender + c, 2 * target + c) for c in range(2)]
-        return lax.ppermute(x, "blk", perm)
 
     def pack(rows):
         return call(
@@ -340,9 +333,11 @@
             56,
             moved=8 * packed_rows * bs * len(rows),
             in_specs=[SMEM_SPEC, VMEM_SPEC, VMEM_SPEC] + [HBM_SPEC] * 3,
+            out_specs=(HBM_SPEC,) * len(rows),
             scratch_shapes=[
                 pltpu.VMEM((len(rows), bs, columns), F32),
-                pltpu.SemaphoreType.DMA((len(rows) * (slots + 2),)),
+                pltpu.VMEM((len(rows), packed_rows - (slots + 1) * bs, bs), F32),
+                pltpu.SemaphoreType.DMA((len(rows) * (slots + 3),)),
             ],
         )
 
@@ -423,7 +418,7 @@
             6 * width * bs * 4,
         )
         values.append(v)
-        near = pass_on(near_out[0], lead, 1) if has_near else None
+        near = shift(near_out[0], -1) if has_near else None
         if has_near and (lead + 1) % pairs == 0 and 0 < lead // pairs:
             r = lead // pairs - 1
             own, _ = lax.optimization_barrier((packed[r], near_out[0]))
@@ -441,7 +436,7 @@
                 6 * width * 4 * bs * bs,
                 6 * width * bs * 4,
             )
-            far_next = pass_on(far_out, lead, 2)
+            far_next = shift(far_out, -2)
         done = lead + 2 * (pieces - 1)
         if done % pairs == 0 and 0 < done // pairs <= top:
             r = done // pairs

time: 136 us -> 254 us (1.87)
  Pallas kernels: 31.5 us -> 154 us
  waiting for transfers between devices: 43.7 us -> 29 us
  starting transfers between devices: 56.7 us -> 69.8 us
    pallas_call x51 -> x47, Pallas kernels: 31.5 us -> 154 us  [call(): pl.pallas_call(kernel, out_shape=outs, in_specs=more.pop('in_specs', [VME...]
    ppermute x3 -> x32, starting transfers between devices: 3 us -> 68.3 us  [shift(): return lax.ppermute(x, 'blk', [(i, (i + 2 * by) % n) for i in range(n)])]
    ppermute x33 -> x0, starting transfers between devices: 52.2 us -> none  [pass_on(): return lax.ppermute(x, 'blk', perm)]
    ppermute x33 -> x0, waiting for transfers between devices: 41.1 us -> none  [pass_on(): return lax.ppermute(x, 'blk', perm)]
    ppermute x3 -> x32, waiting for transfers between devices: 1.39 us -> 27.8 us  [shift(): return lax.ppermute(x, 'blk', [(i, (i + 2 * by) % n) for i in range(n)])]
  transfers between devices with their start and end apart: 45 -> 41, of which waited for: 18 -> 21; matrix products, arithmetic and copies ran while one was open for 0% -> 0% of each run, Pallas kernels for 19% -> 46%
where the time goes in v3:
time: 254 us
  Pallas kernels  154 us (61%)
  starting transfers between devices  69.8 us (27%)
  waiting for transfers between devices  29 us (11%)
    pallas_call x47, Pallas kernels, call(): pl.pallas_call(kernel, out_shape=outs, in_specs=more.pop('in_specs', [VME...  154 us
    ppermute x32, starting transfers between devices, shift(): return lax.ppermute(x, 'blk', [(i, (i + 2 * by) % n) for i in range(n)])  68.3 us
    ppermute x32, waiting for transfers between devices, shift(): return lax.ppermute(x, 'blk', [(i, (i + 2 * by) % n) for i in range(n)])  27.8 us
  transfers between devices with their start and end apart: 41, of which 21 were waited for; matrix products, arithmetic and copies ran while one was open for 0% of the time, Pallas kernels for 46%

profile of v3, /device:TPU:0, one launch (start us, length us, event | category | flops | bytes accessed | tf_op | source)
XLA Modules:
  0.0 253.8 jit_solution(11265210418434494236)
XLA Ops:
  0.6 33.6 %pack.2.own.refs_6_ = f32[1192,256]{1,0:T(8,128)} custom-call(s32[3,1,4]{2,1,0:T(1,128)} %bitcast.1, f32[4,1,256]{2,1,0:T(1,128)} %turnout.3, s32[4,1,256]{2,1,0:T(1,128)} %district.3, f32[4,1,3,256,256]{4,3,2,1,0:T(8,128)} %l_ref.3, f32[4,1,256,256]{3,2,1,0:T(8,128)} %d_ref.3, f32[4,1,256,128]{3,2,1,0:T(8,128)} %r_ref.3), custom_call_target="tpu_custom_call" | custom-call | bytes 2441216 | tf_op jit(solution)/shard_map/pack/pallas_call | solution.py:310
  34.8 97.3 %pack.3 = (f32[1192,256]{1,0:T(8,128)}, f32[1192,256]{1,0:T(8,128)}, f32[1192,256]{1,0:T(8,128)}) custom-call(s32[3,1,4]{2,1,0:T(1,128)} %bitcast.2, f32[4,1,256]{2,1,0:T(1,128)} %turnout.3, s32[4,1,256]{2,1,0:T(1,128)} %district.3, f32[4,1,3,256,256]{4,3,2,1,0:T(8,128)} %l_ref.3, f32[4,1,256,256]{3,2,1,0:T(8,128)} %d_ref.3, f32[4,1,256,128]{3,2,1,0:T(8,128)} %r_ref.3), custom_call_target="tpu_custom_call" | custom-call | bytes 7323648 | tf_op jit(solution)/shard_map/pack/pallas_call | solution.py:310
  132.1 1.2 near_setup.4
  133.9 3.8 %collective-permute-start.2 = (f32[64,512]{1,0:T(8,128)S(1)}, f32[64,512]{1,0:T(8,128)S(1)}, u32[]{:S(2)}, u32[]{:S(2)}) collective-permute-start(f32[64,512]{1,0:T(8,128)S(1)} %get-tuple-element.102), channel_id=1, source_target_pairs={{0,24},{4,28},{8,0},{12,4},{16,8},{20,12},{24,16},{28,20},{1,25},{... | collective-permute-start | bytes 393224 | tf_op jit(solution)/shard_map/ppermute | solution.py:325
  137.6 1.2 far_setup.4
  139.7 1.0 collective-permute-done.2.refs_0_
  141.0 3.5 %collective-permute-start.3 = (f32[64,512]{1,0:T(8,128)S(1)}, f32[64,512]{1,0:T(8,128)S(1)}, u32[]{:S(2)}, u32[]{:S(2)}) collective-permute-start(f32[64,512]{1,0:T(8,128)S(1)} %get-tuple-element.103), channel_id=1, source_target_pairs={{0,24},{4,28},{8,0},{12,4},{16,8},{20,12},{24,16},{28,20},{1,25},{... | collective-permute-start | bytes 393224 | tf_op jit(solution)/shard_map/ppermute | solution.py:325
  145.4 1.7 collective-permute-done.3.refs_1_
  147.3 3.5 %collective-permute-start.6 = (f32[64,512]{1,0:T(8,128)S(1)}, f32[64,512]{1,0:T(8,128)S(1)}, u32[]{:S(2)}, u32[]{:S(2)}) collective-permute-start(f32[64,512]{1,0:T(8,128)S(1)} %get-tuple-element.106), channel_id=1, source_target_pairs={{0,24},{4,28},{8,0},{12,4},{16,8},{20,12},{24,16},{28,20},{1,25},{... | collective-permute-start | bytes 393224 | tf_op jit(solution)/shard_map/ppermute | solution.py:325
  150.8 2.5 collective-permute-done.6.refs_1_
  153.6 3.4 %collective-permute-start.7 = (f32[64,512]{1,0:T(8,128)S(1)}, f32[64,512]{1,0:T(8,128)S(1)}, u32[]{:S(2)}, u32[]{:S(2)}) collective-permute-start(f32[64,512]{1,0:T(8,128)S(1)} %get-tuple-element.107), channel_id=1, source_target_pairs={{0,24},{4,28},{8,0},{12,4},{16,8},{20,12},{24,16},{28,20},{1,25},{... | collective-permute-start | bytes 393224 | tf_op jit(solution)/shard_map/ppermute | solution.py:325
  159.5 1.2 near_setup.5
  160.7 1.6 collective-permute-done.4.refs_0_
  163.6 2.8 %collective-permute-start.11 = (f32[64,512]{1,0:T(8,128)S(1)}, f32[64,512]{1,0:T(8,128)S(1)}, u32[]{:S(2)}, u32[]{:S(2)}) collective-permute-start(f32[64,512]{1,0:T(8,128)S(1)} %get-tuple-element.121), channel_id=1, source_target_pairs={{0,24},{4,28},{8,0},{12,4},{16,8},{20,12},{24,16},{28,20},{1,25},{... | collective-permute-start | bytes 393224 | tf_op jit(solution)/shard_map/ppermute | solution.py:325
  166.3 1.2 far_setup.5
  167.8 1.6 collective-permute-start.9
  169.4 0.9 collective-permute-done.11.refs_1_
  170.6 4.7 %collective-permute-start.12 = (f32[64,512]{1,0:T(8,128)S(1)}, f32[64,512]{1,0:T(8,128)S(1)}, u32[]{:S(2)}, u32[]{:S(2)}) collective-permute-start(f32[64,512]{1,0:T(8,128)S(1)} %get-tuple-element.122), channel_id=1, source_target_pairs={{0,24},{4,28},{8,0},{12,4},{16,8},{20,12},{24,16},{28,20},{1,25},{... | collective-permute-start | bytes 393224 | tf_op jit(solution)/shard_map/ppermute | solution.py:325
  176.1 1.6 collective-permute-done.12.refs_1_
  178.1 3.5 %collective-permute-start.15 = (f32[64,512]{1,0:T(8,128)S(1)}, f32[64,512]{1,0:T(8,128)S(1)}, u32[]{:S(2)}, u32[]{:S(2)}) collective-permute-start(f32[64,512]{1,0:T(8,128)S(1)} %get-tuple-element.125), channel_id=1, source_target_pairs={{0,24},{4,28},{8,0},{12,4},{16,8},{20,12},{24,16},{28,20},{1,25},{... | collective-permute-start | bytes 393224 | tf_op jit(solution)/shard_map/ppermute | solution.py:325
  181.5 2.5 collective-permute-done.15.refs_1_
  184.3 3.4 %collective-permute-start.16 = (f32[64,512]{1,0:T(8,128)S(1)}, f32[64,512]{1,0:T(8,128)S(1)}, u32[]{:S(2)}, u32[]{:S(2)}) collective-permute-start(f32[64,512]{1,0:T(8,128)S(1)} %get-tuple-element.126), channel_id=1, source_target_pairs={{0,24},{4,28},{8,0},{12,4},{16,8},{20,12},{24,16},{28,20},{1,25},{... | collective-permute-start | bytes 393224 | tf_op jit(solution)/shard_map/ppermute | solution.py:325
  190.3 1.2 near_setup.6
  191.5 1.6 collective-permute-done.13.refs_0_
  194.3 2.8 %collective-permute-start.20 = (f32[64,512]{1,0:T(8,128)S(1)}, f32[64,512]{1,0:T(8,128)S(1)}, u32[]{:S(2)}, u32[]{:S(2)}) collective-permute-start(f32[64,512]{1,0:T(8,128)S(1)} %get-tuple-element.141), channel_id=1, source_target_pairs={{0,24},{4,28},{8,0},{12,4},{16,8},{20,12},{24,16},{28,20},{1,25},{... | collective-permute-start | bytes 393224 | tf_op jit(solution)/shard_map/ppermute | solution.py:325
  197.1 1.2 far_setup.6
  198.6 1.6 collective-permute-start.18
  200.1 0.9 collective-permute-done.20.refs_1_
  201.3 4.7 %collective-permute-start.21 = (f32[64,512]{1,0:T(8,128)S(1)}, f32[64,512]{1,0:T(8,128)S(1)}, u32[]{:S(2)}, u32[]{:S(2)}) collective-permute-start(f32[64,512]{1,0:T(8,128)S(1)} %get-tuple-element.142), channel_id=1, source_target_pairs={{0,24},{4,28},{8,0},{12,4},{16,8},{20,12},{24,16},{28,20},{1,25},{... | collective-permute-start | bytes 393224 | tf_op jit(solution)/shard_map/ppermute | solution.py:325
  206.9 1.6 collective-permute-done.21.refs_1_
  208.8 3.5 %collective-permute-start.24 = (f32[64,512]{1,0:T(8,128)S(1)}, f32[64,512]{1,0:T(8,128)S(1)}, u32[]{:S(2)}, u32[]{:S(2)}) collective-permute-start(f32[64,512]{1,0:T(8,128)S(1)} %get-tuple-element.145), channel_id=1, source_target_pairs={{0,24},{4,28},{8,0},{12,4},{16,8},{20,12},{24,16},{28,20},{1,25},{... | collective-permute-start | bytes 393224 | tf_op jit(solution)/shard_map/ppermute | solution.py:325
  212.3 2.5 collective-permute-done.24.refs_1_
  215.1 3.6 %collective-permute-start.25 = (f32[64,512]{1,0:T(8,128)S(1)}, f32[64,512]{1,0:T(8,128)S(1)}, u32[]{:S(2)}, u32[]{:S(2)}) collective-permute-start(f32[64,512]{1,0:T(8,128)S(1)} %get-tuple-element.146), channel_id=1, source_target_pairs={{0,24},{4,28},{8,0},{12,4},{16,8},{20,12},{24,16},{28,20},{1,25},{... | collective-permute-start | bytes 393224 | tf_op jit(solution)/shard_map/ppermute | solution.py:325
  219.8 1.6 collective-permute-start.27
  222.3 1.2 near_setup.7
  224.3 3.2 %collective-permute-start.28 = (f32[64,512]{1,0:T(8,128)S(1)}, f32[64,512]{1,0:T(8,128)S(1)}, u32[]{:S(2)}, u32[]{:S(2)}) collective-permute-start(f32[64,512]{1,0:T(8,128)S(1)} %get-tuple-element.157), channel_id=1, source_target_pairs={{0,24},{4,28},{8,0},{12,4},{16,8},{20,12},{24,16},{28,20},{1,25},{... | collective-permute-start | bytes 393224 | tf_op jit(solution)/shard_map/ppermute | solution.py:325
  227.5 1.2 far_setup.7
  230.6 3.5 %collective-permute-start.30 = (f32[64,512]{1,0:T(8,128)S(1)}, f32[64,512]{1,0:T(8,128)S(1)}, u32[]{:S(2)}, u32[]{:S(2)}) collective-permute-start(f32[64,512]{1,0:T(8,128)S(1)} %get-tuple-element.163), channel_id=1, source_target_pairs={{0,24},{4,28},{8,0},{12,4},{16,8},{20,12},{24,16},{28,20},{1,25},{... | collective-permute-start | bytes 393224 | tf_op jit(solution)/shard_map/ppermute | solution.py:325
  235.0 1.7 collective-permute-done.30.refs_1_
  236.9 3.5 %collective-permute-start.32 = (f32[64,512]{1,0:T(8,128)S(1)}, f32[64,512]{1,0:T(8,128)S(1)}, u32[]{:S(2)}, u32[]{:S(2)}) collective-permute-start(f32[64,512]{1,0:T(8,128)S(1)} %get-tuple-element.165), channel_id=1, source_target_pairs={{0,24},{4,28},{8,0},{12,4},{16,8},{20,12},{24,16},{28,20},{1,25},{... | collective-permute-start | bytes 393224 | tf_op jit(solution)/shard_map/ppermute | solution.py:325
  240.9 2.0 collective-permute-done.32.refs_1_
  242.9 0.9 finish.7
  243.9 2.5 collective-permute-start.33
  246.4 1.5 collective-permute-start.34
  247.9 1.0 field.1
  249.3 1.0 collective-permute-done.34.refs_2_
  250.3 1.5 collective-permute-done.35.refs_3_
  251.9 1.2 collective-permute-done.40.got
  (89 shorter events, 22.9 us)
Async XLA Ops:
  34.3 97.8 %copy-start = (f32[1192,256]{1,0:T(8,128)S(1)}, f32[1192,256]{1,0:T(8,128)}, u32[]{:S(2)}) copy-start(f32[1192,256]{1,0:T(8,128)} %pack.2.own.refs_6_) | copy-start | bytes 3661828
  34.3 97.8 %collective-permute-start = (f32[1192,256]{1,0:T(8,128)}, f32[1192,256]{1,0:T(8,128)S(1)}, u32[]{:S(2)}, u32[]{:S(2)}) collective-permute-start(f32[1192,256]{1,0:T(8,128)} %pack.2.own.refs_6_), channel_id=1, source_target_pairs={{0,4},{4,0},{8,12},{12,8},{16,20},{20,16},{24,28},{28,24},{1,5},{5... | collective-permute-start | bytes 3661832 | tf_op jit(solution)/shard_map/ppermute | solution.py:322
  132.1 1.5 copy-start.3
  133.6 25.9 %collective-permute-start.8 = (f32[1192,256]{1,0:T(8,128)S(1)}, f32[1192,256]{1,0:T(8,128)S(1)}, u32[]{:S(2)}, u32[]{:S(2)}) collective-permute-start(f32[1192,256]{1,0:T(8,128)S(1)} %copy-done.3), channel_id=1, source_target_pairs={{0,4},{4,0},{8,12},{12,8},{16,20},{20,16},{24,28},{28,24},{1,5},{5... | collective-permute-start | bytes 3661832 | tf_op jit(solution)/shard_map/ppermute | solution.py:322
  133.9 6.9 %collective-permute-start.2 = (f32[64,512]{1,0:T(8,128)S(1)}, f32[64,512]{1,0:T(8,128)S(1)}, u32[]{:S(2)}, u32[]{:S(2)}) collective-permute-start(f32[64,512]{1,0:T(8,128)S(1)} %get-tuple-element.102), channel_id=1, source_target_pairs={{0,24},{4,28},{8,0},{12,4},{16,8},{20,12},{24,16},{28,20},{1,25},{... | collective-permute-start | bytes 393224 | tf_op jit(solution)/shard_map/ppermute | solution.py:325
  139.1 6.3 %collective-permute-start.1 = (f32[64,512]{1,0:T(8,128)S(1)}, f32[64,512]{1,0:T(8,128)S(1)}, u32[]{:S(2)}, u32[]{:S(2)}) collective-permute-start(f32[64,512]{1,0:T(8,128)S(1)} %far_terms.14), channel_id=1, source_target_pairs={{0,16},{4,20},{8,24},{12,28},{16,0},{20,4},{24,8},{28,12},{1,17},{... | collective-permute-start | bytes 393224 | tf_op jit(solution)/shard_map/ppermute | solution.py:325
  141.0 6.0 %collective-permute-start.3 = (f32[64,512]{1,0:T(8,128)S(1)}, f32[64,512]{1,0:T(8,128)S(1)}, u32[]{:S(2)}, u32[]{:S(2)}) collective-permute-start(f32[64,512]{1,0:T(8,128)S(1)} %get-tuple-element.103), channel_id=1, source_target_pairs={{0,24},{4,28},{8,0},{12,4},{16,8},{20,12},{24,16},{28,20},{1,25},{... | collective-permute-start | bytes 393224 | tf_op jit(solution)/shard_map/ppermute | solution.py:325
  144.8 6.0 %collective-permute-start.5 = (f32[64,512]{1,0:T(8,128)S(1)}, f32[64,512]{1,0:T(8,128)S(1)}, u32[]{:S(2)}, u32[]{:S(2)}) collective-permute-start(f32[64,512]{1,0:T(8,128)S(1)} %far_terms.16), channel_id=1, source_target_pairs={{0,16},{4,20},{8,24},{12,28},{16,0},{20,4},{24,8},{28,12},{1,17},{... | collective-permute-start | bytes 393224 | tf_op jit(solution)/shard_map/ppermute | solution.py:325
  147.3 6.0 %collective-permute-start.6 = (f32[64,512]{1,0:T(8,128)S(1)}, f32[64,512]{1,0:T(8,128)S(1)}, u32[]{:S(2)}, u32[]{:S(2)}) collective-permute-start(f32[64,512]{1,0:T(8,128)S(1)} %get-tuple-element.106), channel_id=1, source_target_pairs={{0,24},{4,28},{8,0},{12,4},{16,8},{20,12},{24,16},{28,20},{1,25},{... | collective-permute-start | bytes 393224 | tf_op jit(solution)/shard_map/ppermute | solution.py:325
  153.6 5.9 %collective-permute-start.7 = (f32[64,512]{1,0:T(8,128)S(1)}, f32[64,512]{1,0:T(8,128)S(1)}, u32[]{:S(2)}, u32[]{:S(2)}) collective-permute-start(f32[64,512]{1,0:T(8,128)S(1)} %get-tuple-element.107), channel_id=1, source_target_pairs={{0,24},{4,28},{8,0},{12,4},{16,8},{20,12},{24,16},{28,20},{1,25},{... | collective-permute-start | bytes 393224 | tf_op jit(solution)/shard_map/ppermute | solution.py:325
  157.3 5.0 %collective-permute-start.4 = (f32[64,512]{1,0:T(8,128)S(1)}, f32[64,512]{1,0:T(8,128)S(1)}, u32[]{:S(2)}, u32[]{:S(2)}) collective-permute-start(f32[64,512]{1,0:T(8,128)S(1)} %far_terms.15), channel_id=1, source_target_pairs={{0,16},{4,20},{8,24},{12,28},{16,0},{20,4},{24,8},{28,12},{1,17},{... | collective-permute-start | bytes 393224 | tf_op jit(solution)/shard_map/ppermute | solution.py:325
  160.7 1.9 copy-start.2
  162.6 27.7 %collective-permute-start.17 = (f32[1192,256]{1,0:T(8,128)S(1)}, f32[1192,256]{1,0:T(8,128)S(1)}, u32[]{:S(2)}, u32[]{:S(2)}) collective-permute-start(f32[1192,256]{1,0:T(8,128)S(1)} %copy-done.2), channel_id=1, source_target_pairs={{0,4},{4,0},{8,12},{12,8},{16,20},{20,16},{24,28},{28,24},{1,5},{5... | collective-permute-start | bytes 3661832 | tf_op jit(solution)/shard_map/ppermute | solution.py:322
  163.0 6.4 %collective-permute-start.10 = (f32[64,512]{1,0:T(8,128)S(1)}, f32[64,512]{1,0:T(8,128)S(1)}, u32[]{:S(2)}, u32[]{:S(2)}) collective-permute-start(f32[64,512]{1,0:T(8,128)S(1)} %far_terms.18), channel_id=1, source_target_pairs={{0,16},{4,20},{8,24},{12,28},{16,0},{20,4},{24,8},{28,12},{1,17},{... | collective-permute-start | bytes 393224 | tf_op jit(solution)/shard_map/ppermute | solution.py:325
  163.6 6.7 %collective-permute-start.11 = (f32[64,512]{1,0:T(8,128)S(1)}, f32[64,512]{1,0:T(8,128)S(1)}, u32[]{:S(2)}, u32[]{:S(2)}) collective-permute-start(f32[64,512]{1,0:T(8,128)S(1)} %get-tuple-element.121), channel_id=1, source_target_pairs={{0,24},{4,28},{8,0},{12,4},{16,8},{20,12},{24,16},{28,20},{1,25},{... | collective-permute-start | bytes 393224 | tf_op jit(solution)/shard_map/ppermute | solution.py:325
  167.8 8.3 %collective-permute-start.9 = (f32[64,512]{1,0:T(8,128)S(1)}, f32[64,512]{1,0:T(8,128)S(1)}, u32[]{:S(2)}, u32[]{:S(2)}) collective-permute-start(f32[64,512]{1,0:T(8,128)S(1)} %far_terms.17), channel_id=1, source_target_pairs={{0,16},{4,20},{8,24},{12,28},{16,0},{20,4},{24,8},{28,12},{1,17},{... | collective-permute-start | bytes 393224 | tf_op jit(solution)/shard_map/ppermute | solution.py:325
  170.6 7.2 %collective-permute-start.12 = (f32[64,512]{1,0:T(8,128)S(1)}, f32[64,512]{1,0:T(8,128)S(1)}, u32[]{:S(2)}, u32[]{:S(2)}) collective-permute-start(f32[64,512]{1,0:T(8,128)S(1)} %get-tuple-element.122), channel_id=1, source_target_pairs={{0,24},{4,28},{8,0},{12,4},{16,8},{20,12},{24,16},{28,20},{1,25},{... | collective-permute-start | bytes 393224 | tf_op jit(solution)/shard_map/ppermute | solution.py:325
  175.6 6.0 %collective-permute-start.14 = (f32[64,512]{1,0:T(8,128)S(1)}, f32[64,512]{1,0:T(8,128)S(1)}, u32[]{:S(2)}, u32[]{:S(2)}) collective-permute-start(f32[64,512]{1,0:T(8,128)S(1)} %far_terms.20), channel_id=1, source_target_pairs={{0,16},{4,20},{8,24},{12,28},{16,0},{20,4},{24,8},{28,12},{1,17},{... | collective-permute-start | bytes 393224 | tf_op jit(solution)/shard_map/ppermute | solution.py:325
  178.1 6.0 %collective-permute-start.15 = (f32[64,512]{1,0:T(8,128)S(1)}, f32[64,512]{1,0:T(8,128)S(1)}, u32[]{:S(2)}, u32[]{:S(2)}) collective-permute-start(f32[64,512]{1,0:T(8,128)S(1)} %get-tuple-element.125), channel_id=1, source_target_pairs={{0,24},{4,28},{8,0},{12,4},{16,8},{20,12},{24,16},{28,20},{1,25},{... | collective-permute-start | bytes 393224 | tf_op jit(solution)/shard_map/ppermute | solution.py:325
  184.3 5.9 %collective-permute-start.16 = (f32[64,512]{1,0:T(8,128)S(1)}, f32[64,512]{1,0:T(8,128)S(1)}, u32[]{:S(2)}, u32[]{:S(2)}) collective-permute-start(f32[64,512]{1,0:T(8,128)S(1)} %get-tuple-element.126), channel_id=1, source_target_pairs={{0,24},{4,28},{8,0},{12,4},{16,8},{20,12},{24,16},{28,20},{1,25},{... | collective-permute-start | bytes 393224 | tf_op jit(solution)/shard_map/ppermute | solution.py:325
  188.0 5.0 %collective-permute-start.13 = (f32[64,512]{1,0:T(8,128)S(1)}, f32[64,512]{1,0:T(8,128)S(1)}, u32[]{:S(2)}, u32[]{:S(2)}) collective-permute-start(f32[64,512]{1,0:T(8,128)S(1)} %far_terms.19), channel_id=1, source_target_pairs={{0,16},{4,20},{8,24},{12,28},{16,0},{20,4},{24,8},{28,12},{1,17},{... | collective-permute-start | bytes 393224 | tf_op jit(solution)/shard_map/ppermute | solution.py:325
  191.5 1.9 copy-start.1
  193.4 28.9 %collective-permute-start.26 = (f32[1192,256]{1,0:T(8,128)S(1)}, f32[1192,256]{1,0:T(8,128)S(1)}, u32[]{:S(2)}, u32[]{:S(2)}) collective-permute-start(f32[1192,256]{1,0:T(8,128)S(1)} %copy-done.1), channel_id=1, source_target_pairs={{0,4},{4,0},{8,12},{12,8},{16,20},{20,16},{24,28},{28,24},{1,5},{5... | collective-permute-start | bytes 3661832 | tf_op jit(solution)/shard_map/ppermute | solution.py:322
  193.7 6.4 %collective-permute-start.19 = (f32[64,512]{1,0:T(8,128)S(1)}, f32[64,512]{1,0:T(8,128)S(1)}, u32[]{:S(2)}, u32[]{:S(2)}) collective-permute-start(f32[64,512]{1,0:T(8,128)S(1)} %far_terms.22), channel_id=1, source_target_pairs={{0,16},{4,20},{8,24},{12,28},{16,0},{20,4},{24,8},{28,12},{1,17},{... | collective-permute-start | bytes 393224 | tf_op jit(solution)/shard_map/ppermute | solution.py:325
  194.3 6.7 %collective-permute-start.20 = (f32[64,512]{1,0:T(8,128)S(1)}, f32[64,512]{1,0:T(8,128)S(1)}, u32[]{:S(2)}, u32[]{:S(2)}) collective-permute-start(f32[64,512]{1,0:T(8,128)S(1)} %get-tuple-element.141), channel_id=1, source_target_pairs={{0,24},{4,28},{8,0},{12,4},{16,8},{20,12},{24,16},{28,20},{1,25},{... | collective-permute-start | bytes 393224 | tf_op jit(solution)/shard_map/ppermute | solution.py:325
  198.6 8.3 %collective-permute-start.18 = (f32[64,512]{1,0:T(8,128)S(1)}, f32[64,512]{1,0:T(8,128)S(1)}, u32[]{:S(2)}, u32[]{:S(2)}) collective-permute-start(f32[64,512]{1,0:T(8,128)S(1)} %far_terms.21), channel_id=1, source_target_pairs={{0,16},{4,20},{8,24},{12,28},{16,0},{20,4},{24,8},{28,12},{1,17},{... | collective-permute-start | bytes 393224 | tf_op jit(solution)/shard_map/ppermute | solution.py:325
  201.3 7.2 %collective-permute-start.21 = (f32[64,512]{1,0:T(8,128)S(1)}, f32[64,512]{1,0:T(8,128)S(1)}, u32[]{:S(2)}, u32[]{:S(2)}) collective-permute-start(f32[64,512]{1,0:T(8,128)S(1)} %get-tuple-element.142), channel_id=1, source_target_pairs={{0,24},{4,28},{8,0},{12,4},{16,8},{20,12},{24,16},{28,20},{1,25},{... | collective-permute-start | bytes 393224 | tf_op jit(solution)/shard_map/ppermute | solution.py:325
  206.3 6.0 %collective-permute-start.23 = (f32[64,512]{1,0:T(8,128)S(1)}, f32[64,512]{1,0:T(8,128)S(1)}, u32[]{:S(2)}, u32[]{:S(2)}) collective-permute-start(f32[64,512]{1,0:T(8,128)S(1)} %far_terms.24), channel_id=1, source_target_pairs={{0,16},{4,20},{8,24},{12,28},{16,0},{20,4},{24,8},{28,12},{1,17},{... | collective-permute-start | bytes 393224 | tf_op jit(solution)/shard_map/ppermute | solution.py:325
  208.8 6.0 %collective-permute-start.24 = (f32[64,512]{1,0:T(8,128)S(1)}, f32[64,512]{1,0:T(8,128)S(1)}, u32[]{:S(2)}, u32[]{:S(2)}) collective-permute-start(f32[64,512]{1,0:T(8,128)S(1)} %get-tuple-element.145), channel_id=1, source_target_pairs={{0,24},{4,28},{8,0},{12,4},{16,8},{20,12},{24,16},{28,20},{1,25},{... | collective-permute-start | bytes 393224 | tf_op jit(solution)/shard_map/ppermute | solution.py:325
  215.1 7.2 %collective-permute-start.25 = (f32[64,512]{1,0:T(8,128)S(1)}, f32[64,512]{1,0:T(8,128)S(1)}, u32[]{:S(2)}, u32[]{:S(2)}) collective-permute-start(f32[64,512]{1,0:T(8,128)S(1)} %get-tuple-element.146), channel_id=1, source_target_pairs={{0,24},{4,28},{8,0},{12,4},{16,8},{20,12},{24,16},{28,20},{1,25},{... | collective-permute-start | bytes 393224 | tf_op jit(solution)/shard_map/ppermute | solution.py:325
  219.0 5.0 %collective-permute-start.22 = (f32[64,512]{1,0:T(8,128)S(1)}, f32[64,512]{1,0:T(8,128)S(1)}, u32[]{:S(2)}, u32[]{:S(2)}) collective-permute-start(f32[64,512]{1,0:T(8,128)S(1)} %far_terms.23), channel_id=1, source_target_pairs={{0,16},{4,20},{8,24},{12,28},{16,0},{20,4},{24,8},{28,12},{1,17},{... | collective-permute-start | bytes 393224 | tf_op jit(solution)/shard_map/ppermute | solution.py:325
  219.8 9.7 %collective-permute-start.27 = (f32[64,512]{1,0:T(8,128)S(1)}, f32[64,512]{1,0:T(8,128)S(1)}, u32[]{:S(2)}, u32[]{:S(2)}) collective-permute-start(f32[64,512]{1,0:T(8,128)S(1)} %far_terms.25), channel_id=1, source_target_pairs={{0,16},{4,20},{8,24},{12,28},{16,0},{20,4},{24,8},{28,12},{1,17},{... | collective-permute-start | bytes 393224 | tf_op jit(solution)/shard_map/ppermute | solution.py:325
  224.3 6.0 %collective-permute-start.28 = (f32[64,512]{1,0:T(8,128)S(1)}, f32[64,512]{1,0:T(8,128)S(1)}, u32[]{:S(2)}, u32[]{:S(2)}) collective-permute-start(f32[64,512]{1,0:T(8,128)S(1)} %get-tuple-element.157), channel_id=1, source_target_pairs={{0,24},{4,28},{8,0},{12,4},{16,8},{20,12},{24,16},{28,20},{1,25},{... | collective-permute-start | bytes 393224 | tf_op jit(solution)/shard_map/ppermute | solution.py:325
  229.0 6.0 %collective-permute-start.29 = (f32[64,512]{1,0:T(8,128)S(1)}, f32[64,512]{1,0:T(8,128)S(1)}, u32[]{:S(2)}, u32[]{:S(2)}) collective-permute-start(f32[64,512]{1,0:T(8,128)S(1)} %far_terms.26), channel_id=1, source_target_pairs={{0,16},{4,20},{8,24},{12,28},{16,0},{20,4},{24,8},{28,12},{1,17},{... | collective-permute-start | bytes 393224 | tf_op jit(solution)/shard_map/ppermute | solution.py:325
  230.6 6.0 %collective-permute-start.30 = (f32[64,512]{1,0:T(8,128)S(1)}, f32[64,512]{1,0:T(8,128)S(1)}, u32[]{:S(2)}, u32[]{:S(2)}) collective-permute-start(f32[64,512]{1,0:T(8,128)S(1)} %get-tuple-element.163), channel_id=1, source_target_pairs={{0,24},{4,28},{8,0},{12,4},{16,8},{20,12},{24,16},{28,20},{1,25},{... | collective-permute-start | bytes 393224 | tf_op jit(solution)/shard_map/ppermute | solution.py:325
  234.4 6.5 %collective-permute-start.31 = (f32[64,512]{1,0:T(8,128)S(1)}, f32[64,512]{1,0:T(8,128)S(1)}, u32[]{:S(2)}, u32[]{:S(2)}) collective-permute-start(f32[64,512]{1,0:T(8,128)S(1)} %far_terms.27), channel_id=1, source_target_pairs={{0,16},{4,20},{8,24},{12,28},{16,0},{20,4},{24,8},{28,12},{1,17},{... | collective-permute-start | bytes 393224 | tf_op jit(solution)/shard_map/ppermute | solution.py:325
  236.9 6.0 %collective-permute-start.32 = (f32[64,512]{1,0:T(8,128)S(1)}, f32[64,512]{1,0:T(8,128)S(1)}, u32[]{:S(2)}, u32[]{:S(2)}) collective-permute-start(f32[64,512]{1,0:T(8,128)S(1)} %get-tuple-element.165), channel_id=1, source_target_pairs={{0,24},{4,28},{8,0},{12,4},{16,8},{20,12},{24,16},{28,20},{1,25},{... | collective-permute-start | bytes 393224 | tf_op jit(solution)/shard_map/ppermute | solution.py:325
  240.4 6.0 %collective-permute-start.39 = (f32[64,256]{1,0:T(8,128)S(1)}, f32[64,256]{1,0:T(8,128)S(1)}, u32[]{:S(2)}, u32[]{:S(2)}) collective-permute-start(f32[64,256]{1,0:T(8,128)S(1)} %get-tuple-element.178), channel_id=1, source_target_pairs={{0,4},{4,0},{8,12},{12,8},{16,20},{20,16},{24,28},{28,24},{1,5},{5... | collective-permute-start | bytes 196616 | tf_op jit(solution)/shard_map/ppermute | solution.py:322
  240.4 7.5 %collective-permute-start.38 = (f32[64,256]{1,0:T(8,128)S(1)}, f32[64,256]{1,0:T(8,128)S(1)}, u32[]{:S(2)}, u32[]{:S(2)}) collective-permute-start(f32[64,256]{1,0:T(8,128)S(1)} %get-tuple-element.177), channel_id=1, source_target_pairs={{0,4},{4,0},{8,12},{12,8},{16,20},{20,16},{24,28},{28,24},{1,5},{5... | collective-permute-start | bytes 196616 | tf_op jit(solution)/shard_map/ppermute | solution.py:322
  240.9 7.0 %collective-permute-start.37 = (f32[64,256]{1,0:T(8,128)S(1)}, f32[64,256]{1,0:T(8,128)S(1)}, u32[]{:S(2)}, u32[]{:S(2)}) collective-permute-start(f32[64,256]{1,0:T(8,128)S(1)} %get-tuple-element.176), channel_id=1, source_target_pairs={{0,4},{4,0},{8,12},{12,8},{16,20},{20,16},{24,28},{28,24},{1,5},{5... | collective-permute-start | bytes 196616 | tf_op jit(solution)/shard_map/ppermute | solution.py:322
  243.8 4.1 %collective-permute-start.36 = (f32[64,256]{1,0:T(8,128)S(1)}, f32[64,256]{1,0:T(8,128)S(1)}, u32[]{:S(2)}, u32[]{:S(2)}) collective-permute-start(f32[64,256]{1,0:T(8,128)S(1)} %get-tuple-element.175), channel_id=1, source_target_pairs={{0,4},{4,0},{8,12},{12,8},{16,20},{20,16},{24,28},{28,24},{1,5},{5... | collective-permute-start | bytes 196616 | tf_op jit(solution)/shard_map/ppermute | solution.py:322
  243.9 5.4 %collective-permute-start.33 = (f32[64,128]{1,0:T(8,128)S(1)}, f32[64,128]{1,0:T(8,128)S(1)}, u32[]{:S(2)}, u32[]{:S(2)}) collective-permute-start(f32[64,128]{1,0:T(8,128)S(1)} %get-tuple-element.168), channel_id=1, source_target_pairs={{0,8},{4,12},{8,16},{12,20},{16,24},{20,28},{24,0},{28,4},{1,9},{5... | collective-permute-start | bytes 98312 | tf_op jit(solution)/shard_map/ppermute | solution.py:325
  246.4 3.9 %collective-permute-start.34 = (f32[64,128]{1,0:T(8,128)S(1)}, f32[64,128]{1,0:T(8,128)S(1)}, u32[]{:S(2)}, u32[]{:S(2)}) collective-permute-start(f32[64,128]{1,0:T(8,128)S(1)} %get-tuple-element.169), channel_id=1, source_target_pairs={{0,16},{4,20},{8,24},{12,28},{16,0},{20,4},{24,8},{28,12},{1,17},{... | collective-permute-start | bytes 98312 | tf_op jit(solution)/shard_map/ppermute | solution.py:325
  247.9 3.9 %collective-permute-start.35 = (f32[64,128]{1,0:T(8,128)S(1)}, f32[64,128]{1,0:T(8,128)S(1)}, u32[]{:S(2)}, u32[]{:S(2)}) collective-permute-start(f32[64,128]{1,0:T(8,128)S(1)} %get-tuple-element.170), channel_id=1, source_target_pairs={{0,24},{4,28},{8,0},{12,4},{16,8},{20,12},{24,16},{28,20},{1,25},{... | collective-permute-start | bytes 98312 | tf_op jit(solution)/shard_map/ppermute | solution.py:325
  251.8 1.2 collective-permute-start.40

commit v4 on v2

--- a/solution.py
+++ b/solution.py
@@ -179,7 +179,8 @@
         run(*choices[1])
 
 
-def near_kernel(lead, pairs, pieces, split, received, has_near, *refs):
+def near_kernel(lead, pairs, pieces, split, ordered, received, has_near, *refs):
+    refs = refs[ordered:]
     taken = refs[:received]
     outs = refs[-2:] if has_near else refs[-1:]
     refs = refs[received : -len(outs)]
@@ -294,7 +295,7 @@
 def body(rhs, lower_blocks, col_index, diag_inverse, turnout, district_of):
     n = lax.axis_size("blk")
     pairs = n // 2
-    pieces = max(pairs // 2, 1)
+    pieces = 1
     rows_here, _, bs, columns = rhs.shape
     slots = lower_blocks.shape[2]
     half = columns // 2
@@ -331,7 +332,7 @@
                 perm += [(2 * sender + c, 2 * target + c) for c in range(2)]
         return lax.ppermute(x, "blk", perm)
 
-    def pack(rows):
+    def pack(rows, turnout=turnout):
         return call(
             functools.partial(pack_kernel, rows),
             "pack",
@@ -393,11 +394,13 @@
     packs, fixed = {}, {}
     (own,) = pack((top,))
     packs[top] = (own, swap(own))
-    packed = pack(tuple(range(top))) if top else ()
     fixed[top] = setup(top)
+    later, _ = lax.optimization_barrier((turnout, fixed[top][4]))
+    packed = pack(tuple(range(top)), later) if top else ()
 
     keeps, gots = {}, {}
     values = []
+    ordered = ()
     total = near = far_now = far_next = None
     steps = count + 2 * (pieces - 1)
     for step in range(steps):
@@ -414,10 +417,10 @@
             operands += [rt, gh, gl] if has_near else [rt]
         place = (lead, pairs, pieces, high * pairs)
         v, *near_out = call(
-            functools.partial(near_kernel, *place, len(taken), has_near),
+            functools.partial(near_kernel, *place, len(ordered), len(taken), has_near),
             "near_terms",
             (wide, wide) if has_near else (wide,),
-            (*taken, *operands),
+            (*ordered, *taken, *operands),
             4,
             6 * width * 4 * bs * bs,
             6 * width * bs * 4,
@@ -429,7 +432,7 @@
             own, _ = lax.optimization_barrier((packed[r], near_out[0]))
             packs[r] = (own, swap(own))
             fixed[r] = setup(r)
-        far_now, far_next = far_next, None
+        far_now, far_next, ordered = far_next, None, ()
         if has_far:
             operands = [x for r in rows for x in fixed[r][5:]]
             far_out = call(
@@ -442,6 +445,7 @@
                 6 * width * bs * 4,
             )
             far_next = pass_on(far_out, lead, 2)
+            ordered = (far_out,)
         done = lead + 2 * (pieces - 1)
         if done % pairs == 0 and 0 < done // pairs <= top:
             r = done // pairs

time: 136 us -> 126 us (0.926)
  starting transfers between devices: 56.7 us -> 33.1 us
  waiting for transfers between devices: 43.7 us -> 55.8 us
  local copies, waits for them, and re-layouts: 2.03 us -> 3.54 us
    ppermute x33 -> x29, starting transfers between devices: 52.2 us -> 28.3 us  [pass_on(): return lax.ppermute(x, 'blk', perm)]
    ppermute x33 -> x29, waiting for transfers between devices: 41.1 us -> 50.4 us  [pass_on(): return lax.ppermute(x, 'blk', perm)]
    ppermute x9, waiting for transfers between devices: 1.19 us -> 3.93 us  [swap(): return lax.ppermute(x, 'blk', [(i, i ^ 1) for i in range(n)])]
    unnamed x8 -> x10, local copies, waits for them, and re-layouts: 2.03 us -> 3.54 us
    pallas_call x51 -> x47, Pallas kernels: 31.5 us -> 30.8 us  [call(): pl.pallas_call(kernel, out_shape=outs, in_specs=more.pop('in_specs', [VME...]
  transfers between devices with their start and end apart: 45 -> 41, of which waited for: 18 -> 16; matrix products, arithmetic and copies ran while one was open for 0% -> 0% of each run, Pallas kernels for 19% -> 16%
where the time goes in v4:
time: 126 us; the launch traced here: 125 us
  waiting for transfers between devices  55.8 us (44%)
  starting transfers between devices  33.1 us (26%)
  Pallas kernels  30.8 us (24%)
  local copies, waits for them, and re-layouts  3.54 us (3%)
  between operations  1.42 us (1%)
    ppermute x29, waiting for transfers between devices, pass_on(): return lax.ppermute(x, 'blk', perm)  50.4 us
    pallas_call x47, Pallas kernels, call(): pl.pallas_call(kernel, out_shape=outs, in_specs=more.pop('in_specs', [VME...  30.8 us
    ppermute x29, starting transfers between devices, pass_on(): return lax.ppermute(x, 'blk', perm)  28.3 us
    ppermute x9, waiting for transfers between devices, swap(): return lax.ppermute(x, 'blk', [(i, i ^ 1) for i in range(n)])  3.93 us
    unnamed x10, local copies, waits for them, and re-layouts  3.54 us
    ppermute x3, starting transfers between devices, shift(): return lax.ppermute(x, 'blk', [(i, (i + 2 * by) % n) for i in range(n)])  3 us
  transfers between devices with their start and end apart: 41, of which 16 were waited for; matrix products, arithmetic and copies ran while one was open for 0% of the time, Pallas kernels for 16%

profile of v4, /device:TPU:0, one launch (start us, length us, event | category | flops | bytes accessed | tf_op | source)
XLA Modules:
  0.0 124.6 jit_solution(14756121882254009234)
XLA Ops:
  0.6 3.1 %pack.2.own.refs_6_ = f32[1192,256]{1,0:T(8,128)} custom-call(s32[3,1,4]{2,1,0:T(1,128)} %bitcast.1, f32[4,1,256]{2,1,0:T(1,128)} %turnout.2, s32[4,1,256]{2,1,0:T(1,128)} %district.3, f32[4,1,3,256,256]{4,3,2,1,0:T(8,128)} %l_ref.3, f32[4,1,256,256]{3,2,1,0:T(8,128)} %d_ref.3, f32[4,1,256,128]{3,2,1,0:T(8,128)} %r_ref.3), custom_call_target="tpu_custom_call" | custom-call | bytes 2441216 | tf_op jit(solution)/shard_map/pack/pallas_call | solution.py:310
  4.2 2.7 %collective-permute-done.oth.refs_7_ = f32[1192,256]{1,0:T(8,128)S(1)} collective-permute-done((f32[1192,256]{1,0:T(8,128)}, f32[1192,256]{1,0:T(8,128)S(1)}, u32[]{:S(2)}, u32[]{:S(2)}) %collective-permute-start) | collective-permute-done | bytes 1220640 | tf_op jit(solution)/shard_map/ppermute | solution.py:322
  7.0 1.3 %copy-done = f32[1192,256]{1,0:T(8,128)S(1)} copy-done((f32[1192,256]{1,0:T(8,128)S(1)}, f32[1192,256]{1,0:T(8,128)}, u32[]{:S(2)}) %copy-start) | copy-done | bytes 1220632
  8.3 1.1 near_setup.4
  9.4 4.8 %pack.3 = (f32[1192,256]{1,0:T(8,128)}, f32[1192,256]{1,0:T(8,128)}, f32[1192,256]{1,0:T(8,128)}) custom-call(s32[3,1,4]{2,1,0:T(1,128)} %bitcast.2, f32[4,1,256]{2,1,0:T(1,128)} %turnout.2, s32[4,1,256]{2,1,0:T(1,128)} %district.3, f32[4,1,3,256,256]{4,3,2,1,0:T(8,128)} %l_ref.3, f32[4,1,256,256]{3,2,1,0:T(8,128)} %d_ref.3, f32[4,1,256,128]{3,2,1,0:T(8,128)} %r_ref.3), custom_call_target="tpu_custom_call" | custom-call | bytes 7323648 | tf_op jit(solution)/shard_map/pack/pallas_call | solution.py:310
  15.6 1.2 far_setup.4
  19.1 1.3 %collective-permute-start.4 = (f32[64,512]{1,0:T(8,128)S(1)}, f32[64,512]{1,0:T(8,128)S(1)}, u32[]{:S(2)}, u32[]{:S(2)}) collective-permute-start(f32[64,512]{1,0:T(8,128)S(1)} %far_terms.15.refs_0_), channel_id=1, source_target_pairs={{16,0},{20,4},{17,1},{21,5},{18,2},{22,6},{19,3},{23,7}} | collective-permute-start | bytes 393224 | tf_op jit(solution)/shard_map/ppermute | solution.py:333
  20.7 1.3 %collective-permute-start.5 = (f32[64,512]{1,0:T(8,128)S(1)}, f32[64,512]{1,0:T(8,128)S(1)}, u32[]{:S(2)}, u32[]{:S(2)}) collective-permute-start(f32[64,512]{1,0:T(8,128)S(1)} %get-tuple-element.107), channel_id=1, source_target_pairs={{8,0},{12,4},{9,1},{13,5},{10,2},{14,6},{11,3},{15,7}} | collective-permute-start | bytes 393224 | tf_op jit(solution)/shard_map/ppermute | solution.py:333
  22.3 9.4 %collective-permute-done.4.refs_1_ = f32[64,512]{1,0:T(8,128)S(1)} collective-permute-done((f32[64,512]{1,0:T(8,128)S(1)}, f32[64,512]{1,0:T(8,128)S(1)}, u32[]{:S(2)}, u32[]{:S(2)}) %collective-permute-start.4) | collective-permute-done | bytes 131104 | tf_op jit(solution)/shard_map/ppermute | solution.py:333
  31.7 4.4 %collective-permute-done.5.refs_2_ = f32[64,512]{1,0:T(8,128)S(1)} collective-permute-done((f32[64,512]{1,0:T(8,128)S(1)}, f32[64,512]{1,0:T(8,128)S(1)}, u32[]{:S(2)}, u32[]{:S(2)}) %collective-permute-start.5) | collective-permute-done | bytes 131104 | tf_op jit(solution)/shard_map/ppermute | solution.py:333
  36.3 1.3 %collective-permute-start.7 = (f32[64,512]{1,0:T(8,128)S(1)}, f32[64,512]{1,0:T(8,128)S(1)}, u32[]{:S(2)}, u32[]{:S(2)}) collective-permute-start(f32[64,512]{1,0:T(8,128)S(1)} %get-tuple-element.109), channel_id=1, source_target_pairs={{0,24},{4,28},{1,25},{5,29},{2,26},{6,30},{3,27},{7,31}} | collective-permute-start | bytes 393224 | tf_op jit(solution)/shard_map/ppermute | solution.py:333
  38.3 0.8 finish.4
  39.5 0.7 collective-permute-done.7.refs_2_
  40.4 1.2 near_setup.5
  42.0 1.0 copy-done.3
  42.9 1.3 %collective-permute-start.9 = (f32[64,512]{1,0:T(8,128)S(1)}, f32[64,512]{1,0:T(8,128)S(1)}, u32[]{:S(2)}, u32[]{:S(2)}) collective-permute-start(f32[64,512]{1,0:T(8,128)S(1)} %far_terms.17.refs_0_), channel_id=1, source_target_pairs={{0,16},{4,20},{1,17},{5,21},{2,18},{6,22},{3,19},{7,23}} | collective-permute-start | bytes 393224 | tf_op jit(solution)/shard_map/ppermute | solution.py:333
  44.9 1.2 far_setup.5
  47.1 0.8 collective-permute-done.9.refs_1_
  49.2 1.3 %collective-permute-start.13 = (f32[64,512]{1,0:T(8,128)S(1)}, f32[64,512]{1,0:T(8,128)S(1)}, u32[]{:S(2)}, u32[]{:S(2)}) collective-permute-start(f32[64,512]{1,0:T(8,128)S(1)} %far_terms.19.refs_0_), channel_id=1, source_target_pairs={{16,0},{20,4},{17,1},{21,5},{18,2},{22,6},{19,3},{23,7}} | collective-permute-start | bytes 393224 | tf_op jit(solution)/shard_map/ppermute | solution.py:333
  50.8 1.3 %collective-permute-start.14 = (f32[64,512]{1,0:T(8,128)S(1)}, f32[64,512]{1,0:T(8,128)S(1)}, u32[]{:S(2)}, u32[]{:S(2)}) collective-permute-start(f32[64,512]{1,0:T(8,128)S(1)} %get-tuple-element.127), channel_id=1, source_target_pairs={{8,0},{12,4},{9,1},{13,5},{10,2},{14,6},{11,3},{15,7}} | collective-permute-start | bytes 393224 | tf_op jit(solution)/shard_map/ppermute | solution.py:333
  52.4 7.1 %collective-permute-done.13.refs_1_ = f32[64,512]{1,0:T(8,128)S(1)} collective-permute-done((f32[64,512]{1,0:T(8,128)S(1)}, f32[64,512]{1,0:T(8,128)S(1)}, u32[]{:S(2)}, u32[]{:S(2)}) %collective-permute-start.13) | collective-permute-done | bytes 131104 | tf_op jit(solution)/shard_map/ppermute | solution.py:333
  59.5 4.5 %collective-permute-done.14.refs_2_ = f32[64,512]{1,0:T(8,128)S(1)} collective-permute-done((f32[64,512]{1,0:T(8,128)S(1)}, f32[64,512]{1,0:T(8,128)S(1)}, u32[]{:S(2)}, u32[]{:S(2)}) %collective-permute-start.14) | collective-permute-done | bytes 131104 | tf_op jit(solution)/shard_map/ppermute | solution.py:333
  64.3 1.3 %collective-permute-start.16 = (f32[64,512]{1,0:T(8,128)S(1)}, f32[64,512]{1,0:T(8,128)S(1)}, u32[]{:S(2)}, u32[]{:S(2)}) collective-permute-start(f32[64,512]{1,0:T(8,128)S(1)} %get-tuple-element.129), channel_id=1, source_target_pairs={{0,24},{4,28},{1,25},{5,29},{2,26},{6,30},{3,27},{7,31}} | collective-permute-start | bytes 393224 | tf_op jit(solution)/shard_map/ppermute | solution.py:333
  66.3 0.9 finish.5
  68.1 1.2 near_setup.6
  69.6 1.0 copy-done.2
  70.6 1.3 %collective-permute-start.18 = (f32[64,512]{1,0:T(8,128)S(1)}, f32[64,512]{1,0:T(8,128)S(1)}, u32[]{:S(2)}, u32[]{:S(2)}) collective-permute-start(f32[64,512]{1,0:T(8,128)S(1)} %far_terms.21.refs_0_), channel_id=1, source_target_pairs={{0,16},{4,20},{1,17},{5,21},{2,18},{6,22},{3,19},{7,23}} | collective-permute-start | bytes 393224 | tf_op jit(solution)/shard_map/ppermute | solution.py:333
  72.5 1.2 far_setup.6
  74.7 0.8 collective-permute-done.18.refs_1_
  76.8 1.3 %collective-permute-start.22 = (f32[64,512]{1,0:T(8,128)S(1)}, f32[64,512]{1,0:T(8,128)S(1)}, u32[]{:S(2)}, u32[]{:S(2)}) collective-permute-start(f32[64,512]{1,0:T(8,128)S(1)} %far_terms.23.refs_0_), channel_id=1, source_target_pairs={{16,0},{20,4},{17,1},{21,5},{18,2},{22,6},{19,3},{23,7}} | collective-permute-start | bytes 393224 | tf_op jit(solution)/shard_map/ppermute | solution.py:333
  78.4 1.3 %collective-permute-start.23 = (f32[64,512]{1,0:T(8,128)S(1)}, f32[64,512]{1,0:T(8,128)S(1)}, u32[]{:S(2)}, u32[]{:S(2)}) collective-permute-start(f32[64,512]{1,0:T(8,128)S(1)} %get-tuple-element.147), channel_id=1, source_target_pairs={{8,0},{12,4},{9,1},{13,5},{10,2},{14,6},{11,3},{15,7}} | collective-permute-start | bytes 393224 | tf_op jit(solution)/shard_map/ppermute | solution.py:333
  80.0 7.4 %collective-permute-done.22.refs_1_ = f32[64,512]{1,0:T(8,128)S(1)} collective-permute-done((f32[64,512]{1,0:T(8,128)S(1)}, f32[64,512]{1,0:T(8,128)S(1)}, u32[]{:S(2)}, u32[]{:S(2)}) %collective-permute-start.22) | collective-permute-done | bytes 131104 | tf_op jit(solution)/shard_map/ppermute | solution.py:333
  87.4 4.5 %collective-permute-done.23.refs_2_ = f32[64,512]{1,0:T(8,128)S(1)} collective-permute-done((f32[64,512]{1,0:T(8,128)S(1)}, f32[64,512]{1,0:T(8,128)S(1)}, u32[]{:S(2)}, u32[]{:S(2)}) %collective-permute-start.23) | collective-permute-done | bytes 131104 | tf_op jit(solution)/shard_map/ppermute | solution.py:333
  92.2 1.3 %collective-permute-start.25 = (f32[64,512]{1,0:T(8,128)S(1)}, f32[64,512]{1,0:T(8,128)S(1)}, u32[]{:S(2)}, u32[]{:S(2)}) collective-permute-start(f32[64,512]{1,0:T(8,128)S(1)} %get-tuple-element.149), channel_id=1, source_target_pairs={{0,24},{4,28},{1,25},{5,29},{2,26},{6,30},{3,27},{7,31}} | collective-permute-start | bytes 393224 | tf_op jit(solution)/shard_map/ppermute | solution.py:333
  94.5 1.5 %collective-permute-start.27 = (f32[64,512]{1,0:T(8,128)S(1)}, f32[64,512]{1,0:T(8,128)S(1)}, u32[]{:S(2)}, u32[]{:S(2)}) collective-permute-start(f32[64,512]{1,0:T(8,128)S(1)} %far_terms.25.refs_0_), channel_id=1, source_target_pairs={{0,16},{4,20},{1,17},{5,21},{2,18},{6,22},{3,19},{7,23}} | collective-permute-start | bytes 393224 | tf_op jit(solution)/shard_map/ppermute | solution.py:333
  95.9 0.9 finish.6
  96.8 1.2 near_setup.7
  99.0 1.2 far_setup.7
  102.5 1.3 %collective-permute-start.31 = (f32[64,512]{1,0:T(8,128)S(1)}, f32[64,512]{1,0:T(8,128)S(1)}, u32[]{:S(2)}, u32[]{:S(2)}) collective-permute-start(f32[64,512]{1,0:T(8,128)S(1)} %far_terms.27.refs_0_), channel_id=1, source_target_pairs={{16,0},{20,4},{17,1},{21,5},{18,2},{22,6},{19,3},{23,7}} | collective-permute-start | bytes 393224 | tf_op jit(solution)/shard_map/ppermute | solution.py:333
  104.1 1.3 %collective-permute-start.32 = (f32[64,512]{1,0:T(8,128)S(1)}, f32[64,512]{1,0:T(8,128)S(1)}, u32[]{:S(2)}, u32[]{:S(2)}) collective-permute-start(f32[64,512]{1,0:T(8,128)S(1)} %get-tuple-element.167), channel_id=1, source_target_pairs={{8,0},{12,4},{9,1},{13,5},{10,2},{14,6},{11,3},{15,7}} | collective-permute-start | bytes 393224 | tf_op jit(solution)/shard_map/ppermute | solution.py:333
  106.0 5.8 %collective-permute-done.31.refs_0_ = f32[64,512]{1,0:T(8,128)S(1)} collective-permute-done((f32[64,512]{1,0:T(8,128)S(1)}, f32[64,512]{1,0:T(8,128)S(1)}, u32[]{:S(2)}, u32[]{:S(2)}) %collective-permute-start.31) | collective-permute-done | bytes 131104 | tf_op jit(solution)/shard_map/ppermute | solution.py:333
  111.8 4.4 %collective-permute-done.32.refs_1_ = f32[64,512]{1,0:T(8,128)S(1)} collective-permute-done((f32[64,512]{1,0:T(8,128)S(1)}, f32[64,512]{1,0:T(8,128)S(1)}, u32[]{:S(2)}, u32[]{:S(2)}) %collective-permute-start.32) | collective-permute-done | bytes 131104 | tf_op jit(solution)/shard_map/ppermute | solution.py:333
  116.2 0.9 finish.7
  117.3 2.9 %collective-permute-start.35 = (f32[64,128]{1,0:T(8,128)S(1)}, f32[64,128]{1,0:T(8,128)S(1)}, u32[]{:S(2)}, u32[]{:S(2)}) collective-permute-start(f32[64,128]{1,0:T(8,128)S(1)} %get-tuple-element.172), channel_id=1, source_target_pairs={{0,24},{4,28},{8,0},{12,4},{16,8},{20,12},{24,16},{28,20},{1,25},{... | collective-permute-start | bytes 98312 | tf_op jit(solution)/shard_map/ppermute | solution.py:325
  120.2 1.0 field.1
  121.2 1.0 collective-permute-done.33.refs_1_
  122.7 1.2 collective-permute-done.40.got
  123.9 0.8 district_mean.1
  (91 shorter events, 21.6 us)
Async XLA Ops:
  3.7 3.3 %collective-permute-start = (f32[1192,256]{1,0:T(8,128)}, f32[1192,256]{1,0:T(8,128)S(1)}, u32[]{:S(2)}, u32[]{:S(2)}) collective-permute-start(f32[1192,256]{1,0:T(8,128)} %pack.2.own.refs_6_), channel_id=1, source_target_pairs={{0,4},{4,0},{8,12},{12,8},{16,20},{20,16},{24,28},{28,24},{1,5},{5... | collective-permute-start | bytes 3661832 | tf_op jit(solution)/shard_map/ppermute | solution.py:322
  7.0 1.3 %copy-start = (f32[1192,256]{1,0:T(8,128)S(1)}, f32[1192,256]{1,0:T(8,128)}, u32[]{:S(2)}) copy-start(f32[1192,256]{1,0:T(8,128)} %pack.2.own.refs_6_) | copy-start | bytes 3661828
  9.4 6.2 %copy-start.1 = (f32[1192,256]{1,0:T(8,128)S(1)}, f32[1192,256]{1,0:T(8,128)}, u32[]{:S(2)}) copy-start(f32[1192,256]{1,0:T(8,128)} %pack.2.own.refs_6_) | copy-start | bytes 3661828
  14.5 25.6 %collective-permute-start.8 = (f32[1192,256]{1,0:T(8,128)}, f32[1192,256]{1,0:T(8,128)S(1)}, u32[]{:S(2)}, u32[]{:S(2)}) collective-permute-start(f32[1192,256]{1,0:T(8,128)} %get-tuple-element.114.own.refs_6_), channel_id=1, source_target_pairs={{0,4},{4,0},{8,12},{12,8},{16,20},{20,16},{24,28},{28,24},{1,5},{5... | collective-permute-start | bytes 3661832 | tf_op jit(solution)/shard_map/ppermute | solution.py:322
  15.0 2.8 %collective-permute-start.1 = (f32[64,512]{1,0:T(8,128)S(1)}, f32[64,512]{1,0:T(8,128)S(1)}, u32[]{:S(2)}, u32[]{:S(2)}) collective-permute-start(f32[64,512]{1,0:T(8,128)S(1)} %get-tuple-element.103), channel_id=1, source_target_pairs={{24,16},{28,20},{25,17},{29,21},{26,18},{30,22},{27,19},{31,23}} | collective-permute-start | bytes 393224 | tf_op jit(solution)/shard_map/ppermute | solution.py:333
  17.1 3.3 %collective-permute-start.2 = (f32[64,512]{1,0:T(8,128)S(1)}, f32[64,512]{1,0:T(8,128)S(1)}, u32[]{:S(2)}, u32[]{:S(2)}) collective-permute-start(f32[64,512]{1,0:T(8,128)S(1)} %far_terms.14.refs_0_), channel_id=1, source_target_pairs={{24,8},{28,12},{25,9},{29,13},{26,10},{30,14},{27,11},{31,15}} | collective-permute-start | bytes 393224 | tf_op jit(solution)/shard_map/ppermute | solution.py:333
  18.1 2.3 %collective-permute-start.3 = (f32[64,512]{1,0:T(8,128)S(1)}, f32[64,512]{1,0:T(8,128)S(1)}, u32[]{:S(2)}, u32[]{:S(2)}) collective-permute-start(f32[64,512]{1,0:T(8,128)S(1)} %get-tuple-element.105), channel_id=1, source_target_pairs={{16,8},{20,12},{17,9},{21,13},{18,10},{22,14},{19,11},{23,15}} | collective-permute-start | bytes 393224 | tf_op jit(solution)/shard_map/ppermute | solution.py:333
  19.1 12.6 %collective-permute-start.4 = (f32[64,512]{1,0:T(8,128)S(1)}, f32[64,512]{1,0:T(8,128)S(1)}, u32[]{:S(2)}, u32[]{:S(2)}) collective-permute-start(f32[64,512]{1,0:T(8,128)S(1)} %far_terms.15.refs_0_), channel_id=1, source_target_pairs={{16,0},{20,4},{17,1},{21,5},{18,2},{22,6},{19,3},{23,7}} | collective-permute-start | bytes 393224 | tf_op jit(solution)/shard_map/ppermute | solution.py:333
  20.7 15.3 %collective-permute-start.5 = (f32[64,512]{1,0:T(8,128)S(1)}, f32[64,512]{1,0:T(8,128)S(1)}, u32[]{:S(2)}, u32[]{:S(2)}) collective-permute-start(f32[64,512]{1,0:T(8,128)S(1)} %get-tuple-element.107), channel_id=1, source_target_pairs={{8,0},{12,4},{9,1},{13,5},{10,2},{14,6},{11,3},{15,7}} | collective-permute-start | bytes 393224 | tf_op jit(solution)/shard_map/ppermute | solution.py:333
  36.3 3.8 %collective-permute-start.7 = (f32[64,512]{1,0:T(8,128)S(1)}, f32[64,512]{1,0:T(8,128)S(1)}, u32[]{:S(2)}, u32[]{:S(2)}) collective-permute-start(f32[64,512]{1,0:T(8,128)S(1)} %get-tuple-element.109), channel_id=1, source_target_pairs={{0,24},{4,28},{1,25},{5,29},{2,26},{6,30},{3,27},{7,31}} | collective-permute-start | bytes 393224 | tf_op jit(solution)/shard_map/ppermute | solution.py:333
  37.6 4.0 %collective-permute-start.6 = (f32[64,512]{1,0:T(8,128)S(1)}, f32[64,512]{1,0:T(8,128)S(1)}, u32[]{:S(2)}, u32[]{:S(2)}) collective-permute-start(f32[64,512]{1,0:T(8,128)S(1)} %far_terms.16.refs_0_), channel_id=1, source_target_pairs={{8,24},{12,28},{9,25},{13,29},{10,26},{14,30},{11,27},{15,31}} | collective-permute-start | bytes 393224 | tf_op jit(solution)/shard_map/ppermute | solution.py:333
  39.2 1.3 %copy-start.4 = (f32[1192,256]{1,0:T(8,128)S(1)}, f32[1192,256]{1,0:T(8,128)}, u32[]{:S(2)}) copy-start(f32[1192,256]{1,0:T(8,128)} %get-tuple-element.114.own.refs_6_) | copy-start | bytes 3661828
  41.6 1.3 %copy-start.3 = (f32[1192,256]{1,0:T(8,128)S(1)}, f32[1192,256]{1,0:T(8,128)}, u32[]{:S(2)}) copy-start(f32[1192,256]{1,0:T(8,128)} %get-tuple-element.134.own.refs_6_) | copy-start | bytes 3661828
  42.9 25.1 %collective-permute-start.17 = (f32[1192,256]{1,0:T(8,128)S(1)}, f32[1192,256]{1,0:T(8,128)S(1)}, u32[]{:S(2)}, u32[]{:S(2)}) collective-permute-start(f32[1192,256]{1,0:T(8,128)S(1)} %copy-done.3), channel_id=1, source_target_pairs={{0,4},{4,0},{8,12},{12,8},{16,20},{20,16},{24,28},{28,24},{1,5},{5... | collective-permute-start | bytes 3661832 | tf_op jit(solution)/shard_map/ppermute | solution.py:322
  42.9 5.0 %collective-permute-start.9 = (f32[64,512]{1,0:T(8,128)S(1)}, f32[64,512]{1,0:T(8,128)S(1)}, u32[]{:S(2)}, u32[]{:S(2)}) collective-permute-start(f32[64,512]{1,0:T(8,128)S(1)} %far_terms.17.refs_0_), channel_id=1, source_target_pairs={{0,16},{4,20},{1,17},{5,21},{2,18},{6,22},{3,19},{7,23}} | collective-permute-start | bytes 393224 | tf_op jit(solution)/shard_map/ppermute | solution.py:333
  44.2 3.7 %collective-permute-start.10 = (f32[64,512]{1,0:T(8,128)S(1)}, f32[64,512]{1,0:T(8,128)S(1)}, u32[]{:S(2)}, u32[]{:S(2)}) collective-permute-start(f32[64,512]{1,0:T(8,128)S(1)} %get-tuple-element.123), channel_id=1, source_target_pairs={{24,16},{28,20},{25,17},{29,21},{26,18},{30,22},{27,19},{31,23}} | collective-permute-start | bytes 393224 | tf_op jit(solution)/shard_map/ppermute | solution.py:333
  46.4 4.1 %collective-permute-start.11 = (f32[64,512]{1,0:T(8,128)S(1)}, f32[64,512]{1,0:T(8,128)S(1)}, u32[]{:S(2)}, u32[]{:S(2)}) collective-permute-start(f32[64,512]{1,0:T(8,128)S(1)} %far_terms.18.refs_0_), channel_id=1, source_target_pairs={{24,8},{28,12},{25,9},{29,13},{26,10},{30,14},{27,11},{31,15}} | collective-permute-start | bytes 393224 | tf_op jit(solution)/shard_map/ppermute | solution.py:333
  48.2 2.3 %collective-permute-start.12 = (f32[64,512]{1,0:T(8,128)S(1)}, f32[64,512]{1,0:T(8,128)S(1)}, u32[]{:S(2)}, u32[]{:S(2)}) collective-permute-start(f32[64,512]{1,0:T(8,128)S(1)} %get-tuple-element.125), channel_id=1, source_target_pairs={{16,8},{20,12},{17,9},{21,13},{18,10},{22,14},{19,11},{23,15}} | collective-permute-start | bytes 393224 | tf_op jit(solution)/shard_map/ppermute | solution.py:333
  49.2 10.3 %collective-permute-start.13 = (f32[64,512]{1,0:T(8,128)S(1)}, f32[64,512]{1,0:T(8,128)S(1)}, u32[]{:S(2)}, u32[]{:S(2)}) collective-permute-start(f32[64,512]{1,0:T(8,128)S(1)} %far_terms.19.refs_0_), channel_id=1, source_target_pairs={{16,0},{20,4},{17,1},{21,5},{18,2},{22,6},{19,3},{23,7}} | collective-permute-start | bytes 393224 | tf_op jit(solution)/shard_map/ppermute | solution.py:333
  50.8 13.2 %collective-permute-start.14 = (f32[64,512]{1,0:T(8,128)S(1)}, f32[64,512]{1,0:T(8,128)S(1)}, u32[]{:S(2)}, u32[]{:S(2)}) collective-permute-start(f32[64,512]{1,0:T(8,128)S(1)} %get-tuple-element.127), channel_id=1, source_target_pairs={{8,0},{12,4},{9,1},{13,5},{10,2},{14,6},{11,3},{15,7}} | collective-permute-start | bytes 393224 | tf_op jit(solution)/shard_map/ppermute | solution.py:333
  64.3 3.8 %collective-permute-start.16 = (f32[64,512]{1,0:T(8,128)S(1)}, f32[64,512]{1,0:T(8,128)S(1)}, u32[]{:S(2)}, u32[]{:S(2)}) collective-permute-start(f32[64,512]{1,0:T(8,128)S(1)} %get-tuple-element.129), channel_id=1, source_target_pairs={{0,24},{4,28},{1,25},{5,29},{2,26},{6,30},{3,27},{7,31}} | collective-permute-start | bytes 393224 | tf_op jit(solution)/shard_map/ppermute | solution.py:333
  65.6 3.7 %collective-permute-start.15 = (f32[64,512]{1,0:T(8,128)S(1)}, f32[64,512]{1,0:T(8,128)S(1)}, u32[]{:S(2)}, u32[]{:S(2)}) collective-permute-start(f32[64,512]{1,0:T(8,128)S(1)} %far_terms.20.refs_0_), channel_id=1, source_target_pairs={{8,24},{12,28},{9,25},{13,29},{10,26},{14,30},{11,27},{15,31}} | collective-permute-start | bytes 393224 | tf_op jit(solution)/shard_map/ppermute | solution.py:333
  69.3 1.3 %copy-start.2 = (f32[1192,256]{1,0:T(8,128)S(1)}, f32[1192,256]{1,0:T(8,128)}, u32[]{:S(2)}) copy-start(f32[1192,256]{1,0:T(8,128)} %get-tuple-element.154.own.refs_6_) | copy-start | bytes 3661828
  70.6 26.3 %collective-permute-start.26 = (f32[1192,256]{1,0:T(8,128)S(1)}, f32[1192,256]{1,0:T(8,128)S(1)}, u32[]{:S(2)}, u32[]{:S(2)}) collective-permute-start(f32[1192,256]{1,0:T(8,128)S(1)} %copy-done.2), channel_id=1, source_target_pairs={{0,4},{4,0},{8,12},{12,8},{16,20},{20,16},{24,28},{28,24},{1,5},{5... | collective-permute-start | bytes 3661832 | tf_op jit(solution)/shard_map/ppermute | solution.py:322
  70.6 5.0 %collective-permute-start.18 = (f32[64,512]{1,0:T(8,128)S(1)}, f32[64,512]{1,0:T(8,128)S(1)}, u32[]{:S(2)}, u32[]{:S(2)}) collective-permute-start(f32[64,512]{1,0:T(8,128)S(1)} %far_terms.21.refs_0_), channel_id=1, source_target_pairs={{0,16},{4,20},{1,17},{5,21},{2,18},{6,22},{3,19},{7,23}} | collective-permute-start | bytes 393224 | tf_op jit(solution)/shard_map/ppermute | solution.py:333
  71.9 3.7 %collective-permute-start.19 = (f32[64,512]{1,0:T(8,128)S(1)}, f32[64,512]{1,0:T(8,128)S(1)}, u32[]{:S(2)}, u32[]{:S(2)}) collective-permute-start(f32[64,512]{1,0:T(8,128)S(1)} %get-tuple-element.143), channel_id=1, source_target_pairs={{24,16},{28,20},{25,17},{29,21},{26,18},{30,22},{27,19},{31,23}} | collective-permute-start | bytes 393224 | tf_op jit(solution)/shard_map/ppermute | solution.py:333
  74.0 4.1 %collective-permute-start.20 = (f32[64,512]{1,0:T(8,128)S(1)}, f32[64,512]{1,0:T(8,128)S(1)}, u32[]{:S(2)}, u32[]{:S(2)}) collective-permute-start(f32[64,512]{1,0:T(8,128)S(1)} %far_terms.22.refs_0_), channel_id=1, source_target_pairs={{24,8},{28,12},{25,9},{29,13},{26,10},{30,14},{27,11},{31,15}} | collective-permute-start | bytes 393224 | tf_op jit(solution)/shard_map/ppermute | solution.py:333
  75.8 2.3 %collective-permute-start.21 = (f32[64,512]{1,0:T(8,128)S(1)}, f32[64,512]{1,0:T(8,128)S(1)}, u32[]{:S(2)}, u32[]{:S(2)}) collective-permute-start(f32[64,512]{1,0:T(8,128)S(1)} %get-tuple-element.145), channel_id=1, source_target_pairs={{16,8},{20,12},{17,9},{21,13},{18,10},{22,14},{19,11},{23,15}} | collective-permute-start | bytes 393224 | tf_op jit(solution)/shard_map/ppermute | solution.py:333
  76.8 10.6 %collective-permute-start.22 = (f32[64,512]{1,0:T(8,128)S(1)}, f32[64,512]{1,0:T(8,128)S(1)}, u32[]{:S(2)}, u32[]{:S(2)}) collective-permute-start(f32[64,512]{1,0:T(8,128)S(1)} %far_terms.23.refs_0_), channel_id=1, source_target_pairs={{16,0},{20,4},{17,1},{21,5},{18,2},{22,6},{19,3},{23,7}} | collective-permute-start | bytes 393224 | tf_op jit(solution)/shard_map/ppermute | solution.py:333
  78.4 13.5 %collective-permute-start.23 = (f32[64,512]{1,0:T(8,128)S(1)}, f32[64,512]{1,0:T(8,128)S(1)}, u32[]{:S(2)}, u32[]{:S(2)}) collective-permute-start(f32[64,512]{1,0:T(8,128)S(1)} %get-tuple-element.147), channel_id=1, source_target_pairs={{8,0},{12,4},{9,1},{13,5},{10,2},{14,6},{11,3},{15,7}} | collective-permute-start | bytes 393224 | tf_op jit(solution)/shard_map/ppermute | solution.py:333
  92.2 4.6 %collective-permute-start.25 = (f32[64,512]{1,0:T(8,128)S(1)}, f32[64,512]{1,0:T(8,128)S(1)}, u32[]{:S(2)}, u32[]{:S(2)}) collective-permute-start(f32[64,512]{1,0:T(8,128)S(1)} %get-tuple-element.149), channel_id=1, source_target_pairs={{0,24},{4,28},{1,25},{5,29},{2,26},{6,30},{3,27},{7,31}} | collective-permute-start | bytes 393224 | tf_op jit(solution)/shard_map/ppermute | solution.py:333
  93.5 4.6 %collective-permute-start.24 = (f32[64,512]{1,0:T(8,128)S(1)}, f32[64,512]{1,0:T(8,128)S(1)}, u32[]{:S(2)}, u32[]{:S(2)}) collective-permute-start(f32[64,512]{1,0:T(8,128)S(1)} %far_terms.24.refs_0_), channel_id=1, source_target_pairs={{8,24},{12,28},{9,25},{13,29},{10,26},{14,30},{11,27},{15,31}} | collective-permute-start | bytes 393224 | tf_op jit(solution)/shard_map/ppermute | solution.py:333
  94.5 6.7 %collective-permute-start.27 = (f32[64,512]{1,0:T(8,128)S(1)}, f32[64,512]{1,0:T(8,128)S(1)}, u32[]{:S(2)}, u32[]{:S(2)}) collective-permute-start(f32[64,512]{1,0:T(8,128)S(1)} %far_terms.25.refs_0_), channel_id=1, source_target_pairs={{0,16},{4,20},{1,17},{5,21},{2,18},{6,22},{3,19},{7,23}} | collective-permute-start | bytes 393224 | tf_op jit(solution)/shard_map/ppermute | solution.py:333
  98.3 2.8 %collective-permute-start.28 = (f32[64,512]{1,0:T(8,128)S(1)}, f32[64,512]{1,0:T(8,128)S(1)}, u32[]{:S(2)}, u32[]{:S(2)}) collective-permute-start(f32[64,512]{1,0:T(8,128)S(1)} %get-tuple-element.163), channel_id=1, source_target_pairs={{24,16},{28,20},{25,17},{29,21},{26,18},{30,22},{27,19},{31,23}} | collective-permute-start | bytes 393224 | tf_op jit(solution)/shard_map/ppermute | solution.py:333
  100.5 3.3 %collective-permute-start.29 = (f32[64,512]{1,0:T(8,128)S(1)}, f32[64,512]{1,0:T(8,128)S(1)}, u32[]{:S(2)}, u32[]{:S(2)}) collective-permute-start(f32[64,512]{1,0:T(8,128)S(1)} %far_terms.26.refs_0_), channel_id=1, source_target_pairs={{24,8},{28,12},{25,9},{29,13},{26,10},{30,14},{27,11},{31,15}} | collective-permute-start | bytes 393224 | tf_op jit(solution)/shard_map/ppermute | solution.py:333
  101.5 2.3 %collective-permute-start.30 = (f32[64,512]{1,0:T(8,128)S(1)}, f32[64,512]{1,0:T(8,128)S(1)}, u32[]{:S(2)}, u32[]{:S(2)}) collective-permute-start(f32[64,512]{1,0:T(8,128)S(1)} %get-tuple-element.165), channel_id=1, source_target_pairs={{16,8},{20,12},{17,9},{21,13},{18,10},{22,14},{19,11},{23,15}} | collective-permute-start | bytes 393224 | tf_op jit(solution)/shard_map/ppermute | solution.py:333
  102.5 9.3 %collective-permute-start.31 = (f32[64,512]{1,0:T(8,128)S(1)}, f32[64,512]{1,0:T(8,128)S(1)}, u32[]{:S(2)}, u32[]{:S(2)}) collective-permute-start(f32[64,512]{1,0:T(8,128)S(1)} %far_terms.27.refs_0_), channel_id=1, source_target_pairs={{16,0},{20,4},{17,1},{21,5},{18,2},{22,6},{19,3},{23,7}} | collective-permute-start | bytes 393224 | tf_op jit(solution)/shard_map/ppermute | solution.py:333
  104.1 12.1 %collective-permute-start.32 = (f32[64,512]{1,0:T(8,128)S(1)}, f32[64,512]{1,0:T(8,128)S(1)}, u32[]{:S(2)}, u32[]{:S(2)}) collective-permute-start(f32[64,512]{1,0:T(8,128)S(1)} %get-tuple-element.167), channel_id=1, source_target_pairs={{8,0},{12,4},{9,1},{13,5},{10,2},{14,6},{11,3},{15,7}} | collective-permute-start | bytes 393224 | tf_op jit(solution)/shard_map/ppermute | solution.py:333
  105.4 11.9 %collective-permute-start.39 = (f32[64,256]{1,0:T(8,128)S(1)}, f32[64,256]{1,0:T(8,128)S(1)}, u32[]{:S(2)}, u32[]{:S(2)}) collective-permute-start(f32[64,256]{1,0:T(8,128)S(1)} %get-tuple-element.180), channel_id=1, source_target_pairs={{0,4},{4,0},{8,12},{12,8},{16,20},{20,16},{24,28},{28,24},{1,5},{5... | collective-permute-start | bytes 196616 | tf_op jit(solution)/shard_map/ppermute | solution.py:322
  105.5 11.9 %collective-permute-start.38 = (f32[64,256]{1,0:T(8,128)S(1)}, f32[64,256]{1,0:T(8,128)S(1)}, u32[]{:S(2)}, u32[]{:S(2)}) collective-permute-start(f32[64,256]{1,0:T(8,128)S(1)} %get-tuple-element.179), channel_id=1, source_target_pairs={{0,4},{4,0},{8,12},{12,8},{16,20},{20,16},{24,28},{28,24},{1,5},{5... | collective-permute-start | bytes 196616 | tf_op jit(solution)/shard_map/ppermute | solution.py:322
  105.9 14.3 %collective-permute-start.37 = (f32[64,256]{1,0:T(8,128)S(1)}, f32[64,256]{1,0:T(8,128)S(1)}, u32[]{:S(2)}, u32[]{:S(2)}) collective-permute-start(f32[64,256]{1,0:T(8,128)S(1)} %get-tuple-element.178), channel_id=1, source_target_pairs={{0,4},{4,0},{8,12},{12,8},{16,20},{20,16},{24,28},{28,24},{1,5},{5... | collective-permute-start | bytes 196616 | tf_op jit(solution)/shard_map/ppermute | solution.py:322
  117.1 3.1 %collective-permute-start.36 = (f32[64,256]{1,0:T(8,128)S(1)}, f32[64,256]{1,0:T(8,128)S(1)}, u32[]{:S(2)}, u32[]{:S(2)}) collective-permute-start(f32[64,256]{1,0:T(8,128)S(1)} %get-tuple-element.177), channel_id=1, source_target_pairs={{0,4},{4,0},{8,12},{12,8},{16,20},{20,16},{24,28},{28,24},{1,5},{5... | collective-permute-start | bytes 196616 | tf_op jit(solution)/shard_map/ppermute | solution.py:322
  117.2 5.0 %collective-permute-start.33 = (f32[64,128]{1,0:T(8,128)S(1)}, f32[64,128]{1,0:T(8,128)S(1)}, u32[]{:S(2)}, u32[]{:S(2)}) collective-permute-start(f32[64,128]{1,0:T(8,128)S(1)} %get-tuple-element.170), channel_id=1, source_target_pairs={{0,8},{4,12},{8,16},{12,20},{16,24},{20,28},{24,0},{28,4},{1,9},{5... | collective-permute-start | bytes 98312 | tf_op jit(solution)/shard_map/ppermute | solution.py:325
  117.2 5.0 %collective-permute-start.34 = (f32[64,128]{1,0:T(8,128)S(1)}, f32[64,128]{1,0:T(8,128)S(1)}, u32[]{:S(2)}, u32[]{:S(2)}) collective-permute-start(f32[64,128]{1,0:T(8,128)S(1)} %get-tuple-element.171), channel_id=1, source_target_pairs={{0,16},{4,20},{8,24},{12,28},{16,0},{20,4},{24,8},{28,12},{1,17},{... | collective-permute-start | bytes 98312 | tf_op jit(solution)/shard_map/ppermute | solution.py:325
  117.3 5.3 %collective-permute-start.35 = (f32[64,128]{1,0:T(8,128)S(1)}, f32[64,128]{1,0:T(8,128)S(1)}, u32[]{:S(2)}, u32[]{:S(2)}) collective-permute-start(f32[64,128]{1,0:T(8,128)S(1)} %get-tuple-element.172), channel_id=1, source_target_pairs={{0,24},{4,28},{8,0},{12,4},{16,8},{20,12},{24,16},{28,20},{1,25},{... | collective-permute-start | bytes 98312 | tf_op jit(solution)/shard_map/ppermute | solution.py:325
  122.6 1.2 %collective-permute-start.40 = (f32[32,128]{1,0:T(8,128)S(1)}, f32[32,128]{1,0:T(8,128)S(1)}, u32[]{:S(2)}, u32[]{:S(2)}) collective-permute-start(f32[32,128]{1,0:T(8,128)S(1)} %get-tuple-element.187), channel_id=1, source_target_pairs={{0,4},{4,0},{8,12},{12,8},{16,20},{20,16},{24,28},{28,24},{1,5},{5... | collective-permute-start | bytes 49160 | tf_op jit(solution)/shard_map/ppermute | solution.py:322
